TPU v7x, 32 devices: a whole 2x2x4 slice. The times are simulated.
32 devices in a mesh: segment: 4 (over y, x), feat: 4 (over z), tok: 2 (over core).
Axes of the slice: x: 2, y: 2, z: 4, core: 2. Of those that a mesh axis runs over, the one named last changes fastest.
Arguments:
- layer_inputs: bfloat16 [4, 448, 2304], P('segment', 'feat', 'tok'), may hold values from -6 to 6
- targets: bfloat16 [4, 448, 2304], P('segment', 'tok', 'feat'), may hold values from -6 to 6
- enc_weight: bfloat16 [4, 2304, 12288], P('segment', 'feat', 'tok'), may hold values from -0.125 to 0.125
- enc_bias: float32 [4, 12288], P('segment', 'tok'), may hold values from -3 to 3
- dec_weight: bfloat16 [4, 4, 2304, 12288], P('segment', None, 'feat', 'tok'), may hold values from -0.0546875 to 0.0546875
Outputs:
- features: bfloat16 [4, 448, 12288], P('segment', 'feat', 'tok')
- residual: float32 [4, 448, 2304], P('segment', 'tok', 'feat')
All inputs are finite; a program needn't handle non-finite values.
Results may differ from a plain program's by a relative error of at most 0.01.
Values may be sent and summed in bfloat16 or wider, within the bound.
No kernel may reach another device: no remote copies, remote signals or barrier semaphores. Data moves between devices by JAX's collectives and lax.ppermute only.
A program may use at most 128 MiB of HBM per device.

v0:
```python
import jax
import jax.numpy as jnp
from jax import lax
from jax.sharding import PartitionSpec as P

BF16 = jnp.bfloat16
F32 = jnp.float32
GROUPS = 2
CHUNKS = 2
STREAMS = 2
PIECES = 2


def local(segments, ring, cores, layer_inputs, targets, enc_weight, enc_bias, dec_weight):
    z = lax.axis_index("feat")
    core = lax.axis_index("tok")
    segment = lax.axis_index("segment")
    odd = z % 2 == 1
    rows = layer_inputs.shape[1] // GROUPS
    width = enc_weight.shape[2] // CHUNKS
    depth = enc_weight.shape[1]
    weight = enc_weight[0]
    decoders = dec_weight[0]
    layers = decoders.shape[0]
    per_core = ring // cores

    own_rows = lax.all_gather(layer_inputs[0], "tok", axis=1, tiled=True)

    swaps = ring & (ring - 1) == 0

    def exchanged():
        share = own_rows.shape[0] // cores
        block = lax.dynamic_slice_in_dim(own_rows, core * share, share, axis=0)
        parts = []
        for k in range(ring):
            to = z ^ k if swaps else (z + k) % ring
            part = lax.dynamic_slice_in_dim(block, to * depth, depth, axis=1)
            if k:
                pairs = [(i, i ^ k if swaps else (i + k) % ring) for i in range(ring)]
                part = lax.ppermute(part, "feat", pairs)
            parts.append(part)
        every = lax.all_gather(jnp.stack(parts), "tok", axis=1, tiled=True)
        order = [z ^ ((z - k) % ring) if swaps else k for k in range(ring)]
        every = [lax.dynamic_index_in_dim(every, i, axis=0, keepdims=False) for i in order]
        return [
            jnp.concatenate([part[group * rows : (group + 1) * rows] for part in every], axis=0)
            for group in range(GROUPS)
        ]

    columns = exchanged()

    def partial_sums(group, chunk):
        part = jnp.dot(
            columns[group], weight[:, chunk * width : (chunk + 1) * width], preferred_element_type=F32
        ).astype(BF16)
        return [part[k * rows : (k + 1) * rows] for k in range(ring)]

    units = [(group, chunk) for group in range(GROUPS) for chunk in range(CHUNKS)]
    finished = {}
    decoded = {}
    waiting = []
    ordered = [None]
    last = []
    totals = {}
    residuals = {}

    def after(values, others):
        others = [x for x in jax.tree.leaves(others) if x is not None]
        return lax.optimization_barrier((values, others))[0] if others else values

    def background(sent):
        ordered[0] = sent
        for _ in range(min(PIECES, len(waiting))):
            ordered[0] = sent = waiting.pop(0)(sent)

    every = list(range(ring))

    def decode(unit, own, got):
        group, chunk = unit
        codes = {}

        def selected(places, sent):
            used = {slot for m in places if m for slot in (m - 1, ring - m - 1)}
            needed = tuple({slot: came[slot] for slot in sorted(used & set(came))} for came in got)
            mine, (even, other) = after((own, needed), sent)
            zero = jnp.zeros_like(mine)
            parts = []
            for m in places:
                a, b = m - 1, ring - m - 1
                left = jnp.where(odd, even.get(a, zero), other.get(a, zero))
                right = jnp.where(odd, other.get(b, zero), even.get(b, zero))
                parts.append(jnp.where(m <= z, left, right) if m else mine)
            return jnp.concatenate(parts, axis=0)

        def piece(layer, places):
            def run(sent):
                key = tuple(places)
                if key not in codes:
                    codes[key] = selected(places, sent)
                out = lax.dot_general(
                    after(codes[key], sent),
                    decoders[layer, :, chunk * width : (chunk + 1) * width],
                    (((1,), (1,)), ((), ())),
                    preferred_element_type=F32,
                )
                key = group, layer
                decoded[key] = out if key not in decoded else decoded[key] + out
                return decoded[key]

            return run

        if group < GROUPS - 1:
            waiting.extend(piece(layer, every) for layer in reversed(range(layers)))
        else:
            last.append(piece)

    class Stream:
        def __init__(self, own):
            self.own = own
            self.step = 0
            self.slot = 1
            self.got = [{}, {}]
            self.sums = partial_sums(*own[0])

        def swap(self, value, side):
            i, k, n = self.step, self.slot, len(self.own)
            pairs = []
            for p in range(side, ring - 1, 2):
                q = ring - 2 - p
                if not (i == 0 and p >= k or i == n and p < k):
                    pairs.append((p, p + 1))
                if not (i == 0 and q >= k or i == n and q < k):
                    pairs.append((p + 1, p))
            return lax.ppermute(value, "feat", pairs) if pairs else None

        def advance(self):
            i, k, n = self.step, self.slot, len(self.own)
            sent = []
            for side in range(2):
                if k == 0:
                    sent.append(finished[self.own[i - 1]])
                    continue
                value = self.got[1 - side].get(k - 1)
                if value is not None:
                    value = after(value, ordered)
                if i < n:
                    rightward = odd == (side == 1)
                    zero = jnp.zeros_like(self.sums[k])
                    own = jnp.where(
                        rightward,
                        jnp.where(k > z, self.sums[k], zero),
                        jnp.where(k > ring - 1 - z, self.sums[ring - k], zero),
                    )
                    value = own if value is None else (own.astype(F32) + value.astype(F32)).astype(BF16)
                sent.append(value)
            for side in range(2):
                got = self.swap(sent[side], side) if sent[side] is not None else None
                if got is not None:
                    self.got[side][k] = got
            if i < n or k < ring - 2:
                background(sent)
            self.sent = sent
            if i and k == ring - 2:
                unit = self.own[i - 1]
                decode(unit, finished[unit], tuple(dict(got) for got in self.got))
            self.slot += 1
            if i < n and k == ring - 1:
                chunk = self.own[i][1]
                bias = enc_bias[0, chunk * width : (chunk + 1) * width][None, :]
                total = self.sums[0].astype(F32) + self.got[0][k].astype(F32) + self.got[1][k].astype(F32)
                finished[self.own[i]] = jax.nn.relu(total + bias).astype(BF16)
                self.slot, self.step = 0, i + 1
                if i + 1 < n:
                    self.sums = partial_sums(*self.own[i + 1])
                self.got = [{}, {}]
                return True
            return not (i == n and k == ring - 2)

    def share_cores(group, sent, first=1):
        blocks = after([decoded[group, layer] for layer in range(first, layers if first else 1)], sent)
        blocks = jnp.stack(blocks).reshape(-1, ring, rows, depth)

        def share(index):
            begin = index * per_core
            return jnp.stack(
                [
                    lax.dynamic_index_in_dim(blocks, (z - begin - b) % ring, axis=1, keepdims=False)
                    for b in range(per_core)
                ],
                axis=1,
            )

        total = share(core)
        given = []
        for k in range(1, cores):
            given.append(share((core + k) % cores).astype(BF16))
            got = lax.ppermute(given[-1], "tok", [(i, (i + k) % cores) for i in range(cores)])
            total += got.astype(F32)
        totals[group, first] = total
        return given

    def share_segments(group, sent):
        total = after(totals[group, 1], sent)
        paired = segments & (segments - 1) == 0
        received, given = [], []
        for k in range(1, segments):
            place = segment ^ k if paired else jnp.minimum(segment + k, layers - 1)
            given.append(lax.dynamic_index_in_dim(total, jnp.maximum(place, 1) - 1, axis=0, keepdims=False).astype(BF16))
            pairs = [(i, i ^ k if paired else i + k) for i in range(segments)]
            got = lax.ppermute(given[-1], "segment", [(i, j) for i, j in pairs if i < j < segments])
            received.append(got)
        own = jnp.where(
            segment == 0,
            totals[group, 0][0],
            lax.dynamic_index_in_dim(total, jnp.maximum(segment, 1) - 1, axis=0, keepdims=False),
        )
        residuals[group] = sum([got.astype(F32) for got in received], own)
        return given

    streams = [Stream(units[i::STREAMS]) for i in range(STREAMS)]
    going = [True] * STREAMS
    while any(going):
        for i, stream in enumerate(streams):
            if going[i]:
                going[i] = stream.advance()
    sent = [stream.sent for stream in streams]
    for work in waiting:
        sent = work(sent)
    for group in range(GROUPS - 1):
        sent = share_cores(group, sent)
        share_cores(group, sent, 0)
        sent = share_segments(group, sent)
    for layer in reversed(range(layers)):
        for piece in last:
            sent = piece(layer, every)([sent, residuals.get(GROUPS - 2)] if layer == 0 else sent)
        if layer == 1:
            sent = share_cores(GROUPS - 1, sent)
    share_cores(GROUPS - 1, sent, 0)
    share_segments(GROUPS - 1, sent)
    own = jnp.stack([residuals[group] for group in range(GROUPS)], axis=1)
    residual = targets[0].astype(F32) - own.reshape(targets.shape[1:])
    features = jnp.concatenate(
        [
            jnp.concatenate([finished[group, chunk] for chunk in range(CHUNKS)], axis=1)
            for group in range(GROUPS)
        ],
        axis=0,
    )
    return (features[None], residual[None])


def solution(mesh):
    in_specs = (
        P("segment", "feat", "tok"),
        P("segment", "tok", "feat"),
        P("segment", "feat", "tok"),
        P("segment", "tok"),
        P("segment", None, "feat", "tok"),
    )
    out_specs = (P("segment", "feat", "tok"), P("segment", "tok", "feat"))
    sizes = (mesh.shape["segment"], mesh.shape["feat"], mesh.shape["tok"])
    return jax.shard_map(
        lambda *args: local(*sizes, *args), mesh=mesh, in_specs=in_specs, out_specs=out_specs, check_vma=False
    )
```

profile of v0, /device:TPU:0, one launch (start us, length us, event | category | flops | bytes accessed | tf_op | source)
XLA Modules:
  0.0 208.4 jit_solution(16301720672343061506)
XLA Ops:
  0.7 2.5 %all-gather = bf16[1,112,2304]{2,1,0:T(8,128)(2,1)S(1)} all-gather(bf16[1,112,1152]{2,1,0:T(8,128)(2,1)} %param.5), channel_id=2, replica_groups=mesh['segment'=4,'feat'=4,'tok'=2] {'tok'}, dimensions={2}, use_global_device_ids=true | all-gather | bytes 774144 | tf_op jit(solution)/shard_map/all_gather | solution.py:27
  3.3 3.0 %collective-permute-start = (bf16[56,576]{1,0:T(8,128)(2,1)S(1)}, bf16[56,576]{1,0:T(8,128)(2,1)S(1)}, u32[]{:S(2)}, u32[]{:S(2)}) collective-permute-start(bf16[56,576]{1,0:T(8,128)(2,1)S(1)} %get-tuple-element.214), channel_id=1, source_target_pairs={{0,2},{2,0},{4,6},{6,4},{1,3},{3,1},{5,7},{7,5},{8,10},{10,8},{12,... | collective-permute-start | bytes 193544 | tf_op jit(solution)/shard_map/ppermute | solution.py:40
  6.3 2.6 %collective-permute-start.1 = (bf16[56,576]{1,0:T(8,128)(2,1)S(1)}, bf16[56,576]{1,0:T(8,128)(2,1)S(1)}, u32[]{:S(2)}, u32[]{:S(2)}) collective-permute-start(bf16[56,576]{1,0:T(8,128)(2,1)S(1)} %get-tuple-element.213), channel_id=1, source_target_pairs={{0,4},{2,6},{4,0},{6,2},{1,5},{3,7},{5,1},{7,3},{8,12},{10,14},{12... | collective-permute-start | bytes 193544 | tf_op jit(solution)/shard_map/ppermute | solution.py:40
  9.7 4.6 %collective-permute-done.1 = bf16[56,576]{1,0:T(8,128)(2,1)S(1)} collective-permute-done((bf16[56,576]{1,0:T(8,128)(2,1)S(1)}, bf16[56,576]{1,0:T(8,128)(2,1)S(1)}, u32[]{:S(2)}, u32[]{:S(2)}) %collective-permute-start.1) | collective-permute-done | bytes 64544 | tf_op jit(solution)/shard_map/ppermute | solution.py:40
  17.5 3.4 %convolution_convert_fusion.3 = bf16[224,3072]{1,0:T(8,128)(2,1)S(1)} fusion(bf16[576,6144]{1,0:T(8,128)(2,1)} %bitcast.174, bf16[56,576]{1,0:T(8,128)(2,1)S(1)} %get-tuple-element.205, bf16[56,576]{1,0:T(8,128)(2,1)S(1)} %get-tuple-element.206, bf16[56,576]{1,0:T(8,128)(2,1)S(1)} %get-tuple-element.207, bf16[56,576]{1,0:T(8,128)(2,1)S(1)} %get-tuple-element.208), kind=kOutput, calls=%fused_computation.3 | convolution fusion | flops 794443776 | bytes 5173248 | tf_op jit(solution)/shard_map/dot_general | solution.py:53
  22.9 3.5 %collective-permute-start.3 = (bf16[56,3072]{1,0:T(8,128)(2,1)S(1)}, bf16[56,3072]{1,0:T(8,128)(2,1)S(1)}, u32[]{:S(2)}, u32[]{:S(2)}) collective-permute-start(bf16[56,3072]{1,0:T(8,128)(2,1)S(1)} %get-tuple-element.183), channel_id=1, source_target_pairs={{0,2},{6,4},{1,3},{7,5},{8,10},{14,12},{9,11},{15,13},{16,18},{22,... | collective-permute-start | bytes 1032200 | tf_op jit(solution)/shard_map/ppermute | solution.py:134
  35.6 6.5 %collective-permute-done.5 = bf16[56,3072]{1,0:T(8,128)(2,1)S(1)} collective-permute-done((bf16[56,3072]{1,0:T(8,128)(2,1)S(1)}, bf16[56,3072]{1,0:T(8,128)(2,1)S(1)}, u32[]{:S(2)}, u32[]{:S(2)}) %collective-permute-start.5) | collective-permute-done | bytes 344096 | tf_op jit(solution)/shard_map/ppermute | solution.py:134
  43.0 6.5 %collective-permute-done.7 = bf16[56,3072]{1,0:T(8,128)(2,1)S(1)} collective-permute-done((bf16[56,3072]{1,0:T(8,128)(2,1)S(1)}, bf16[56,3072]{1,0:T(8,128)(2,1)S(1)}, u32[]{:S(2)}, u32[]{:S(2)}) %collective-permute-start.7) | collective-permute-done | bytes 344096 | tf_op jit(solution)/shard_map/ppermute | solution.py:134
  49.8 2.5 %collective-permute-start.6 = (bf16[56,3072]{1,0:T(8,128)(2,1)S(1)}, bf16[56,3072]{1,0:T(8,128)(2,1)S(1)}, u32[]{:S(2)}, u32[]{:S(2)}) collective-permute-start(bf16[56,3072]{1,0:T(8,128)(2,1)S(1)} %get-tuple-element.181), channel_id=1, source_target_pairs={{0,2},{2,0},{4,6},{6,4},{1,3},{3,1},{5,7},{7,5},{8,10},{10,8},{12,... | collective-permute-start | bytes 1032200 | tf_op jit(solution)/shard_map/ppermute | solution.py:134
  53.1 3.8 %collective-permute-done.11 = bf16[56,3072]{1,0:T(8,128)(2,1)S(1)} collective-permute-done((bf16[56,3072]{1,0:T(8,128)(2,1)S(1)}, bf16[56,3072]{1,0:T(8,128)(2,1)S(1)}, u32[]{:S(2)}, u32[]{:S(2)}) %collective-permute-start.11) | collective-permute-done | bytes 344096 | tf_op jit(solution)/shard_map/ppermute | solution.py:134
  57.1 2.5 %collective-permute-start.10 = (bf16[56,3072]{1,0:T(8,128)(2,1)S(1)}, bf16[56,3072]{1,0:T(8,128)(2,1)S(1)}, u32[]{:S(2)}, u32[]{:S(2)}) collective-permute-start(bf16[56,3072]{1,0:T(8,128)(2,1)S(1)} %get-tuple-element.178), channel_id=1, source_target_pairs={{0,2},{2,0},{4,6},{6,4},{1,3},{3,1},{5,7},{7,5},{8,10},{10,8},{12,... | collective-permute-start | bytes 1032200 | tf_op jit(solution)/shard_map/ppermute | solution.py:134
  60.4 3.9 %collective-permute-done.6 = bf16[56,3072]{1,0:T(8,128)(2,1)S(1)} collective-permute-done((bf16[56,3072]{1,0:T(8,128)(2,1)S(1)}, bf16[56,3072]{1,0:T(8,128)(2,1)S(1)}, u32[]{:S(2)}, u32[]{:S(2)}) %collective-permute-start.6) | collective-permute-done | bytes 344096 | tf_op jit(solution)/shard_map/ppermute | solution.py:134
  65.1 5.3 %collective-permute-start.16 = (bf16[56,3072]{1,0:T(8,128)(2,1)S(1)}, bf16[56,3072]{1,0:T(8,128)(2,1)S(1)}, u32[]{:S(2)}, u32[]{:S(2)}) collective-permute-start(bf16[56,3072]{1,0:T(8,128)(2,1)S(1)} %maximum_convert_fusion.3), channel_id=1, source_target_pairs={{0,2},{2,0},{4,6},{6,4},{1,3},{3,1},{5,7},{7,5},{8,10},{10,8},{12,... | collective-permute-start | bytes 1032200 | tf_op jit(solution)/shard_map/ppermute | solution.py:134
  71.8 2.5 %collective-permute-start.17 = (bf16[56,3072]{1,0:T(8,128)(2,1)S(1)}, bf16[56,3072]{1,0:T(8,128)(2,1)S(1)}, u32[]{:S(2)}, u32[]{:S(2)}) collective-permute-start(bf16[56,3072]{1,0:T(8,128)(2,1)S(1)} %maximum_convert_fusion.2), channel_id=1, source_target_pairs={{0,2},{2,0},{4,6},{6,4},{1,3},{3,1},{5,7},{7,5},{8,10},{10,8},{12,... | collective-permute-start | bytes 1032200 | tf_op jit(solution)/shard_map/ppermute | solution.py:134
  75.0 4.3 %collective-permute-done.16 = bf16[56,3072]{1,0:T(8,128)(2,1)S(1)} collective-permute-done((bf16[56,3072]{1,0:T(8,128)(2,1)S(1)}, bf16[56,3072]{1,0:T(8,128)(2,1)S(1)}, u32[]{:S(2)}, u32[]{:S(2)}) %collective-permute-start.16) | collective-permute-done | bytes 344096 | tf_op jit(solution)/shard_map/ppermute | solution.py:134
  80.3 4.9 %collective-permute-start.14 = (bf16[56,3072]{1,0:T(8,128)(2,1)S(1)}, bf16[56,3072]{1,0:T(8,128)(2,1)S(1)}, u32[]{:S(2)}, u32[]{:S(2)}) collective-permute-start(bf16[56,3072]{1,0:T(8,128)(2,1)S(1)} %get-tuple-element.177), channel_id=1, source_target_pairs={{0,2},{2,0},{4,6},{6,4},{1,3},{3,1},{5,7},{7,5},{8,10},{10,8},{12,... | collective-permute-start | bytes 1032200 | tf_op jit(solution)/shard_map/ppermute | solution.py:134
  87.3 5.3 %collective-permute-start.22 = (bf16[56,3072]{1,0:T(8,128)(2,1)S(1)}, bf16[56,3072]{1,0:T(8,128)(2,1)S(1)}, u32[]{:S(2)}, u32[]{:S(2)}) collective-permute-start(bf16[56,3072]{1,0:T(8,128)(2,1)S(1)} %get-tuple-element.174), channel_id=1, source_target_pairs={{0,2},{2,0},{4,6},{6,4},{1,3},{3,1},{5,7},{7,5},{8,10},{10,8},{12,... | collective-permute-start | bytes 1032200 | tf_op jit(solution)/shard_map/ppermute | solution.py:134
  94.7 5.3 %collective-permute-start.20 = (bf16[56,3072]{1,0:T(8,128)(2,1)S(1)}, bf16[56,3072]{1,0:T(8,128)(2,1)S(1)}, u32[]{:S(2)}, u32[]{:S(2)}) collective-permute-start(bf16[56,3072]{1,0:T(8,128)(2,1)S(1)} %get-tuple-element.173), channel_id=1, source_target_pairs={{0,2},{2,0},{4,6},{6,4},{1,3},{3,1},{5,7},{7,5},{8,10},{10,8},{12,... | collective-permute-start | bytes 1032200 | tf_op jit(solution)/shard_map/ppermute | solution.py:134
  101.3 2.5 %collective-permute-start.27 = (bf16[56,3072]{1,0:T(8,128)(2,1)S(1)}, bf16[56,3072]{1,0:T(8,128)(2,1)S(1)}, u32[]{:S(2)}, u32[]{:S(2)}) collective-permute-start(bf16[56,3072]{1,0:T(8,128)(2,1)S(1)} %get-tuple-element.171), channel_id=1, source_target_pairs={{0,2},{2,0},{4,6},{6,4},{1,3},{3,1},{5,7},{7,5},{8,10},{10,8},{12,... | collective-permute-start | bytes 1032200 | tf_op jit(solution)/shard_map/ppermute | solution.py:134
  104.8 4.2 %collective-permute-done.20 = bf16[56,3072]{1,0:T(8,128)(2,1)S(1)} collective-permute-done((bf16[56,3072]{1,0:T(8,128)(2,1)S(1)}, bf16[56,3072]{1,0:T(8,128)(2,1)S(1)}, u32[]{:S(2)}, u32[]{:S(2)}) %collective-permute-start.20) | collective-permute-done | bytes 344096 | tf_op jit(solution)/shard_map/ppermute | solution.py:134
  118.4 2.8 %collective-permute-start.26 = (bf16[56,3072]{1,0:T(8,128)(2,1)S(1)}, bf16[56,3072]{1,0:T(8,128)(2,1)S(1)}, u32[]{:S(2)}, u32[]{:S(2)}) collective-permute-start(bf16[56,3072]{1,0:T(8,128)(2,1)S(1)} %get-tuple-element.164), channel_id=1, source_target_pairs={{0,2},{2,0},{4,6},{6,4},{1,3},{3,1},{5,7},{7,5},{8,10},{10,8},{12,... | collective-permute-start | bytes 1032200 | tf_op jit(solution)/shard_map/ppermute | solution.py:134
  128.0 2.6 %collective-permute-done.26 = bf16[56,3072]{1,0:T(8,128)(2,1)S(1)} collective-permute-done((bf16[56,3072]{1,0:T(8,128)(2,1)S(1)}, bf16[56,3072]{1,0:T(8,128)(2,1)S(1)}, u32[]{:S(2)}, u32[]{:S(2)}) %collective-permute-start.26) | collective-permute-done | bytes 344096 | tf_op jit(solution)/shard_map/ppermute | solution.py:134
  130.8 3.6 %collective-permute-start.33 = (bf16[56,3072]{1,0:T(8,128)(2,1)S(1)}, bf16[56,3072]{1,0:T(8,128)(2,1)S(1)}, u32[]{:S(2)}, u32[]{:S(2)}) collective-permute-start(bf16[56,3072]{1,0:T(8,128)(2,1)S(1)} %maximum_convert_fusion), channel_id=1, source_target_pairs={{0,2},{2,0},{4,6},{6,4},{1,3},{3,1},{5,7},{7,5},{8,10},{10,8},{12,... | collective-permute-start | bytes 1032200 | tf_op jit(solution)/shard_map/ppermute | solution.py:134
  138.7 5.9 %collective-permute-done.33 = bf16[56,3072]{1,0:T(8,128)(2,1)S(1)} collective-permute-done((bf16[56,3072]{1,0:T(8,128)(2,1)S(1)}, bf16[56,3072]{1,0:T(8,128)(2,1)S(1)}, u32[]{:S(2)}, u32[]{:S(2)}) %collective-permute-start.33) | collective-permute-done | bytes 344096 | tf_op jit(solution)/shard_map/ppermute | solution.py:134
  154.6 7.6 %collective-permute-done.40 = bf16[56,3072]{1,0:T(8,128)(2,1)S(1)} collective-permute-done((bf16[56,3072]{1,0:T(8,128)(2,1)S(1)}, bf16[56,3072]{1,0:T(8,128)(2,1)S(1)}, u32[]{:S(2)}, u32[]{:S(2)}) %collective-permute-start.40) | collective-permute-done | bytes 344096 | tf_op jit(solution)/shard_map/ppermute | solution.py:134
  162.2 3.4 %collective-permute-start.37 = (bf16[2,56,576]{2,1,0:T(8,128)(2,1)S(1)}, bf16[2,56,576]{2,1,0:T(8,128)(2,1)S(1)}, u32[]{:S(2)}, u32[]{:S(2)}) collective-permute-start(bf16[2,56,576]{2,1,0:T(8,128)(2,1)S(1)} %get-tuple-element.195), channel_id=1, source_target_pairs={{0,8},{16,24},{1,9},{17,25},{2,10},{18,26},{3,11},{19,27},{4,12},{... | collective-permute-start | bytes 387080 | tf_op jit(solution)/shard_map/ppermute | solution.py:210
  165.6 11.3 %collective-permute-done.41 = bf16[56,3072]{1,0:T(8,128)(2,1)S(1)} collective-permute-done((bf16[56,3072]{1,0:T(8,128)(2,1)S(1)}, bf16[56,3072]{1,0:T(8,128)(2,1)S(1)}, u32[]{:S(2)}, u32[]{:S(2)}) %collective-permute-start.41) | collective-permute-done | bytes 344096 | tf_op jit(solution)/shard_map/ppermute | solution.py:134
  176.9 3.4 %collective-permute-start.38 = (bf16[2,56,576]{2,1,0:T(8,128)(2,1)S(1)}, bf16[2,56,576]{2,1,0:T(8,128)(2,1)S(1)}, u32[]{:S(2)}, u32[]{:S(2)}) collective-permute-start(bf16[2,56,576]{2,1,0:T(8,128)(2,1)S(1)} %get-tuple-element.194), channel_id=1, source_target_pairs={{0,16},{8,24},{1,17},{9,25},{2,18},{10,26},{3,19},{11,27},{4,20},{... | collective-permute-start | bytes 387080 | tf_op jit(solution)/shard_map/ppermute | solution.py:210
  182.0 2.2 %collective-permute-start.39 = (bf16[2,56,576]{2,1,0:T(8,128)(2,1)S(1)}, bf16[2,56,576]{2,1,0:T(8,128)(2,1)S(1)}, u32[]{:S(2)}, u32[]{:S(2)}) collective-permute-start(bf16[2,56,576]{2,1,0:T(8,128)(2,1)S(1)} %get-tuple-element.193), channel_id=1, source_target_pairs={{0,24},{8,16},{1,25},{9,17},{2,26},{10,18},{3,27},{11,19},{4,28},{... | collective-permute-start | bytes 387080 | tf_op jit(solution)/shard_map/ppermute | solution.py:210
  196.2 2.5 %collective-permute-start.46 = (bf16[2,56,576]{2,1,0:T(8,128)(2,1)S(1)}, bf16[2,56,576]{2,1,0:T(8,128)(2,1)S(1)}, u32[]{:S(2)}, u32[]{:S(2)}) collective-permute-start(bf16[2,56,576]{2,1,0:T(8,128)(2,1)S(1)} %get-tuple-element.190), channel_id=1, source_target_pairs={{0,8},{16,24},{1,9},{17,25},{2,10},{18,26},{3,11},{19,27},{4,12},{... | collective-permute-start | bytes 387080 | tf_op jit(solution)/shard_map/ppermute | solution.py:210
  198.7 2.6 %collective-permute-start.47 = (bf16[2,56,576]{2,1,0:T(8,128)(2,1)S(1)}, bf16[2,56,576]{2,1,0:T(8,128)(2,1)S(1)}, u32[]{:S(2)}, u32[]{:S(2)}) collective-permute-start(bf16[2,56,576]{2,1,0:T(8,128)(2,1)S(1)} %get-tuple-element.192), channel_id=1, source_target_pairs={{0,16},{8,24},{1,17},{9,25},{2,18},{10,26},{3,19},{11,27},{4,20},{... | collective-permute-start | bytes 387080 | tf_op jit(solution)/shard_map/ppermute | solution.py:210
  203.9 3.4 %collective-permute-done.47 = bf16[2,56,576]{2,1,0:T(8,128)(2,1)S(1)} collective-permute-done((bf16[2,56,576]{2,1,0:T(8,128)(2,1)S(1)}, bf16[2,56,576]{2,1,0:T(8,128)(2,1)S(1)}, u32[]{:S(2)}, u32[]{:S(2)}) %collective-permute-start.47) | collective-permute-done | bytes 129056 | tf_op jit(solution)/shard_map/ppermute | solution.py:210
  (162 shorter events, 75.7 us)
Async XLA Ops:
  22.9 11.9 %collective-permute-start.3 = (bf16[56,3072]{1,0:T(8,128)(2,1)S(1)}, bf16[56,3072]{1,0:T(8,128)(2,1)S(1)}, u32[]{:S(2)}, u32[]{:S(2)}) collective-permute-start(bf16[56,3072]{1,0:T(8,128)(2,1)S(1)} %get-tuple-element.183), channel_id=1, source_target_pairs={{0,2},{6,4},{1,3},{7,5},{8,10},{14,12},{9,11},{15,13},{16,18},{22,... | collective-permute-start | bytes 1032200 | tf_op jit(solution)/shard_map/ppermute | solution.py:134
  26.5 15.7 %collective-permute-start.5 = (bf16[56,3072]{1,0:T(8,128)(2,1)S(1)}, bf16[56,3072]{1,0:T(8,128)(2,1)S(1)}, u32[]{:S(2)}, u32[]{:S(2)}) collective-permute-start(bf16[56,3072]{1,0:T(8,128)(2,1)S(1)} %get-tuple-element.184), channel_id=1, source_target_pairs={{0,2},{6,4},{1,3},{7,5},{8,10},{14,12},{9,11},{15,13},{16,18},{22,... | collective-permute-start | bytes 1032200 | tf_op jit(solution)/shard_map/ppermute | solution.py:134
  27.8 21.7 %collective-permute-start.7 = (bf16[56,3072]{1,0:T(8,128)(2,1)S(1)}, bf16[56,3072]{1,0:T(8,128)(2,1)S(1)}, u32[]{:S(2)}, u32[]{:S(2)}) collective-permute-start(bf16[56,3072]{1,0:T(8,128)(2,1)S(1)} %get-tuple-element.182), channel_id=1, source_target_pairs={{0,2},{6,4},{1,3},{7,5},{8,10},{14,12},{9,11},{15,13},{16,18},{22,... | collective-permute-start | bytes 1032200 | tf_op jit(solution)/shard_map/ppermute | solution.py:134
  29.1 27.8 %collective-permute-start.11 = (bf16[56,3072]{1,0:T(8,128)(2,1)S(1)}, bf16[56,3072]{1,0:T(8,128)(2,1)S(1)}, u32[]{:S(2)}, u32[]{:S(2)}) collective-permute-start(bf16[56,3072]{1,0:T(8,128)(2,1)S(1)} %get-tuple-element.185), channel_id=1, source_target_pairs={{0,2},{6,4},{1,3},{7,5},{8,10},{14,12},{9,11},{15,13},{16,18},{22,... | collective-permute-start | bytes 1032200 | tf_op jit(solution)/shard_map/ppermute | solution.py:134
  34.9 14.6 %collective-permute-start.4 = (bf16[56,3072]{1,0:T(8,128)(2,1)S(1)}, bf16[56,3072]{1,0:T(8,128)(2,1)S(1)}, u32[]{:S(2)}, u32[]{:S(2)}) collective-permute-start(bf16[56,3072]{1,0:T(8,128)(2,1)S(1)} %add_convert_fusion.17), channel_id=1, source_target_pairs={{2,4},{4,2},{3,5},{5,3},{10,12},{12,10},{11,13},{13,11},{18,20},{2... | collective-permute-start | bytes 1032200 | tf_op jit(solution)/shard_map/ppermute | solution.py:134
  42.3 14.6 %collective-permute-start.9 = (bf16[56,3072]{1,0:T(8,128)(2,1)S(1)}, bf16[56,3072]{1,0:T(8,128)(2,1)S(1)}, u32[]{:S(2)}, u32[]{:S(2)}) collective-permute-start(bf16[56,3072]{1,0:T(8,128)(2,1)S(1)} %add_convert_fusion.16), channel_id=1, source_target_pairs={{2,4},{4,2},{3,5},{5,3},{10,12},{12,10},{11,13},{13,11},{18,20},{2... | collective-permute-start | bytes 1032200 | tf_op jit(solution)/shard_map/ppermute | solution.py:134
  49.8 14.5 %collective-permute-start.6 = (bf16[56,3072]{1,0:T(8,128)(2,1)S(1)}, bf16[56,3072]{1,0:T(8,128)(2,1)S(1)}, u32[]{:S(2)}, u32[]{:S(2)}) collective-permute-start(bf16[56,3072]{1,0:T(8,128)(2,1)S(1)} %get-tuple-element.181), channel_id=1, source_target_pairs={{0,2},{2,0},{4,6},{6,4},{1,3},{3,1},{5,7},{7,5},{8,10},{10,8},{12,... | collective-permute-start | bytes 1032200 | tf_op jit(solution)/shard_map/ppermute | solution.py:134
  52.3 11.9 %collective-permute-start.8 = (bf16[56,3072]{1,0:T(8,128)(2,1)S(1)}, bf16[56,3072]{1,0:T(8,128)(2,1)S(1)}, u32[]{:S(2)}, u32[]{:S(2)}) collective-permute-start(bf16[56,3072]{1,0:T(8,128)(2,1)S(1)} %get-tuple-element.180), channel_id=1, source_target_pairs={{2,4},{4,2},{3,5},{5,3},{10,12},{12,10},{11,13},{13,11},{18,20},{2... | collective-permute-start | bytes 1032200 | tf_op jit(solution)/shard_map/ppermute | solution.py:134
  57.1 14.5 %collective-permute-start.10 = (bf16[56,3072]{1,0:T(8,128)(2,1)S(1)}, bf16[56,3072]{1,0:T(8,128)(2,1)S(1)}, u32[]{:S(2)}, u32[]{:S(2)}) collective-permute-start(bf16[56,3072]{1,0:T(8,128)(2,1)S(1)} %get-tuple-element.178), channel_id=1, source_target_pairs={{0,2},{2,0},{4,6},{6,4},{1,3},{3,1},{5,7},{7,5},{8,10},{10,8},{12,... | collective-permute-start | bytes 1032200 | tf_op jit(solution)/shard_map/ppermute | solution.py:134
  59.7 11.9 %collective-permute-start.12 = (bf16[56,3072]{1,0:T(8,128)(2,1)S(1)}, bf16[56,3072]{1,0:T(8,128)(2,1)S(1)}, u32[]{:S(2)}, u32[]{:S(2)}) collective-permute-start(bf16[56,3072]{1,0:T(8,128)(2,1)S(1)} %get-tuple-element.179), channel_id=1, source_target_pairs={{2,4},{4,2},{3,5},{5,3},{10,12},{12,10},{11,13},{13,11},{18,20},{2... | collective-permute-start | bytes 1032200 | tf_op jit(solution)/shard_map/ppermute | solution.py:134
  65.1 14.3 %collective-permute-start.16 = (bf16[56,3072]{1,0:T(8,128)(2,1)S(1)}, bf16[56,3072]{1,0:T(8,128)(2,1)S(1)}, u32[]{:S(2)}, u32[]{:S(2)}) collective-permute-start(bf16[56,3072]{1,0:T(8,128)(2,1)S(1)} %maximum_convert_fusion.3), channel_id=1, source_target_pairs={{0,2},{2,0},{4,6},{6,4},{1,3},{3,1},{5,7},{7,5},{8,10},{10,8},{12,... | collective-permute-start | bytes 1032200 | tf_op jit(solution)/shard_map/ppermute | solution.py:134
  71.8 14.6 %collective-permute-start.17 = (bf16[56,3072]{1,0:T(8,128)(2,1)S(1)}, bf16[56,3072]{1,0:T(8,128)(2,1)S(1)}, u32[]{:S(2)}, u32[]{:S(2)}) collective-permute-start(bf16[56,3072]{1,0:T(8,128)(2,1)S(1)} %maximum_convert_fusion.2), channel_id=1, source_target_pairs={{0,2},{2,0},{4,6},{6,4},{1,3},{3,1},{5,7},{7,5},{8,10},{10,8},{12,... | collective-permute-start | bytes 1032200 | tf_op jit(solution)/shard_map/ppermute | solution.py:134
  74.3 12.0 %collective-permute-start.15 = (bf16[56,3072]{1,0:T(8,128)(2,1)S(1)}, bf16[56,3072]{1,0:T(8,128)(2,1)S(1)}, u32[]{:S(2)}, u32[]{:S(2)}) collective-permute-start(bf16[56,3072]{1,0:T(8,128)(2,1)S(1)} %maximum_convert_fusion.2), channel_id=1, source_target_pairs={{2,4},{4,2},{3,5},{5,3},{10,12},{12,10},{11,13},{13,11},{18,20},{2... | collective-permute-start | bytes 1032200 | tf_op jit(solution)/shard_map/ppermute | solution.py:134
  79.6 13.0 %collective-permute-start.19 = (bf16[56,3072]{1,0:T(8,128)(2,1)S(1)}, bf16[56,3072]{1,0:T(8,128)(2,1)S(1)}, u32[]{:S(2)}, u32[]{:S(2)}) collective-permute-start(bf16[56,3072]{1,0:T(8,128)(2,1)S(1)} %get-tuple-element.176), channel_id=1, source_target_pairs={{2,4},{4,2},{3,5},{5,3},{10,12},{12,10},{11,13},{13,11},{18,20},{2... | collective-permute-start | bytes 1032200 | tf_op jit(solution)/shard_map/ppermute | solution.py:134
  80.3 13.4 %collective-permute-start.14 = (bf16[56,3072]{1,0:T(8,128)(2,1)S(1)}, bf16[56,3072]{1,0:T(8,128)(2,1)S(1)}, u32[]{:S(2)}, u32[]{:S(2)}) collective-permute-start(bf16[56,3072]{1,0:T(8,128)(2,1)S(1)} %get-tuple-element.177), channel_id=1, source_target_pairs={{0,2},{2,0},{4,6},{6,4},{1,3},{3,1},{5,7},{7,5},{8,10},{10,8},{12,... | collective-permute-start | bytes 1032200 | tf_op jit(solution)/shard_map/ppermute | solution.py:134
  86.6 13.3 %collective-permute-start.21 = (bf16[56,3072]{1,0:T(8,128)(2,1)S(1)}, bf16[56,3072]{1,0:T(8,128)(2,1)S(1)}, u32[]{:S(2)}, u32[]{:S(2)}) collective-permute-start(bf16[56,3072]{1,0:T(8,128)(2,1)S(1)} %get-tuple-element.175), channel_id=1, source_target_pairs={{2,4},{4,2},{3,5},{5,3},{10,12},{12,10},{11,13},{13,11},{18,20},{2... | collective-permute-start | bytes 1032200 | tf_op jit(solution)/shard_map/ppermute | solution.py:134
  87.3 13.8 %collective-permute-start.22 = (bf16[56,3072]{1,0:T(8,128)(2,1)S(1)}, bf16[56,3072]{1,0:T(8,128)(2,1)S(1)}, u32[]{:S(2)}, u32[]{:S(2)}) collective-permute-start(bf16[56,3072]{1,0:T(8,128)(2,1)S(1)} %get-tuple-element.174), channel_id=1, source_target_pairs={{0,2},{2,0},{4,6},{6,4},{1,3},{3,1},{5,7},{7,5},{8,10},{10,8},{12,... | collective-permute-start | bytes 1032200 | tf_op jit(solution)/shard_map/ppermute | solution.py:134
  94.7 14.3 %collective-permute-start.20 = (bf16[56,3072]{1,0:T(8,128)(2,1)S(1)}, bf16[56,3072]{1,0:T(8,128)(2,1)S(1)}, u32[]{:S(2)}, u32[]{:S(2)}) collective-permute-start(bf16[56,3072]{1,0:T(8,128)(2,1)S(1)} %get-tuple-element.173), channel_id=1, source_target_pairs={{0,2},{2,0},{4,6},{6,4},{1,3},{3,1},{5,7},{7,5},{8,10},{10,8},{12,... | collective-permute-start | bytes 1032200 | tf_op jit(solution)/shard_map/ppermute | solution.py:134
  101.3 16.8 %collective-permute-start.27 = (bf16[56,3072]{1,0:T(8,128)(2,1)S(1)}, bf16[56,3072]{1,0:T(8,128)(2,1)S(1)}, u32[]{:S(2)}, u32[]{:S(2)}) collective-permute-start(bf16[56,3072]{1,0:T(8,128)(2,1)S(1)} %get-tuple-element.171), channel_id=1, source_target_pairs={{0,2},{2,0},{4,6},{6,4},{1,3},{3,1},{5,7},{7,5},{8,10},{10,8},{12,... | collective-permute-start | bytes 1032200 | tf_op jit(solution)/shard_map/ppermute | solution.py:134
  103.9 14.2 %collective-permute-start.25 = (bf16[56,3072]{1,0:T(8,128)(2,1)S(1)}, bf16[56,3072]{1,0:T(8,128)(2,1)S(1)}, u32[]{:S(2)}, u32[]{:S(2)}) collective-permute-start(bf16[56,3072]{1,0:T(8,128)(2,1)S(1)} %get-tuple-element.170), channel_id=1, source_target_pairs={{2,4},{4,2},{3,5},{5,3},{10,12},{12,10},{11,13},{13,11},{18,20},{2... | collective-permute-start | bytes 1032200 | tf_op jit(solution)/shard_map/ppermute | solution.py:134
  112.4 12.6 %collective-permute-start.23 = (bf16[56,3072]{1,0:T(8,128)(2,1)S(1)}, bf16[56,3072]{1,0:T(8,128)(2,1)S(1)}, u32[]{:S(2)}, u32[]{:S(2)}) collective-permute-start(bf16[56,3072]{1,0:T(8,128)(2,1)S(1)} %get-tuple-element.167), channel_id=1, source_target_pairs={{0,2},{2,0},{4,6},{6,4},{1,3},{3,1},{5,7},{7,5},{8,10},{10,8},{12,... | collective-permute-start | bytes 1032200 | tf_op jit(solution)/shard_map/ppermute | solution.py:134
  118.4 12.2 %collective-permute-start.26 = (bf16[56,3072]{1,0:T(8,128)(2,1)S(1)}, bf16[56,3072]{1,0:T(8,128)(2,1)S(1)}, u32[]{:S(2)}, u32[]{:S(2)}) collective-permute-start(bf16[56,3072]{1,0:T(8,128)(2,1)S(1)} %get-tuple-element.164), channel_id=1, source_target_pairs={{0,2},{2,0},{4,6},{6,4},{1,3},{3,1},{5,7},{7,5},{8,10},{10,8},{12,... | collective-permute-start | bytes 1032200 | tf_op jit(solution)/shard_map/ppermute | solution.py:134
  125.2 12.7 %collective-permute-start.29 = (bf16[56,3072]{1,0:T(8,128)(2,1)S(1)}, bf16[56,3072]{1,0:T(8,128)(2,1)S(1)}, u32[]{:S(2)}, u32[]{:S(2)}) collective-permute-start(bf16[56,3072]{1,0:T(8,128)(2,1)S(1)} %maximum_convert_fusion.1), channel_id=1, source_target_pairs={{0,2},{2,0},{4,6},{6,4},{1,3},{3,1},{5,7},{7,5},{8,10},{10,8},{12,... | collective-permute-start | bytes 1032200 | tf_op jit(solution)/shard_map/ppermute | solution.py:134
  130.8 13.8 %collective-permute-start.33 = (bf16[56,3072]{1,0:T(8,128)(2,1)S(1)}, bf16[56,3072]{1,0:T(8,128)(2,1)S(1)}, u32[]{:S(2)}, u32[]{:S(2)}) collective-permute-start(bf16[56,3072]{1,0:T(8,128)(2,1)S(1)} %maximum_convert_fusion), channel_id=1, source_target_pairs={{0,2},{2,0},{4,6},{6,4},{1,3},{3,1},{5,7},{7,5},{8,10},{10,8},{12,... | collective-permute-start | bytes 1032200 | tf_op jit(solution)/shard_map/ppermute | solution.py:134
  134.4 13.6 %collective-permute-start.31 = (bf16[56,3072]{1,0:T(8,128)(2,1)S(1)}, bf16[56,3072]{1,0:T(8,128)(2,1)S(1)}, u32[]{:S(2)}, u32[]{:S(2)}) collective-permute-start(bf16[56,3072]{1,0:T(8,128)(2,1)S(1)} %maximum_convert_fusion), channel_id=1, source_target_pairs={{2,4},{4,2},{3,5},{5,3},{10,12},{12,10},{11,13},{13,11},{18,20},{2... | collective-permute-start | bytes 1032200 | tf_op jit(solution)/shard_map/ppermute | solution.py:134
  146.7 15.5 %collective-permute-start.40 = (bf16[56,3072]{1,0:T(8,128)(2,1)S(1)}, bf16[56,3072]{1,0:T(8,128)(2,1)S(1)}, u32[]{:S(2)}, u32[]{:S(2)}) collective-permute-start(bf16[56,3072]{1,0:T(8,128)(2,1)S(1)} %collective-permute-done.32), channel_id=1, source_target_pairs={{2,0},{4,6},{3,1},{5,7},{10,8},{12,14},{11,9},{13,15},{18,16},{20,... | collective-permute-start | bytes 1032200 | tf_op jit(solution)/shard_map/ppermute | solution.py:134
  148.0 34.0 %collective-permute-start.42 = (bf16[56,3072]{1,0:T(8,128)(2,1)S(1)}, bf16[56,3072]{1,0:T(8,128)(2,1)S(1)}, u32[]{:S(2)}, u32[]{:S(2)}) collective-permute-start(bf16[56,3072]{1,0:T(8,128)(2,1)S(1)} %collective-permute-done.31), channel_id=1, source_target_pairs={{2,0},{4,6},{3,1},{5,7},{10,8},{12,14},{11,9},{13,15},{18,16},{20,... | collective-permute-start | bytes 1032200 | tf_op jit(solution)/shard_map/ppermute | solution.py:134
  149.3 27.6 %collective-permute-start.41 = (bf16[56,3072]{1,0:T(8,128)(2,1)S(1)}, bf16[56,3072]{1,0:T(8,128)(2,1)S(1)}, u32[]{:S(2)}, u32[]{:S(2)}) collective-permute-start(bf16[56,3072]{1,0:T(8,128)(2,1)S(1)} %collective-permute-done.30), channel_id=1, source_target_pairs={{2,0},{4,6},{3,1},{5,7},{10,8},{12,14},{11,9},{13,15},{18,16},{20,... | collective-permute-start | bytes 1032200 | tf_op jit(solution)/shard_map/ppermute | solution.py:134
  150.6 33.6 %collective-permute-start.43 = (bf16[56,3072]{1,0:T(8,128)(2,1)S(1)}, bf16[56,3072]{1,0:T(8,128)(2,1)S(1)}, u32[]{:S(2)}, u32[]{:S(2)}) collective-permute-start(bf16[56,3072]{1,0:T(8,128)(2,1)S(1)} %collective-permute-done.34), channel_id=1, source_target_pairs={{2,0},{4,6},{3,1},{5,7},{10,8},{12,14},{11,9},{13,15},{18,16},{20,... | collective-permute-start | bytes 1032200 | tf_op jit(solution)/shard_map/ppermute | solution.py:134
  154.3 38.1 %collective-permute-start.35 = (bf16[1,2,56,576]{3,2,1,0:T(8,128)(2,1)S(1)}, bf16[1,2,56,576]{3,2,1,0:T(8,128)(2,1)S(1)}, u32[]{:S(2)}, u32[]{:S(2)}) collective-permute-start(bf16[1,2,56,576]{3,2,1,0:T(8,128)(2,1)S(1)} %pad_maximum_fusion.12), channel_id=1, source_target_pairs={{0,1},{1,0},{2,3},{3,2},{4,5},{5,4},{6,7},{7,6},{8,9},{9,8},{10,11... | collective-permute-start | bytes 387080 | tf_op jit(solution)/shard_map/ppermute | solution.py:197
  162.2 30.2 %collective-permute-start.37 = (bf16[2,56,576]{2,1,0:T(8,128)(2,1)S(1)}, bf16[2,56,576]{2,1,0:T(8,128)(2,1)S(1)}, u32[]{:S(2)}, u32[]{:S(2)}) collective-permute-start(bf16[2,56,576]{2,1,0:T(8,128)(2,1)S(1)} %get-tuple-element.195), channel_id=1, source_target_pairs={{0,8},{16,24},{1,9},{17,25},{2,10},{18,26},{3,11},{19,27},{4,12},{... | collective-permute-start | bytes 387080 | tf_op jit(solution)/shard_map/ppermute | solution.py:210
  176.9 15.4 %collective-permute-start.38 = (bf16[2,56,576]{2,1,0:T(8,128)(2,1)S(1)}, bf16[2,56,576]{2,1,0:T(8,128)(2,1)S(1)}, u32[]{:S(2)}, u32[]{:S(2)}) collective-permute-start(bf16[2,56,576]{2,1,0:T(8,128)(2,1)S(1)} %get-tuple-element.194), channel_id=1, source_target_pairs={{0,16},{8,24},{1,17},{9,25},{2,18},{10,26},{3,19},{11,27},{4,20},{... | collective-permute-start | bytes 387080 | tf_op jit(solution)/shard_map/ppermute | solution.py:210
  (26 other events, 644.3 us)
where the time goes:
time: 209 us; the launch traced here: 208 us
  starting transfers between devices  87.3 us (42%)
  waiting for transfers between devices  75.2 us (36%)
  matrix products  30.4 us (15%)
  other arithmetic  7.08 us (3%)
  blocking collectives  4.68 us (2%)
  local copies, waits for them, and re-layouts  2.24 us (1%)
    ppermute x36, starting transfers between devices, swap(): return lax.ppermute(value, 'feat', pairs) if pairs else None  65.4 us
    ppermute x36, waiting for transfers between devices, swap(): return lax.ppermute(value, 'feat', pairs) if pairs else None  64.6 us
    dot_general x16, matrix products, run(): lax.dot_general(after(codes[key], sent), decoders[layer, :, chunk * width...  23.2 us
    ppermute x6, starting transfers between devices, share_segments(): lax.ppermute(given[-1], 'segment', [(i, j) for i, j in pairs if i < j < s...  15.4 us
    dot_general x4, matrix products, partial_sums(): jnp.dot(columns[group], weight[:, chunk * width:(chunk + 1) * width], pre...  7.17 us
    ppermute x3, starting transfers between devices, exchanged(): part = lax.ppermute(part, 'feat', pairs)  5.6 us
    ppermute x3, waiting for transfers between devices, exchanged(): part = lax.ppermute(part, 'feat', pairs)  5.5 us
  transfers between devices with their start and end apart: 49, of which 20 were waited for; matrix products, arithmetic and copies ran while one was open for 16% of the time, Pallas kernels for 0%

commit v1 on v0

--- a/solution.py
+++ b/solution.py
@@ -49,9 +49,9 @@
 
     columns = exchanged()
 
-    def partial_sums(group, chunk):
+    def partial_sums(group, chunk, sent=None):
         part = jnp.dot(
-            columns[group], weight[:, chunk * width : (chunk + 1) * width], preferred_element_type=F32
+            after(columns[group], sent), weight[:, chunk * width : (chunk + 1) * width], preferred_element_type=F32
         ).astype(BF16)
         return [part[k * rows : (k + 1) * rows] for k in range(ring)]
 
@@ -120,7 +120,7 @@
             self.step = 0
             self.slot = 1
             self.got = [{}, {}]
-            self.sums = partial_sums(*own[0])
+            self.sums = None
 
         def swap(self, value, side):
             i, k, n = self.step, self.slot, len(self.own)
@@ -135,6 +135,8 @@
 
         def advance(self):
             i, k, n = self.step, self.slot, len(self.own)
+            if self.sums is None:
+                self.sums = partial_sums(*self.own[0], ordered)
             sent = []
             for side in range(2):
                 if k == 0:

time: 209 us -> 208 us (level)
  no operation moved by 1% of the time
where the time goes in v1:
time: 208 us; the launch traced here: 207 us
  starting transfers between devices  86.7 us (42%)
  waiting for transfers between devices  74.7 us (36%)
  matrix products  30.3 us (15%)
  other arithmetic  7 us (3%)
  blocking collectives  4.68 us (2%)
    ppermute x36, starting transfers between devices, swap(): return lax.ppermute(value, 'feat', pairs) if pairs else None  64.8 us
    ppermute x36, waiting for transfers between devices, swap(): return lax.ppermute(value, 'feat', pairs) if pairs else None  64.2 us
    dot_general x16, matrix products, run(): lax.dot_general(after(codes[key], sent), decoders[layer, :, chunk * width...  23.2 us
    ppermute x6, starting transfers between devices, share_segments(): lax.ppermute(given[-1], 'segment', [(i, j) for i, j in pairs if i < j < s...  15.5 us
    dot_general x4, matrix products, partial_sums(): jnp.dot(after(columns[group], sent), weight[:, chunk * width:(chunk + 1)...  7.15 us
    ppermute x3, starting transfers between devices, exchanged(): part = lax.ppermute(part, 'feat', pairs)  5.6 us
    ppermute x3, waiting for transfers between devices, exchanged(): part = lax.ppermute(part, 'feat', pairs)  5.5 us
  transfers between devices with their start and end apart: 49, of which 20 were waited for; matrix products, arithmetic and copies ran while one was open for 16% of the time, Pallas kernels for 0%

profile of v1, /device:TPU:0, one launch (start us, length us, event | category | flops | bytes accessed | tf_op | source)
XLA Modules:
  0.0 206.7 jit_solution(11897869187496252622)
XLA Ops:
  0.7 2.5 %all-gather = bf16[1,112,2304]{2,1,0:T(8,128)(2,1)S(1)} all-gather(bf16[1,112,1152]{2,1,0:T(8,128)(2,1)} %param.5), channel_id=2, replica_groups=mesh['segment'=4,'feat'=4,'tok'=2] {'tok'}, dimensions={2}, use_global_device_ids=true | all-gather | bytes 774144 | tf_op jit(solution)/shard_map/all_gather | solution.py:27
  3.3 3.0 %collective-permute-start = (bf16[56,576]{1,0:T(8,128)(2,1)S(1)}, bf16[56,576]{1,0:T(8,128)(2,1)S(1)}, u32[]{:S(2)}, u32[]{:S(2)}) collective-permute-start(bf16[56,576]{1,0:T(8,128)(2,1)S(1)} %get-tuple-element.216), channel_id=1, source_target_pairs={{0,2},{2,0},{4,6},{6,4},{1,3},{3,1},{5,7},{7,5},{8,10},{10,8},{12,... | collective-permute-start | bytes 193544 | tf_op jit(solution)/shard_map/ppermute | solution.py:40
  6.3 2.6 %collective-permute-start.1 = (bf16[56,576]{1,0:T(8,128)(2,1)S(1)}, bf16[56,576]{1,0:T(8,128)(2,1)S(1)}, u32[]{:S(2)}, u32[]{:S(2)}) collective-permute-start(bf16[56,576]{1,0:T(8,128)(2,1)S(1)} %get-tuple-element.215), channel_id=1, source_target_pairs={{0,4},{2,6},{4,0},{6,2},{1,5},{3,7},{5,1},{7,3},{8,12},{10,14},{12... | collective-permute-start | bytes 193544 | tf_op jit(solution)/shard_map/ppermute | solution.py:40
  9.7 4.6 %collective-permute-done.1 = bf16[56,576]{1,0:T(8,128)(2,1)S(1)} collective-permute-done((bf16[56,576]{1,0:T(8,128)(2,1)S(1)}, bf16[56,576]{1,0:T(8,128)(2,1)S(1)}, u32[]{:S(2)}, u32[]{:S(2)}) %collective-permute-start.1) | collective-permute-done | bytes 64544 | tf_op jit(solution)/shard_map/ppermute | solution.py:40
  17.6 3.4 %convolution_convert_fusion.3 = bf16[224,3072]{1,0:T(8,128)(2,1)S(1)} fusion(bf16[576,6144]{1,0:T(8,128)(2,1)} %bitcast.175, bf16[56,576]{1,0:T(8,128)(2,1)S(1)} %get-tuple-element.207, bf16[56,576]{1,0:T(8,128)(2,1)S(1)} %get-tuple-element.208, bf16[56,576]{1,0:T(8,128)(2,1)S(1)} %get-tuple-element.209, bf16[56,576]{1,0:T(8,128)(2,1)S(1)} %get-tuple-element.210), kind=kOutput, calls=%fused_computation.3 | convolution fusion | flops 794443776 | bytes 5173248 | tf_op jit(solution)/shard_map/dot_general | solution.py:53
  21.1 3.6 %collective-permute-start.3 = (bf16[56,3072]{1,0:T(8,128)(2,1)S(1)}, bf16[56,3072]{1,0:T(8,128)(2,1)S(1)}, u32[]{:S(2)}, u32[]{:S(2)}) collective-permute-start(bf16[56,3072]{1,0:T(8,128)(2,1)S(1)} %get-tuple-element.185), channel_id=1, source_target_pairs={{0,2},{6,4},{1,3},{7,5},{8,10},{14,12},{9,11},{15,13},{16,18},{22,... | collective-permute-start | bytes 1032200 | tf_op jit(solution)/shard_map/ppermute | solution.py:134
  33.9 6.5 %collective-permute-done.5 = bf16[56,3072]{1,0:T(8,128)(2,1)S(1)} collective-permute-done((bf16[56,3072]{1,0:T(8,128)(2,1)S(1)}, bf16[56,3072]{1,0:T(8,128)(2,1)S(1)}, u32[]{:S(2)}, u32[]{:S(2)}) %collective-permute-start.5) | collective-permute-done | bytes 344096 | tf_op jit(solution)/shard_map/ppermute | solution.py:134
  41.3 6.5 %collective-permute-done.7 = bf16[56,3072]{1,0:T(8,128)(2,1)S(1)} collective-permute-done((bf16[56,3072]{1,0:T(8,128)(2,1)S(1)}, bf16[56,3072]{1,0:T(8,128)(2,1)S(1)}, u32[]{:S(2)}, u32[]{:S(2)}) %collective-permute-start.7) | collective-permute-done | bytes 344096 | tf_op jit(solution)/shard_map/ppermute | solution.py:134
  48.1 2.5 %collective-permute-start.6 = (bf16[56,3072]{1,0:T(8,128)(2,1)S(1)}, bf16[56,3072]{1,0:T(8,128)(2,1)S(1)}, u32[]{:S(2)}, u32[]{:S(2)}) collective-permute-start(bf16[56,3072]{1,0:T(8,128)(2,1)S(1)} %get-tuple-element.183), channel_id=1, source_target_pairs={{0,2},{2,0},{4,6},{6,4},{1,3},{3,1},{5,7},{7,5},{8,10},{10,8},{12,... | collective-permute-start | bytes 1032200 | tf_op jit(solution)/shard_map/ppermute | solution.py:134
  51.3 3.9 %collective-permute-done.11 = bf16[56,3072]{1,0:T(8,128)(2,1)S(1)} collective-permute-done((bf16[56,3072]{1,0:T(8,128)(2,1)S(1)}, bf16[56,3072]{1,0:T(8,128)(2,1)S(1)}, u32[]{:S(2)}, u32[]{:S(2)}) %collective-permute-start.11) | collective-permute-done | bytes 344096 | tf_op jit(solution)/shard_map/ppermute | solution.py:134
  55.5 2.5 %collective-permute-start.10 = (bf16[56,3072]{1,0:T(8,128)(2,1)S(1)}, bf16[56,3072]{1,0:T(8,128)(2,1)S(1)}, u32[]{:S(2)}, u32[]{:S(2)}) collective-permute-start(bf16[56,3072]{1,0:T(8,128)(2,1)S(1)} %get-tuple-element.180), channel_id=1, source_target_pairs={{0,2},{2,0},{4,6},{6,4},{1,3},{3,1},{5,7},{7,5},{8,10},{10,8},{12,... | collective-permute-start | bytes 1032200 | tf_op jit(solution)/shard_map/ppermute | solution.py:134
  58.7 3.9 %collective-permute-done.6 = bf16[56,3072]{1,0:T(8,128)(2,1)S(1)} collective-permute-done((bf16[56,3072]{1,0:T(8,128)(2,1)S(1)}, bf16[56,3072]{1,0:T(8,128)(2,1)S(1)}, u32[]{:S(2)}, u32[]{:S(2)}) %collective-permute-start.6) | collective-permute-done | bytes 344096 | tf_op jit(solution)/shard_map/ppermute | solution.py:134
  63.6 5.4 %collective-permute-start.16 = (bf16[56,3072]{1,0:T(8,128)(2,1)S(1)}, bf16[56,3072]{1,0:T(8,128)(2,1)S(1)}, u32[]{:S(2)}, u32[]{:S(2)}) collective-permute-start(bf16[56,3072]{1,0:T(8,128)(2,1)S(1)} %maximum_convert_fusion.3), channel_id=1, source_target_pairs={{0,2},{2,0},{4,6},{6,4},{1,3},{3,1},{5,7},{7,5},{8,10},{10,8},{12,... | collective-permute-start | bytes 1032200 | tf_op jit(solution)/shard_map/ppermute | solution.py:134
  70.2 2.5 %collective-permute-start.17 = (bf16[56,3072]{1,0:T(8,128)(2,1)S(1)}, bf16[56,3072]{1,0:T(8,128)(2,1)S(1)}, u32[]{:S(2)}, u32[]{:S(2)}) collective-permute-start(bf16[56,3072]{1,0:T(8,128)(2,1)S(1)} %maximum_convert_fusion.2), channel_id=1, source_target_pairs={{0,2},{2,0},{4,6},{6,4},{1,3},{3,1},{5,7},{7,5},{8,10},{10,8},{12,... | collective-permute-start | bytes 1032200 | tf_op jit(solution)/shard_map/ppermute | solution.py:134
  73.4 4.6 %collective-permute-done.16 = bf16[56,3072]{1,0:T(8,128)(2,1)S(1)} collective-permute-done((bf16[56,3072]{1,0:T(8,128)(2,1)S(1)}, bf16[56,3072]{1,0:T(8,128)(2,1)S(1)}, u32[]{:S(2)}, u32[]{:S(2)}) %collective-permute-start.16) | collective-permute-done | bytes 344096 | tf_op jit(solution)/shard_map/ppermute | solution.py:134
  78.9 4.6 %collective-permute-start.14 = (bf16[56,3072]{1,0:T(8,128)(2,1)S(1)}, bf16[56,3072]{1,0:T(8,128)(2,1)S(1)}, u32[]{:S(2)}, u32[]{:S(2)}) collective-permute-start(bf16[56,3072]{1,0:T(8,128)(2,1)S(1)} %get-tuple-element.179), channel_id=1, source_target_pairs={{0,2},{2,0},{4,6},{6,4},{1,3},{3,1},{5,7},{7,5},{8,10},{10,8},{12,... | collective-permute-start | bytes 1032200 | tf_op jit(solution)/shard_map/ppermute | solution.py:134
  85.9 5.1 %collective-permute-start.22 = (bf16[56,3072]{1,0:T(8,128)(2,1)S(1)}, bf16[56,3072]{1,0:T(8,128)(2,1)S(1)}, u32[]{:S(2)}, u32[]{:S(2)}) collective-permute-start(bf16[56,3072]{1,0:T(8,128)(2,1)S(1)} %get-tuple-element.176), channel_id=1, source_target_pairs={{0,2},{2,0},{4,6},{6,4},{1,3},{3,1},{5,7},{7,5},{8,10},{10,8},{12,... | collective-permute-start | bytes 1032200 | tf_op jit(solution)/shard_map/ppermute | solution.py:134
  93.2 5.1 %collective-permute-start.20 = (bf16[56,3072]{1,0:T(8,128)(2,1)S(1)}, bf16[56,3072]{1,0:T(8,128)(2,1)S(1)}, u32[]{:S(2)}, u32[]{:S(2)}) collective-permute-start(bf16[56,3072]{1,0:T(8,128)(2,1)S(1)} %get-tuple-element.175), channel_id=1, source_target_pairs={{0,2},{2,0},{4,6},{6,4},{1,3},{3,1},{5,7},{7,5},{8,10},{10,8},{12,... | collective-permute-start | bytes 1032200 | tf_op jit(solution)/shard_map/ppermute | solution.py:134
  99.9 2.5 %collective-permute-start.27 = (bf16[56,3072]{1,0:T(8,128)(2,1)S(1)}, bf16[56,3072]{1,0:T(8,128)(2,1)S(1)}, u32[]{:S(2)}, u32[]{:S(2)}) collective-permute-start(bf16[56,3072]{1,0:T(8,128)(2,1)S(1)} %get-tuple-element.173), channel_id=1, source_target_pairs={{0,2},{2,0},{4,6},{6,4},{1,3},{3,1},{5,7},{7,5},{8,10},{10,8},{12,... | collective-permute-start | bytes 1032200 | tf_op jit(solution)/shard_map/ppermute | solution.py:134
  103.3 4.0 %collective-permute-done.20 = bf16[56,3072]{1,0:T(8,128)(2,1)S(1)} collective-permute-done((bf16[56,3072]{1,0:T(8,128)(2,1)S(1)}, bf16[56,3072]{1,0:T(8,128)(2,1)S(1)}, u32[]{:S(2)}, u32[]{:S(2)}) %collective-permute-start.20) | collective-permute-done | bytes 344096 | tf_op jit(solution)/shard_map/ppermute | solution.py:134
  110.7 2.3 %collective-permute-start.23 = (bf16[56,3072]{1,0:T(8,128)(2,1)S(1)}, bf16[56,3072]{1,0:T(8,128)(2,1)S(1)}, u32[]{:S(2)}, u32[]{:S(2)}) collective-permute-start(bf16[56,3072]{1,0:T(8,128)(2,1)S(1)} %get-tuple-element.169), channel_id=1, source_target_pairs={{0,2},{2,0},{4,6},{6,4},{1,3},{3,1},{5,7},{7,5},{8,10},{10,8},{12,... | collective-permute-start | bytes 1032200 | tf_op jit(solution)/shard_map/ppermute | solution.py:134
  116.9 2.6 %collective-permute-start.26 = (bf16[56,3072]{1,0:T(8,128)(2,1)S(1)}, bf16[56,3072]{1,0:T(8,128)(2,1)S(1)}, u32[]{:S(2)}, u32[]{:S(2)}) collective-permute-start(bf16[56,3072]{1,0:T(8,128)(2,1)S(1)} %get-tuple-element.166), channel_id=1, source_target_pairs={{0,2},{2,0},{4,6},{6,4},{1,3},{3,1},{5,7},{7,5},{8,10},{10,8},{12,... | collective-permute-start | bytes 1032200 | tf_op jit(solution)/shard_map/ppermute | solution.py:134
  126.3 2.9 %collective-permute-done.26 = bf16[56,3072]{1,0:T(8,128)(2,1)S(1)} collective-permute-done((bf16[56,3072]{1,0:T(8,128)(2,1)S(1)}, bf16[56,3072]{1,0:T(8,128)(2,1)S(1)}, u32[]{:S(2)}, u32[]{:S(2)}) %collective-permute-start.26) | collective-permute-done | bytes 344096 | tf_op jit(solution)/shard_map/ppermute | solution.py:134
  129.3 3.3 %collective-permute-start.33 = (bf16[56,3072]{1,0:T(8,128)(2,1)S(1)}, bf16[56,3072]{1,0:T(8,128)(2,1)S(1)}, u32[]{:S(2)}, u32[]{:S(2)}) collective-permute-start(bf16[56,3072]{1,0:T(8,128)(2,1)S(1)} %maximum_convert_fusion), channel_id=1, source_target_pairs={{0,2},{2,0},{4,6},{6,4},{1,3},{3,1},{5,7},{7,5},{8,10},{10,8},{12,... | collective-permute-start | bytes 1032200 | tf_op jit(solution)/shard_map/ppermute | solution.py:134
  137.2 5.7 %collective-permute-done.33 = bf16[56,3072]{1,0:T(8,128)(2,1)S(1)} collective-permute-done((bf16[56,3072]{1,0:T(8,128)(2,1)S(1)}, bf16[56,3072]{1,0:T(8,128)(2,1)S(1)}, u32[]{:S(2)}, u32[]{:S(2)}) %collective-permute-start.33) | collective-permute-done | bytes 344096 | tf_op jit(solution)/shard_map/ppermute | solution.py:134
  152.9 7.6 %collective-permute-done.40 = bf16[56,3072]{1,0:T(8,128)(2,1)S(1)} collective-permute-done((bf16[56,3072]{1,0:T(8,128)(2,1)S(1)}, bf16[56,3072]{1,0:T(8,128)(2,1)S(1)}, u32[]{:S(2)}, u32[]{:S(2)}) %collective-permute-start.40) | collective-permute-done | bytes 344096 | tf_op jit(solution)/shard_map/ppermute | solution.py:134
  160.5 3.4 %collective-permute-start.37 = (bf16[2,56,576]{2,1,0:T(8,128)(2,1)S(1)}, bf16[2,56,576]{2,1,0:T(8,128)(2,1)S(1)}, u32[]{:S(2)}, u32[]{:S(2)}) collective-permute-start(bf16[2,56,576]{2,1,0:T(8,128)(2,1)S(1)} %get-tuple-element.197), channel_id=1, source_target_pairs={{0,8},{16,24},{1,9},{17,25},{2,10},{18,26},{3,11},{19,27},{4,12},{... | collective-permute-start | bytes 387080 | tf_op jit(solution)/shard_map/ppermute | solution.py:212
  163.9 11.3 %collective-permute-done.41 = bf16[56,3072]{1,0:T(8,128)(2,1)S(1)} collective-permute-done((bf16[56,3072]{1,0:T(8,128)(2,1)S(1)}, bf16[56,3072]{1,0:T(8,128)(2,1)S(1)}, u32[]{:S(2)}, u32[]{:S(2)}) %collective-permute-start.41) | collective-permute-done | bytes 344096 | tf_op jit(solution)/shard_map/ppermute | solution.py:134
  175.3 3.4 %collective-permute-start.38 = (bf16[2,56,576]{2,1,0:T(8,128)(2,1)S(1)}, bf16[2,56,576]{2,1,0:T(8,128)(2,1)S(1)}, u32[]{:S(2)}, u32[]{:S(2)}) collective-permute-start(bf16[2,56,576]{2,1,0:T(8,128)(2,1)S(1)} %get-tuple-element.196), channel_id=1, source_target_pairs={{0,16},{8,24},{1,17},{9,25},{2,18},{10,26},{3,19},{11,27},{4,20},{... | collective-permute-start | bytes 387080 | tf_op jit(solution)/shard_map/ppermute | solution.py:212
  194.5 2.5 %collective-permute-start.46 = (bf16[2,56,576]{2,1,0:T(8,128)(2,1)S(1)}, bf16[2,56,576]{2,1,0:T(8,128)(2,1)S(1)}, u32[]{:S(2)}, u32[]{:S(2)}) collective-permute-start(bf16[2,56,576]{2,1,0:T(8,128)(2,1)S(1)} %get-tuple-element.192), channel_id=1, source_target_pairs={{0,8},{16,24},{1,9},{17,25},{2,10},{18,26},{3,11},{19,27},{4,12},{... | collective-permute-start | bytes 387080 | tf_op jit(solution)/shard_map/ppermute | solution.py:212
  197.0 2.6 %collective-permute-start.47 = (bf16[2,56,576]{2,1,0:T(8,128)(2,1)S(1)}, bf16[2,56,576]{2,1,0:T(8,128)(2,1)S(1)}, u32[]{:S(2)}, u32[]{:S(2)}) collective-permute-start(bf16[2,56,576]{2,1,0:T(8,128)(2,1)S(1)} %get-tuple-element.194), channel_id=1, source_target_pairs={{0,16},{8,24},{1,17},{9,25},{2,18},{10,26},{3,19},{11,27},{4,20},{... | collective-permute-start | bytes 387080 | tf_op jit(solution)/shard_map/ppermute | solution.py:212
  202.1 3.4 %collective-permute-done.47 = bf16[2,56,576]{2,1,0:T(8,128)(2,1)S(1)} collective-permute-done((bf16[2,56,576]{2,1,0:T(8,128)(2,1)S(1)}, bf16[2,56,576]{2,1,0:T(8,128)(2,1)S(1)}, u32[]{:S(2)}, u32[]{:S(2)}) %collective-permute-start.47) | collective-permute-done | bytes 129056 | tf_op jit(solution)/shard_map/ppermute | solution.py:212
  (163 shorter events, 74.4 us)
Async XLA Ops:
  21.1 12.0 %collective-permute-start.3 = (bf16[56,3072]{1,0:T(8,128)(2,1)S(1)}, bf16[56,3072]{1,0:T(8,128)(2,1)S(1)}, u32[]{:S(2)}, u32[]{:S(2)}) collective-permute-start(bf16[56,3072]{1,0:T(8,128)(2,1)S(1)} %get-tuple-element.185), channel_id=1, source_target_pairs={{0,2},{6,4},{1,3},{7,5},{8,10},{14,12},{9,11},{15,13},{16,18},{22,... | collective-permute-start | bytes 1032200 | tf_op jit(solution)/shard_map/ppermute | solution.py:134
  26.1 14.4 %collective-permute-start.5 = (bf16[56,3072]{1,0:T(8,128)(2,1)S(1)}, bf16[56,3072]{1,0:T(8,128)(2,1)S(1)}, u32[]{:S(2)}, u32[]{:S(2)}) collective-permute-start(bf16[56,3072]{1,0:T(8,128)(2,1)S(1)} %get-tuple-element.186), channel_id=1, source_target_pairs={{0,2},{6,4},{1,3},{7,5},{8,10},{14,12},{9,11},{15,13},{16,18},{22,... | collective-permute-start | bytes 1032200 | tf_op jit(solution)/shard_map/ppermute | solution.py:134
  27.4 20.5 %collective-permute-start.7 = (bf16[56,3072]{1,0:T(8,128)(2,1)S(1)}, bf16[56,3072]{1,0:T(8,128)(2,1)S(1)}, u32[]{:S(2)}, u32[]{:S(2)}) collective-permute-start(bf16[56,3072]{1,0:T(8,128)(2,1)S(1)} %get-tuple-element.184), channel_id=1, source_target_pairs={{0,2},{6,4},{1,3},{7,5},{8,10},{14,12},{9,11},{15,13},{16,18},{22,... | collective-permute-start | bytes 1032200 | tf_op jit(solution)/shard_map/ppermute | solution.py:134
  28.7 26.5 %collective-permute-start.11 = (bf16[56,3072]{1,0:T(8,128)(2,1)S(1)}, bf16[56,3072]{1,0:T(8,128)(2,1)S(1)}, u32[]{:S(2)}, u32[]{:S(2)}) collective-permute-start(bf16[56,3072]{1,0:T(8,128)(2,1)S(1)} %get-tuple-element.187), channel_id=1, source_target_pairs={{0,2},{6,4},{1,3},{7,5},{8,10},{14,12},{9,11},{15,13},{16,18},{22,... | collective-permute-start | bytes 1032200 | tf_op jit(solution)/shard_map/ppermute | solution.py:134
  33.3 14.6 %collective-permute-start.4 = (bf16[56,3072]{1,0:T(8,128)(2,1)S(1)}, bf16[56,3072]{1,0:T(8,128)(2,1)S(1)}, u32[]{:S(2)}, u32[]{:S(2)}) collective-permute-start(bf16[56,3072]{1,0:T(8,128)(2,1)S(1)} %add_convert_fusion.17), channel_id=1, source_target_pairs={{2,4},{4,2},{3,5},{5,3},{10,12},{12,10},{11,13},{13,11},{18,20},{2... | collective-permute-start | bytes 1032200 | tf_op jit(solution)/shard_map/ppermute | solution.py:134
  40.6 14.6 %collective-permute-start.9 = (bf16[56,3072]{1,0:T(8,128)(2,1)S(1)}, bf16[56,3072]{1,0:T(8,128)(2,1)S(1)}, u32[]{:S(2)}, u32[]{:S(2)}) collective-permute-start(bf16[56,3072]{1,0:T(8,128)(2,1)S(1)} %add_convert_fusion.16), channel_id=1, source_target_pairs={{2,4},{4,2},{3,5},{5,3},{10,12},{12,10},{11,13},{13,11},{18,20},{2... | collective-permute-start | bytes 1032200 | tf_op jit(solution)/shard_map/ppermute | solution.py:134
  48.1 14.5 %collective-permute-start.6 = (bf16[56,3072]{1,0:T(8,128)(2,1)S(1)}, bf16[56,3072]{1,0:T(8,128)(2,1)S(1)}, u32[]{:S(2)}, u32[]{:S(2)}) collective-permute-start(bf16[56,3072]{1,0:T(8,128)(2,1)S(1)} %get-tuple-element.183), channel_id=1, source_target_pairs={{0,2},{2,0},{4,6},{6,4},{1,3},{3,1},{5,7},{7,5},{8,10},{10,8},{12,... | collective-permute-start | bytes 1032200 | tf_op jit(solution)/shard_map/ppermute | solution.py:134
  50.7 11.9 %collective-permute-start.8 = (bf16[56,3072]{1,0:T(8,128)(2,1)S(1)}, bf16[56,3072]{1,0:T(8,128)(2,1)S(1)}, u32[]{:S(2)}, u32[]{:S(2)}) collective-permute-start(bf16[56,3072]{1,0:T(8,128)(2,1)S(1)} %get-tuple-element.182), channel_id=1, source_target_pairs={{2,4},{4,2},{3,5},{5,3},{10,12},{12,10},{11,13},{13,11},{18,20},{2... | collective-permute-start | bytes 1032200 | tf_op jit(solution)/shard_map/ppermute | solution.py:134
  55.5 14.5 %collective-permute-start.10 = (bf16[56,3072]{1,0:T(8,128)(2,1)S(1)}, bf16[56,3072]{1,0:T(8,128)(2,1)S(1)}, u32[]{:S(2)}, u32[]{:S(2)}) collective-permute-start(bf16[56,3072]{1,0:T(8,128)(2,1)S(1)} %get-tuple-element.180), channel_id=1, source_target_pairs={{0,2},{2,0},{4,6},{6,4},{1,3},{3,1},{5,7},{7,5},{8,10},{10,8},{12,... | collective-permute-start | bytes 1032200 | tf_op jit(solution)/shard_map/ppermute | solution.py:134
  58.0 11.9 %collective-permute-start.12 = (bf16[56,3072]{1,0:T(8,128)(2,1)S(1)}, bf16[56,3072]{1,0:T(8,128)(2,1)S(1)}, u32[]{:S(2)}, u32[]{:S(2)}) collective-permute-start(bf16[56,3072]{1,0:T(8,128)(2,1)S(1)} %get-tuple-element.181), channel_id=1, source_target_pairs={{2,4},{4,2},{3,5},{5,3},{10,12},{12,10},{11,13},{13,11},{18,20},{2... | collective-permute-start | bytes 1032200 | tf_op jit(solution)/shard_map/ppermute | solution.py:134
  63.6 14.4 %collective-permute-start.16 = (bf16[56,3072]{1,0:T(8,128)(2,1)S(1)}, bf16[56,3072]{1,0:T(8,128)(2,1)S(1)}, u32[]{:S(2)}, u32[]{:S(2)}) collective-permute-start(bf16[56,3072]{1,0:T(8,128)(2,1)S(1)} %maximum_convert_fusion.3), channel_id=1, source_target_pairs={{0,2},{2,0},{4,6},{6,4},{1,3},{3,1},{5,7},{7,5},{8,10},{10,8},{12,... | collective-permute-start | bytes 1032200 | tf_op jit(solution)/shard_map/ppermute | solution.py:134
  70.2 14.8 %collective-permute-start.17 = (bf16[56,3072]{1,0:T(8,128)(2,1)S(1)}, bf16[56,3072]{1,0:T(8,128)(2,1)S(1)}, u32[]{:S(2)}, u32[]{:S(2)}) collective-permute-start(bf16[56,3072]{1,0:T(8,128)(2,1)S(1)} %maximum_convert_fusion.2), channel_id=1, source_target_pairs={{0,2},{2,0},{4,6},{6,4},{1,3},{3,1},{5,7},{7,5},{8,10},{10,8},{12,... | collective-permute-start | bytes 1032200 | tf_op jit(solution)/shard_map/ppermute | solution.py:134
  72.7 12.2 %collective-permute-start.15 = (bf16[56,3072]{1,0:T(8,128)(2,1)S(1)}, bf16[56,3072]{1,0:T(8,128)(2,1)S(1)}, u32[]{:S(2)}, u32[]{:S(2)}) collective-permute-start(bf16[56,3072]{1,0:T(8,128)(2,1)S(1)} %maximum_convert_fusion.2), channel_id=1, source_target_pairs={{2,4},{4,2},{3,5},{5,3},{10,12},{12,10},{11,13},{13,11},{18,20},{2... | collective-permute-start | bytes 1032200 | tf_op jit(solution)/shard_map/ppermute | solution.py:134
  78.3 12.7 %collective-permute-start.19 = (bf16[56,3072]{1,0:T(8,128)(2,1)S(1)}, bf16[56,3072]{1,0:T(8,128)(2,1)S(1)}, u32[]{:S(2)}, u32[]{:S(2)}) collective-permute-start(bf16[56,3072]{1,0:T(8,128)(2,1)S(1)} %get-tuple-element.178), channel_id=1, source_target_pairs={{2,4},{4,2},{3,5},{5,3},{10,12},{12,10},{11,13},{13,11},{18,20},{2... | collective-permute-start | bytes 1032200 | tf_op jit(solution)/shard_map/ppermute | solution.py:134
  78.9 13.3 %collective-permute-start.14 = (bf16[56,3072]{1,0:T(8,128)(2,1)S(1)}, bf16[56,3072]{1,0:T(8,128)(2,1)S(1)}, u32[]{:S(2)}, u32[]{:S(2)}) collective-permute-start(bf16[56,3072]{1,0:T(8,128)(2,1)S(1)} %get-tuple-element.179), channel_id=1, source_target_pairs={{0,2},{2,0},{4,6},{6,4},{1,3},{3,1},{5,7},{7,5},{8,10},{10,8},{12,... | collective-permute-start | bytes 1032200 | tf_op jit(solution)/shard_map/ppermute | solution.py:134
  85.2 13.1 %collective-permute-start.21 = (bf16[56,3072]{1,0:T(8,128)(2,1)S(1)}, bf16[56,3072]{1,0:T(8,128)(2,1)S(1)}, u32[]{:S(2)}, u32[]{:S(2)}) collective-permute-start(bf16[56,3072]{1,0:T(8,128)(2,1)S(1)} %get-tuple-element.177), channel_id=1, source_target_pairs={{2,4},{4,2},{3,5},{5,3},{10,12},{12,10},{11,13},{13,11},{18,20},{2... | collective-permute-start | bytes 1032200 | tf_op jit(solution)/shard_map/ppermute | solution.py:134
  85.9 13.8 %collective-permute-start.22 = (bf16[56,3072]{1,0:T(8,128)(2,1)S(1)}, bf16[56,3072]{1,0:T(8,128)(2,1)S(1)}, u32[]{:S(2)}, u32[]{:S(2)}) collective-permute-start(bf16[56,3072]{1,0:T(8,128)(2,1)S(1)} %get-tuple-element.176), channel_id=1, source_target_pairs={{0,2},{2,0},{4,6},{6,4},{1,3},{3,1},{5,7},{7,5},{8,10},{10,8},{12,... | collective-permute-start | bytes 1032200 | tf_op jit(solution)/shard_map/ppermute | solution.py:134
  93.2 14.1 %collective-permute-start.20 = (bf16[56,3072]{1,0:T(8,128)(2,1)S(1)}, bf16[56,3072]{1,0:T(8,128)(2,1)S(1)}, u32[]{:S(2)}, u32[]{:S(2)}) collective-permute-start(bf16[56,3072]{1,0:T(8,128)(2,1)S(1)} %get-tuple-element.175), channel_id=1, source_target_pairs={{0,2},{2,0},{4,6},{6,4},{1,3},{3,1},{5,7},{7,5},{8,10},{10,8},{12,... | collective-permute-start | bytes 1032200 | tf_op jit(solution)/shard_map/ppermute | solution.py:134
  99.9 16.7 %collective-permute-start.27 = (bf16[56,3072]{1,0:T(8,128)(2,1)S(1)}, bf16[56,3072]{1,0:T(8,128)(2,1)S(1)}, u32[]{:S(2)}, u32[]{:S(2)}) collective-permute-start(bf16[56,3072]{1,0:T(8,128)(2,1)S(1)} %get-tuple-element.173), channel_id=1, source_target_pairs={{0,2},{2,0},{4,6},{6,4},{1,3},{3,1},{5,7},{7,5},{8,10},{10,8},{12,... | collective-permute-start | bytes 1032200 | tf_op jit(solution)/shard_map/ppermute | solution.py:134
  102.4 14.2 %collective-permute-start.25 = (bf16[56,3072]{1,0:T(8,128)(2,1)S(1)}, bf16[56,3072]{1,0:T(8,128)(2,1)S(1)}, u32[]{:S(2)}, u32[]{:S(2)}) collective-permute-start(bf16[56,3072]{1,0:T(8,128)(2,1)S(1)} %get-tuple-element.172), channel_id=1, source_target_pairs={{2,4},{4,2},{3,5},{5,3},{10,12},{12,10},{11,13},{13,11},{18,20},{2... | collective-permute-start | bytes 1032200 | tf_op jit(solution)/shard_map/ppermute | solution.py:134
  110.7 12.6 %collective-permute-start.23 = (bf16[56,3072]{1,0:T(8,128)(2,1)S(1)}, bf16[56,3072]{1,0:T(8,128)(2,1)S(1)}, u32[]{:S(2)}, u32[]{:S(2)}) collective-permute-start(bf16[56,3072]{1,0:T(8,128)(2,1)S(1)} %get-tuple-element.169), channel_id=1, source_target_pairs={{0,2},{2,0},{4,6},{6,4},{1,3},{3,1},{5,7},{7,5},{8,10},{10,8},{12,... | collective-permute-start | bytes 1032200 | tf_op jit(solution)/shard_map/ppermute | solution.py:134
  116.9 12.3 %collective-permute-start.26 = (bf16[56,3072]{1,0:T(8,128)(2,1)S(1)}, bf16[56,3072]{1,0:T(8,128)(2,1)S(1)}, u32[]{:S(2)}, u32[]{:S(2)}) collective-permute-start(bf16[56,3072]{1,0:T(8,128)(2,1)S(1)} %get-tuple-element.166), channel_id=1, source_target_pairs={{0,2},{2,0},{4,6},{6,4},{1,3},{3,1},{5,7},{7,5},{8,10},{10,8},{12,... | collective-permute-start | bytes 1032200 | tf_op jit(solution)/shard_map/ppermute | solution.py:134
  123.6 13.0 %collective-permute-start.29 = (bf16[56,3072]{1,0:T(8,128)(2,1)S(1)}, bf16[56,3072]{1,0:T(8,128)(2,1)S(1)}, u32[]{:S(2)}, u32[]{:S(2)}) collective-permute-start(bf16[56,3072]{1,0:T(8,128)(2,1)S(1)} %maximum_convert_fusion.1), channel_id=1, source_target_pairs={{0,2},{2,0},{4,6},{6,4},{1,3},{3,1},{5,7},{7,5},{8,10},{10,8},{12,... | collective-permute-start | bytes 1032200 | tf_op jit(solution)/shard_map/ppermute | solution.py:134
  129.3 13.6 %collective-permute-start.33 = (bf16[56,3072]{1,0:T(8,128)(2,1)S(1)}, bf16[56,3072]{1,0:T(8,128)(2,1)S(1)}, u32[]{:S(2)}, u32[]{:S(2)}) collective-permute-start(bf16[56,3072]{1,0:T(8,128)(2,1)S(1)} %maximum_convert_fusion), channel_id=1, source_target_pairs={{0,2},{2,0},{4,6},{6,4},{1,3},{3,1},{5,7},{7,5},{8,10},{10,8},{12,... | collective-permute-start | bytes 1032200 | tf_op jit(solution)/shard_map/ppermute | solution.py:134
  132.7 13.7 %collective-permute-start.31 = (bf16[56,3072]{1,0:T(8,128)(2,1)S(1)}, bf16[56,3072]{1,0:T(8,128)(2,1)S(1)}, u32[]{:S(2)}, u32[]{:S(2)}) collective-permute-start(bf16[56,3072]{1,0:T(8,128)(2,1)S(1)} %maximum_convert_fusion), channel_id=1, source_target_pairs={{2,4},{4,2},{3,5},{5,3},{10,12},{12,10},{11,13},{13,11},{18,20},{2... | collective-permute-start | bytes 1032200 | tf_op jit(solution)/shard_map/ppermute | solution.py:134
  145.0 15.5 %collective-permute-start.40 = (bf16[56,3072]{1,0:T(8,128)(2,1)S(1)}, bf16[56,3072]{1,0:T(8,128)(2,1)S(1)}, u32[]{:S(2)}, u32[]{:S(2)}) collective-permute-start(bf16[56,3072]{1,0:T(8,128)(2,1)S(1)} %collective-permute-done.32), channel_id=1, source_target_pairs={{2,0},{4,6},{3,1},{5,7},{10,8},{12,14},{11,9},{13,15},{18,16},{20,... | collective-permute-start | bytes 1032200 | tf_op jit(solution)/shard_map/ppermute | solution.py:134
  146.3 34.0 %collective-permute-start.42 = (bf16[56,3072]{1,0:T(8,128)(2,1)S(1)}, bf16[56,3072]{1,0:T(8,128)(2,1)S(1)}, u32[]{:S(2)}, u32[]{:S(2)}) collective-permute-start(bf16[56,3072]{1,0:T(8,128)(2,1)S(1)} %collective-permute-done.31), channel_id=1, source_target_pairs={{2,0},{4,6},{3,1},{5,7},{10,8},{12,14},{11,9},{13,15},{18,16},{20,... | collective-permute-start | bytes 1032200 | tf_op jit(solution)/shard_map/ppermute | solution.py:134
  147.7 27.6 %collective-permute-start.41 = (bf16[56,3072]{1,0:T(8,128)(2,1)S(1)}, bf16[56,3072]{1,0:T(8,128)(2,1)S(1)}, u32[]{:S(2)}, u32[]{:S(2)}) collective-permute-start(bf16[56,3072]{1,0:T(8,128)(2,1)S(1)} %collective-permute-done.30), channel_id=1, source_target_pairs={{2,0},{4,6},{3,1},{5,7},{10,8},{12,14},{11,9},{13,15},{18,16},{20,... | collective-permute-start | bytes 1032200 | tf_op jit(solution)/shard_map/ppermute | solution.py:134
  149.0 33.6 %collective-permute-start.43 = (bf16[56,3072]{1,0:T(8,128)(2,1)S(1)}, bf16[56,3072]{1,0:T(8,128)(2,1)S(1)}, u32[]{:S(2)}, u32[]{:S(2)}) collective-permute-start(bf16[56,3072]{1,0:T(8,128)(2,1)S(1)} %collective-permute-done.34), channel_id=1, source_target_pairs={{2,0},{4,6},{3,1},{5,7},{10,8},{12,14},{11,9},{13,15},{18,16},{20,... | collective-permute-start | bytes 1032200 | tf_op jit(solution)/shard_map/ppermute | solution.py:134
  152.6 38.0 %collective-permute-start.35 = (bf16[1,2,56,576]{3,2,1,0:T(8,128)(2,1)S(1)}, bf16[1,2,56,576]{3,2,1,0:T(8,128)(2,1)S(1)}, u32[]{:S(2)}, u32[]{:S(2)}) collective-permute-start(bf16[1,2,56,576]{3,2,1,0:T(8,128)(2,1)S(1)} %pad_maximum_fusion.12), channel_id=1, source_target_pairs={{0,1},{1,0},{2,3},{3,2},{4,5},{5,4},{6,7},{7,6},{8,9},{9,8},{10,11... | collective-permute-start | bytes 387080 | tf_op jit(solution)/shard_map/ppermute | solution.py:199
  160.5 30.1 %collective-permute-start.37 = (bf16[2,56,576]{2,1,0:T(8,128)(2,1)S(1)}, bf16[2,56,576]{2,1,0:T(8,128)(2,1)S(1)}, u32[]{:S(2)}, u32[]{:S(2)}) collective-permute-start(bf16[2,56,576]{2,1,0:T(8,128)(2,1)S(1)} %get-tuple-element.197), channel_id=1, source_target_pairs={{0,8},{16,24},{1,9},{17,25},{2,10},{18,26},{3,11},{19,27},{4,12},{... | collective-permute-start | bytes 387080 | tf_op jit(solution)/shard_map/ppermute | solution.py:212
  175.3 15.4 %collective-permute-start.38 = (bf16[2,56,576]{2,1,0:T(8,128)(2,1)S(1)}, bf16[2,56,576]{2,1,0:T(8,128)(2,1)S(1)}, u32[]{:S(2)}, u32[]{:S(2)}) collective-permute-start(bf16[2,56,576]{2,1,0:T(8,128)(2,1)S(1)} %get-tuple-element.196), channel_id=1, source_target_pairs={{0,16},{8,24},{1,17},{9,25},{2,18},{10,26},{3,19},{11,27},{4,20},{... | collective-permute-start | bytes 387080 | tf_op jit(solution)/shard_map/ppermute | solution.py:212
  (26 other events, 629.7 us)

commit v2 on v1

--- a/solution.py
+++ b/solution.py
@@ -63,6 +63,7 @@
     last = []
     totals = {}
     residuals = {}
+    arrived = {}
 
     def after(values, others):
         others = [x for x in jax.tree.leaves(others) if x is not None]
@@ -211,13 +212,17 @@
             pairs = [(i, i ^ k if paired else i + k) for i in range(segments)]
             got = lax.ppermute(given[-1], "segment", [(i, j) for i, j in pairs if i < j < segments])
             received.append(got)
+        arrived[group] = total, received
+        return given
+
+    def finish(group):
+        total, received = arrived[group]
         own = jnp.where(
             segment == 0,
             totals[group, 0][0],
             lax.dynamic_index_in_dim(total, jnp.maximum(segment, 1) - 1, axis=0, keepdims=False),
         )
         residuals[group] = sum([got.astype(F32) for got in received], own)
-        return given
 
     streams = [Stream(units[i::STREAMS]) for i in range(STREAMS)]
     going = [True] * STREAMS
@@ -232,13 +237,16 @@
         sent = share_cores(group, sent)
         share_cores(group, sent, 0)
         sent = share_segments(group, sent)
-    for layer in reversed(range(layers)):
+        finish(group)
+    for layer in reversed(range(1, layers)):
         for piece in last:
-            sent = piece(layer, every)([sent, residuals.get(GROUPS - 2)] if layer == 0 else sent)
-        if layer == 1:
-            sent = share_cores(GROUPS - 1, sent)
+            sent = piece(layer, every)(sent)
+    sent = share_cores(GROUPS - 1, sent)
+    sent = share_segments(GROUPS - 1, sent)
+    for piece in last:
+        sent = piece(0, every)([sent, residuals.get(GROUPS - 2)])
     share_cores(GROUPS - 1, sent, 0)
-    share_segments(GROUPS - 1, sent)
+    finish(GROUPS - 1)
     own = jnp.stack([residuals[group] for group in range(GROUPS)], axis=1)
     residual = targets[0].astype(F32) - own.reshape(targets.shape[1:])
     features = jnp.concatenate(

time: 208 us -> 230 us (1.11)
  waiting for transfers between devices: 74.7 us -> 96 us
    ppermute x36, waiting for transfers between devices: 64.2 us -> 85.8 us  [swap(): return lax.ppermute(value, 'feat', pairs) if pairs else None]
  transfers between devices with their start and end apart: 49 -> 49, of which waited for: 20 -> 21; matrix products, arithmetic and copies ran while one was open for 16% -> 11% of each run, Pallas kernels for 0% -> 0%
where the time goes in v2:
time: 230 us; the launch traced here: 229 us
  waiting for transfers between devices  96 us (42%)
  starting transfers between devices  86.9 us (38%)
  matrix products  30.3 us (13%)
  other arithmetic  7.1 us (3%)
  blocking collectives  4.68 us (2%)
    ppermute x36, waiting for transfers between devices, swap(): return lax.ppermute(value, 'feat', pairs) if pairs else None  85.8 us
    ppermute x36, starting transfers between devices, swap(): return lax.ppermute(value, 'feat', pairs) if pairs else None  65.1 us
    dot_general x16, matrix products, run(): lax.dot_general(after(codes[key], sent), decoders[layer, :, chunk * width...  23.2 us
    ppermute x6, starting transfers between devices, share_segments(): lax.ppermute(given[-1], 'segment', [(i, j) for i, j in pairs if i < j < s...  15.4 us
    dot_general x4, matrix products, partial_sums(): jnp.dot(after(columns[group], sent), weight[:, chunk * width:(chunk + 1)...  7.15 us
    ppermute x3, starting transfers between devices, exchanged(): part = lax.ppermute(part, 'feat', pairs)  5.6 us
    ppermute x3, waiting for transfers between devices, exchanged(): part = lax.ppermute(part, 'feat', pairs)  5.5 us
  transfers between devices with their start and end apart: 49, of which 21 were waited for; matrix products, arithmetic and copies ran while one was open for 11% of the time, Pallas kernels for 0%

profile of v2, /device:TPU:0, one launch (start us, length us, event | category | flops | bytes accessed | tf_op | source)
XLA Modules:
  0.0 228.9 jit_solution(17619210170523783653)
XLA Ops:
  0.7 2.5 %all-gather = bf16[1,112,2304]{2,1,0:T(8,128)(2,1)S(1)} all-gather(bf16[1,112,1152]{2,1,0:T(8,128)(2,1)} %param.5), channel_id=2, replica_groups=mesh['segment'=4,'feat'=4,'tok'=2] {'tok'}, dimensions={2}, use_global_device_ids=true | all-gather | bytes 774144 | tf_op jit(solution)/shard_map/all_gather | solution.py:27
  3.3 3.0 %collective-permute-start = (bf16[56,576]{1,0:T(8,128)(2,1)S(1)}, bf16[56,576]{1,0:T(8,128)(2,1)S(1)}, u32[]{:S(2)}, u32[]{:S(2)}) collective-permute-start(bf16[56,576]{1,0:T(8,128)(2,1)S(1)} %get-tuple-element.214), channel_id=1, source_target_pairs={{0,2},{2,0},{4,6},{6,4},{1,3},{3,1},{5,7},{7,5},{8,10},{10,8},{12,... | collective-permute-start | bytes 193544 | tf_op jit(solution)/shard_map/ppermute | solution.py:40
  6.3 2.6 %collective-permute-start.1 = (bf16[56,576]{1,0:T(8,128)(2,1)S(1)}, bf16[56,576]{1,0:T(8,128)(2,1)S(1)}, u32[]{:S(2)}, u32[]{:S(2)}) collective-permute-start(bf16[56,576]{1,0:T(8,128)(2,1)S(1)} %get-tuple-element.213), channel_id=1, source_target_pairs={{0,4},{2,6},{4,0},{6,2},{1,5},{3,7},{5,1},{7,3},{8,12},{10,14},{12... | collective-permute-start | bytes 193544 | tf_op jit(solution)/shard_map/ppermute | solution.py:40
  9.7 4.6 %collective-permute-done.1 = bf16[56,576]{1,0:T(8,128)(2,1)S(1)} collective-permute-done((bf16[56,576]{1,0:T(8,128)(2,1)S(1)}, bf16[56,576]{1,0:T(8,128)(2,1)S(1)}, u32[]{:S(2)}, u32[]{:S(2)}) %collective-permute-start.1) | collective-permute-done | bytes 64544 | tf_op jit(solution)/shard_map/ppermute | solution.py:40
  17.6 3.4 %convolution_convert_fusion.3 = bf16[224,3072]{1,0:T(8,128)(2,1)S(1)} fusion(bf16[576,6144]{1,0:T(8,128)(2,1)} %bitcast.175, bf16[56,576]{1,0:T(8,128)(2,1)S(1)} %get-tuple-element.205, bf16[56,576]{1,0:T(8,128)(2,1)S(1)} %get-tuple-element.206, bf16[56,576]{1,0:T(8,128)(2,1)S(1)} %get-tuple-element.207, bf16[56,576]{1,0:T(8,128)(2,1)S(1)} %get-tuple-element.208), kind=kOutput, calls=%fused_computation.3 | convolution fusion | flops 794443776 | bytes 5173248 | tf_op jit(solution)/shard_map/dot_general | solution.py:53
  21.1 3.6 %collective-permute-start.3 = (bf16[56,3072]{1,0:T(8,128)(2,1)S(1)}, bf16[56,3072]{1,0:T(8,128)(2,1)S(1)}, u32[]{:S(2)}, u32[]{:S(2)}) collective-permute-start(bf16[56,3072]{1,0:T(8,128)(2,1)S(1)} %get-tuple-element.183), channel_id=1, source_target_pairs={{0,2},{6,4},{1,3},{7,5},{8,10},{14,12},{9,11},{15,13},{16,18},{22,... | collective-permute-start | bytes 1032200 | tf_op jit(solution)/shard_map/ppermute | solution.py:135
  33.9 6.5 %collective-permute-done.5 = bf16[56,3072]{1,0:T(8,128)(2,1)S(1)} collective-permute-done((bf16[56,3072]{1,0:T(8,128)(2,1)S(1)}, bf16[56,3072]{1,0:T(8,128)(2,1)S(1)}, u32[]{:S(2)}, u32[]{:S(2)}) %collective-permute-start.5) | collective-permute-done | bytes 344096 | tf_op jit(solution)/shard_map/ppermute | solution.py:135
  41.3 6.5 %collective-permute-done.7 = bf16[56,3072]{1,0:T(8,128)(2,1)S(1)} collective-permute-done((bf16[56,3072]{1,0:T(8,128)(2,1)S(1)}, bf16[56,3072]{1,0:T(8,128)(2,1)S(1)}, u32[]{:S(2)}, u32[]{:S(2)}) %collective-permute-start.7) | collective-permute-done | bytes 344096 | tf_op jit(solution)/shard_map/ppermute | solution.py:135
  48.1 2.5 %collective-permute-start.6 = (bf16[56,3072]{1,0:T(8,128)(2,1)S(1)}, bf16[56,3072]{1,0:T(8,128)(2,1)S(1)}, u32[]{:S(2)}, u32[]{:S(2)}) collective-permute-start(bf16[56,3072]{1,0:T(8,128)(2,1)S(1)} %get-tuple-element.181), channel_id=1, source_target_pairs={{0,2},{2,0},{4,6},{6,4},{1,3},{3,1},{5,7},{7,5},{8,10},{10,8},{12,... | collective-permute-start | bytes 1032200 | tf_op jit(solution)/shard_map/ppermute | solution.py:135
  51.3 3.9 %collective-permute-done.11 = bf16[56,3072]{1,0:T(8,128)(2,1)S(1)} collective-permute-done((bf16[56,3072]{1,0:T(8,128)(2,1)S(1)}, bf16[56,3072]{1,0:T(8,128)(2,1)S(1)}, u32[]{:S(2)}, u32[]{:S(2)}) %collective-permute-start.11) | collective-permute-done | bytes 344096 | tf_op jit(solution)/shard_map/ppermute | solution.py:135
  55.5 2.5 %collective-permute-start.10 = (bf16[56,3072]{1,0:T(8,128)(2,1)S(1)}, bf16[56,3072]{1,0:T(8,128)(2,1)S(1)}, u32[]{:S(2)}, u32[]{:S(2)}) collective-permute-start(bf16[56,3072]{1,0:T(8,128)(2,1)S(1)} %get-tuple-element.178), channel_id=1, source_target_pairs={{0,2},{2,0},{4,6},{6,4},{1,3},{3,1},{5,7},{7,5},{8,10},{10,8},{12,... | collective-permute-start | bytes 1032200 | tf_op jit(solution)/shard_map/ppermute | solution.py:135
  58.7 3.9 %collective-permute-done.6 = bf16[56,3072]{1,0:T(8,128)(2,1)S(1)} collective-permute-done((bf16[56,3072]{1,0:T(8,128)(2,1)S(1)}, bf16[56,3072]{1,0:T(8,128)(2,1)S(1)}, u32[]{:S(2)}, u32[]{:S(2)}) %collective-permute-start.6) | collective-permute-done | bytes 344096 | tf_op jit(solution)/shard_map/ppermute | solution.py:135
  63.6 5.4 %collective-permute-start.16 = (bf16[56,3072]{1,0:T(8,128)(2,1)S(1)}, bf16[56,3072]{1,0:T(8,128)(2,1)S(1)}, u32[]{:S(2)}, u32[]{:S(2)}) collective-permute-start(bf16[56,3072]{1,0:T(8,128)(2,1)S(1)} %maximum_convert_fusion.3), channel_id=1, source_target_pairs={{0,2},{2,0},{4,6},{6,4},{1,3},{3,1},{5,7},{7,5},{8,10},{10,8},{12,... | collective-permute-start | bytes 1032200 | tf_op jit(solution)/shard_map/ppermute | solution.py:135
  70.2 2.5 %collective-permute-start.17 = (bf16[56,3072]{1,0:T(8,128)(2,1)S(1)}, bf16[56,3072]{1,0:T(8,128)(2,1)S(1)}, u32[]{:S(2)}, u32[]{:S(2)}) collective-permute-start(bf16[56,3072]{1,0:T(8,128)(2,1)S(1)} %maximum_convert_fusion.2), channel_id=1, source_target_pairs={{0,2},{2,0},{4,6},{6,4},{1,3},{3,1},{5,7},{7,5},{8,10},{10,8},{12,... | collective-permute-start | bytes 1032200 | tf_op jit(solution)/shard_map/ppermute | solution.py:135
  73.4 4.6 %collective-permute-done.16 = bf16[56,3072]{1,0:T(8,128)(2,1)S(1)} collective-permute-done((bf16[56,3072]{1,0:T(8,128)(2,1)S(1)}, bf16[56,3072]{1,0:T(8,128)(2,1)S(1)}, u32[]{:S(2)}, u32[]{:S(2)}) %collective-permute-start.16) | collective-permute-done | bytes 344096 | tf_op jit(solution)/shard_map/ppermute | solution.py:135
  78.9 4.6 %collective-permute-start.14 = (bf16[56,3072]{1,0:T(8,128)(2,1)S(1)}, bf16[56,3072]{1,0:T(8,128)(2,1)S(1)}, u32[]{:S(2)}, u32[]{:S(2)}) collective-permute-start(bf16[56,3072]{1,0:T(8,128)(2,1)S(1)} %get-tuple-element.177), channel_id=1, source_target_pairs={{0,2},{2,0},{4,6},{6,4},{1,3},{3,1},{5,7},{7,5},{8,10},{10,8},{12,... | collective-permute-start | bytes 1032200 | tf_op jit(solution)/shard_map/ppermute | solution.py:135
  85.9 5.1 %collective-permute-start.22 = (bf16[56,3072]{1,0:T(8,128)(2,1)S(1)}, bf16[56,3072]{1,0:T(8,128)(2,1)S(1)}, u32[]{:S(2)}, u32[]{:S(2)}) collective-permute-start(bf16[56,3072]{1,0:T(8,128)(2,1)S(1)} %get-tuple-element.174), channel_id=1, source_target_pairs={{0,2},{2,0},{4,6},{6,4},{1,3},{3,1},{5,7},{7,5},{8,10},{10,8},{12,... | collective-permute-start | bytes 1032200 | tf_op jit(solution)/shard_map/ppermute | solution.py:135
  93.2 5.1 %collective-permute-start.20 = (bf16[56,3072]{1,0:T(8,128)(2,1)S(1)}, bf16[56,3072]{1,0:T(8,128)(2,1)S(1)}, u32[]{:S(2)}, u32[]{:S(2)}) collective-permute-start(bf16[56,3072]{1,0:T(8,128)(2,1)S(1)} %get-tuple-element.173), channel_id=1, source_target_pairs={{0,2},{2,0},{4,6},{6,4},{1,3},{3,1},{5,7},{7,5},{8,10},{10,8},{12,... | collective-permute-start | bytes 1032200 | tf_op jit(solution)/shard_map/ppermute | solution.py:135
  99.9 2.5 %collective-permute-start.27 = (bf16[56,3072]{1,0:T(8,128)(2,1)S(1)}, bf16[56,3072]{1,0:T(8,128)(2,1)S(1)}, u32[]{:S(2)}, u32[]{:S(2)}) collective-permute-start(bf16[56,3072]{1,0:T(8,128)(2,1)S(1)} %get-tuple-element.171), channel_id=1, source_target_pairs={{0,2},{2,0},{4,6},{6,4},{1,3},{3,1},{5,7},{7,5},{8,10},{10,8},{12,... | collective-permute-start | bytes 1032200 | tf_op jit(solution)/shard_map/ppermute | solution.py:135
  103.3 4.0 %collective-permute-done.20 = bf16[56,3072]{1,0:T(8,128)(2,1)S(1)} collective-permute-done((bf16[56,3072]{1,0:T(8,128)(2,1)S(1)}, bf16[56,3072]{1,0:T(8,128)(2,1)S(1)}, u32[]{:S(2)}, u32[]{:S(2)}) %collective-permute-start.20) | collective-permute-done | bytes 344096 | tf_op jit(solution)/shard_map/ppermute | solution.py:135
  116.9 2.6 %collective-permute-start.26 = (bf16[56,3072]{1,0:T(8,128)(2,1)S(1)}, bf16[56,3072]{1,0:T(8,128)(2,1)S(1)}, u32[]{:S(2)}, u32[]{:S(2)}) collective-permute-start(bf16[56,3072]{1,0:T(8,128)(2,1)S(1)} %get-tuple-element.164), channel_id=1, source_target_pairs={{0,2},{2,0},{4,6},{6,4},{1,3},{3,1},{5,7},{7,5},{8,10},{10,8},{12,... | collective-permute-start | bytes 1032200 | tf_op jit(solution)/shard_map/ppermute | solution.py:135
  122.2 2.3 %collective-permute-start.29 = (bf16[56,3072]{1,0:T(8,128)(2,1)S(1)}, bf16[56,3072]{1,0:T(8,128)(2,1)S(1)}, u32[]{:S(2)}, u32[]{:S(2)}) collective-permute-start(bf16[56,3072]{1,0:T(8,128)(2,1)S(1)} %maximum_convert_fusion.1), channel_id=1, source_target_pairs={{0,2},{2,0},{4,6},{6,4},{1,3},{3,1},{5,7},{7,5},{8,10},{10,8},{12,... | collective-permute-start | bytes 1032200 | tf_op jit(solution)/shard_map/ppermute | solution.py:135
  125.2 4.0 %collective-permute-done.26 = bf16[56,3072]{1,0:T(8,128)(2,1)S(1)} collective-permute-done((bf16[56,3072]{1,0:T(8,128)(2,1)S(1)}, bf16[56,3072]{1,0:T(8,128)(2,1)S(1)}, u32[]{:S(2)}, u32[]{:S(2)}) %collective-permute-start.26) | collective-permute-done | bytes 344096 | tf_op jit(solution)/shard_map/ppermute | solution.py:135
  129.3 3.4 %collective-permute-start.33 = (bf16[56,3072]{1,0:T(8,128)(2,1)S(1)}, bf16[56,3072]{1,0:T(8,128)(2,1)S(1)}, u32[]{:S(2)}, u32[]{:S(2)}) collective-permute-start(bf16[56,3072]{1,0:T(8,128)(2,1)S(1)} %maximum_convert_fusion), channel_id=1, source_target_pairs={{0,2},{2,0},{4,6},{6,4},{1,3},{3,1},{5,7},{7,5},{8,10},{10,8},{12,... | collective-permute-start | bytes 1032200 | tf_op jit(solution)/shard_map/ppermute | solution.py:135
  137.2 5.7 %collective-permute-done.33 = bf16[56,3072]{1,0:T(8,128)(2,1)S(1)} collective-permute-done((bf16[56,3072]{1,0:T(8,128)(2,1)S(1)}, bf16[56,3072]{1,0:T(8,128)(2,1)S(1)}, u32[]{:S(2)}, u32[]{:S(2)}) %collective-permute-start.33) | collective-permute-done | bytes 344096 | tf_op jit(solution)/shard_map/ppermute | solution.py:135
  152.7 19.2 %collective-permute-done.40 = bf16[56,3072]{1,0:T(8,128)(2,1)S(1)} collective-permute-done((bf16[56,3072]{1,0:T(8,128)(2,1)S(1)}, bf16[56,3072]{1,0:T(8,128)(2,1)S(1)}, u32[]{:S(2)}, u32[]{:S(2)}) %collective-permute-start.40) | collective-permute-done | bytes 344096 | tf_op jit(solution)/shard_map/ppermute | solution.py:135
  171.9 14.7 %collective-permute-done.41 = bf16[56,3072]{1,0:T(8,128)(2,1)S(1)} collective-permute-done((bf16[56,3072]{1,0:T(8,128)(2,1)S(1)}, bf16[56,3072]{1,0:T(8,128)(2,1)S(1)}, u32[]{:S(2)}, u32[]{:S(2)}) %collective-permute-start.41) | collective-permute-done | bytes 344096 | tf_op jit(solution)/shard_map/ppermute | solution.py:135
  188.4 5.5 %collective-permute-done.43 = bf16[56,3072]{1,0:T(8,128)(2,1)S(1)} collective-permute-done((bf16[56,3072]{1,0:T(8,128)(2,1)S(1)}, bf16[56,3072]{1,0:T(8,128)(2,1)S(1)}, u32[]{:S(2)}, u32[]{:S(2)}) %collective-permute-start.43) | collective-permute-done | bytes 344096 | tf_op jit(solution)/shard_map/ppermute | solution.py:135
  202.3 3.4 %collective-permute-start.37 = (bf16[2,56,576]{2,1,0:T(8,128)(2,1)S(1)}, bf16[2,56,576]{2,1,0:T(8,128)(2,1)S(1)}, u32[]{:S(2)}, u32[]{:S(2)}) collective-permute-start(bf16[2,56,576]{2,1,0:T(8,128)(2,1)S(1)} %get-tuple-element.195), channel_id=1, source_target_pairs={{0,8},{16,24},{1,9},{17,25},{2,10},{18,26},{3,11},{19,27},{4,12},{... | collective-permute-start | bytes 387080 | tf_op jit(solution)/shard_map/ppermute | solution.py:213
  205.8 3.4 %collective-permute-start.38 = (bf16[2,56,576]{2,1,0:T(8,128)(2,1)S(1)}, bf16[2,56,576]{2,1,0:T(8,128)(2,1)S(1)}, u32[]{:S(2)}, u32[]{:S(2)}) collective-permute-start(bf16[2,56,576]{2,1,0:T(8,128)(2,1)S(1)} %get-tuple-element.194), channel_id=1, source_target_pairs={{0,16},{8,24},{1,17},{9,25},{2,18},{10,26},{3,19},{11,27},{4,20},{... | collective-permute-start | bytes 387080 | tf_op jit(solution)/shard_map/ppermute | solution.py:213
  210.6 4.5 %collective-permute-done.38 = bf16[2,56,576]{2,1,0:T(8,128)(2,1)S(1)} collective-permute-done((bf16[2,56,576]{2,1,0:T(8,128)(2,1)S(1)}, bf16[2,56,576]{2,1,0:T(8,128)(2,1)S(1)}, u32[]{:S(2)}, u32[]{:S(2)}) %collective-permute-start.38) | collective-permute-done | bytes 129056 | tf_op jit(solution)/shard_map/ppermute | solution.py:213
  217.1 4.4 %collective-permute-start.47 = (bf16[2,56,576]{2,1,0:T(8,128)(2,1)S(1)}, bf16[2,56,576]{2,1,0:T(8,128)(2,1)S(1)}, u32[]{:S(2)}, u32[]{:S(2)}) collective-permute-start(bf16[2,56,576]{2,1,0:T(8,128)(2,1)S(1)} %get-tuple-element.191), channel_id=1, source_target_pairs={{0,16},{8,24},{1,17},{9,25},{2,18},{10,26},{3,19},{11,27},{4,20},{... | collective-permute-start | bytes 387080 | tf_op jit(solution)/shard_map/ppermute | solution.py:213
  (163 shorter events, 74.5 us)
Async XLA Ops:
  21.1 12.0 %collective-permute-start.3 = (bf16[56,3072]{1,0:T(8,128)(2,1)S(1)}, bf16[56,3072]{1,0:T(8,128)(2,1)S(1)}, u32[]{:S(2)}, u32[]{:S(2)}) collective-permute-start(bf16[56,3072]{1,0:T(8,128)(2,1)S(1)} %get-tuple-element.183), channel_id=1, source_target_pairs={{0,2},{6,4},{1,3},{7,5},{8,10},{14,12},{9,11},{15,13},{16,18},{22,... | collective-permute-start | bytes 1032200 | tf_op jit(solution)/shard_map/ppermute | solution.py:135
  26.1 14.4 %collective-permute-start.5 = (bf16[56,3072]{1,0:T(8,128)(2,1)S(1)}, bf16[56,3072]{1,0:T(8,128)(2,1)S(1)}, u32[]{:S(2)}, u32[]{:S(2)}) collective-permute-start(bf16[56,3072]{1,0:T(8,128)(2,1)S(1)} %get-tuple-element.184), channel_id=1, source_target_pairs={{0,2},{6,4},{1,3},{7,5},{8,10},{14,12},{9,11},{15,13},{16,18},{22,... | collective-permute-start | bytes 1032200 | tf_op jit(solution)/shard_map/ppermute | solution.py:135
  27.4 20.5 %collective-permute-start.7 = (bf16[56,3072]{1,0:T(8,128)(2,1)S(1)}, bf16[56,3072]{1,0:T(8,128)(2,1)S(1)}, u32[]{:S(2)}, u32[]{:S(2)}) collective-permute-start(bf16[56,3072]{1,0:T(8,128)(2,1)S(1)} %get-tuple-element.182), channel_id=1, source_target_pairs={{0,2},{6,4},{1,3},{7,5},{8,10},{14,12},{9,11},{15,13},{16,18},{22,... | collective-permute-start | bytes 1032200 | tf_op jit(solution)/shard_map/ppermute | solution.py:135
  28.7 26.5 %collective-permute-start.11 = (bf16[56,3072]{1,0:T(8,128)(2,1)S(1)}, bf16[56,3072]{1,0:T(8,128)(2,1)S(1)}, u32[]{:S(2)}, u32[]{:S(2)}) collective-permute-start(bf16[56,3072]{1,0:T(8,128)(2,1)S(1)} %get-tuple-element.185), channel_id=1, source_target_pairs={{0,2},{6,4},{1,3},{7,5},{8,10},{14,12},{9,11},{15,13},{16,18},{22,... | collective-permute-start | bytes 1032200 | tf_op jit(solution)/shard_map/ppermute | solution.py:135
  33.3 14.6 %collective-permute-start.4 = (bf16[56,3072]{1,0:T(8,128)(2,1)S(1)}, bf16[56,3072]{1,0:T(8,128)(2,1)S(1)}, u32[]{:S(2)}, u32[]{:S(2)}) collective-permute-start(bf16[56,3072]{1,0:T(8,128)(2,1)S(1)} %add_convert_fusion.17), channel_id=1, source_target_pairs={{2,4},{4,2},{3,5},{5,3},{10,12},{12,10},{11,13},{13,11},{18,20},{2... | collective-permute-start | bytes 1032200 | tf_op jit(solution)/shard_map/ppermute | solution.py:135
  40.6 14.6 %collective-permute-start.9 = (bf16[56,3072]{1,0:T(8,128)(2,1)S(1)}, bf16[56,3072]{1,0:T(8,128)(2,1)S(1)}, u32[]{:S(2)}, u32[]{:S(2)}) collective-permute-start(bf16[56,3072]{1,0:T(8,128)(2,1)S(1)} %add_convert_fusion.16), channel_id=1, source_target_pairs={{2,4},{4,2},{3,5},{5,3},{10,12},{12,10},{11,13},{13,11},{18,20},{2... | collective-permute-start | bytes 1032200 | tf_op jit(solution)/shard_map/ppermute | solution.py:135
  48.1 14.5 %collective-permute-start.6 = (bf16[56,3072]{1,0:T(8,128)(2,1)S(1)}, bf16[56,3072]{1,0:T(8,128)(2,1)S(1)}, u32[]{:S(2)}, u32[]{:S(2)}) collective-permute-start(bf16[56,3072]{1,0:T(8,128)(2,1)S(1)} %get-tuple-element.181), channel_id=1, source_target_pairs={{0,2},{2,0},{4,6},{6,4},{1,3},{3,1},{5,7},{7,5},{8,10},{10,8},{12,... | collective-permute-start | bytes 1032200 | tf_op jit(solution)/shard_map/ppermute | solution.py:135
  50.7 11.9 %collective-permute-start.8 = (bf16[56,3072]{1,0:T(8,128)(2,1)S(1)}, bf16[56,3072]{1,0:T(8,128)(2,1)S(1)}, u32[]{:S(2)}, u32[]{:S(2)}) collective-permute-start(bf16[56,3072]{1,0:T(8,128)(2,1)S(1)} %get-tuple-element.180), channel_id=1, source_target_pairs={{2,4},{4,2},{3,5},{5,3},{10,12},{12,10},{11,13},{13,11},{18,20},{2... | collective-permute-start | bytes 1032200 | tf_op jit(solution)/shard_map/ppermute | solution.py:135
  55.5 14.5 %collective-permute-start.10 = (bf16[56,3072]{1,0:T(8,128)(2,1)S(1)}, bf16[56,3072]{1,0:T(8,128)(2,1)S(1)}, u32[]{:S(2)}, u32[]{:S(2)}) collective-permute-start(bf16[56,3072]{1,0:T(8,128)(2,1)S(1)} %get-tuple-element.178), channel_id=1, source_target_pairs={{0,2},{2,0},{4,6},{6,4},{1,3},{3,1},{5,7},{7,5},{8,10},{10,8},{12,... | collective-permute-start | bytes 1032200 | tf_op jit(solution)/shard_map/ppermute | solution.py:135
  58.0 11.9 %collective-permute-start.12 = (bf16[56,3072]{1,0:T(8,128)(2,1)S(1)}, bf16[56,3072]{1,0:T(8,128)(2,1)S(1)}, u32[]{:S(2)}, u32[]{:S(2)}) collective-permute-start(bf16[56,3072]{1,0:T(8,128)(2,1)S(1)} %get-tuple-element.179), channel_id=1, source_target_pairs={{2,4},{4,2},{3,5},{5,3},{10,12},{12,10},{11,13},{13,11},{18,20},{2... | collective-permute-start | bytes 1032200 | tf_op jit(solution)/shard_map/ppermute | solution.py:135
  63.6 14.4 %collective-permute-start.16 = (bf16[56,3072]{1,0:T(8,128)(2,1)S(1)}, bf16[56,3072]{1,0:T(8,128)(2,1)S(1)}, u32[]{:S(2)}, u32[]{:S(2)}) collective-permute-start(bf16[56,3072]{1,0:T(8,128)(2,1)S(1)} %maximum_convert_fusion.3), channel_id=1, source_target_pairs={{0,2},{2,0},{4,6},{6,4},{1,3},{3,1},{5,7},{7,5},{8,10},{10,8},{12,... | collective-permute-start | bytes 1032200 | tf_op jit(solution)/shard_map/ppermute | solution.py:135
  70.2 14.8 %collective-permute-start.17 = (bf16[56,3072]{1,0:T(8,128)(2,1)S(1)}, bf16[56,3072]{1,0:T(8,128)(2,1)S(1)}, u32[]{:S(2)}, u32[]{:S(2)}) collective-permute-start(bf16[56,3072]{1,0:T(8,128)(2,1)S(1)} %maximum_convert_fusion.2), channel_id=1, source_target_pairs={{0,2},{2,0},{4,6},{6,4},{1,3},{3,1},{5,7},{7,5},{8,10},{10,8},{12,... | collective-permute-start | bytes 1032200 | tf_op jit(solution)/shard_map/ppermute | solution.py:135
  72.7 12.2 %collective-permute-start.15 = (bf16[56,3072]{1,0:T(8,128)(2,1)S(1)}, bf16[56,3072]{1,0:T(8,128)(2,1)S(1)}, u32[]{:S(2)}, u32[]{:S(2)}) collective-permute-start(bf16[56,3072]{1,0:T(8,128)(2,1)S(1)} %maximum_convert_fusion.2), channel_id=1, source_target_pairs={{2,4},{4,2},{3,5},{5,3},{10,12},{12,10},{11,13},{13,11},{18,20},{2... | collective-permute-start | bytes 1032200 | tf_op jit(solution)/shard_map/ppermute | solution.py:135
  78.3 12.7 %collective-permute-start.19 = (bf16[56,3072]{1,0:T(8,128)(2,1)S(1)}, bf16[56,3072]{1,0:T(8,128)(2,1)S(1)}, u32[]{:S(2)}, u32[]{:S(2)}) collective-permute-start(bf16[56,3072]{1,0:T(8,128)(2,1)S(1)} %get-tuple-element.176), channel_id=1, source_target_pairs={{2,4},{4,2},{3,5},{5,3},{10,12},{12,10},{11,13},{13,11},{18,20},{2... | collective-permute-start | bytes 1032200 | tf_op jit(solution)/shard_map/ppermute | solution.py:135
  78.9 13.3 %collective-permute-start.14 = (bf16[56,3072]{1,0:T(8,128)(2,1)S(1)}, bf16[56,3072]{1,0:T(8,128)(2,1)S(1)}, u32[]{:S(2)}, u32[]{:S(2)}) collective-permute-start(bf16[56,3072]{1,0:T(8,128)(2,1)S(1)} %get-tuple-element.177), channel_id=1, source_target_pairs={{0,2},{2,0},{4,6},{6,4},{1,3},{3,1},{5,7},{7,5},{8,10},{10,8},{12,... | collective-permute-start | bytes 1032200 | tf_op jit(solution)/shard_map/ppermute | solution.py:135
  85.2 13.1 %collective-permute-start.21 = (bf16[56,3072]{1,0:T(8,128)(2,1)S(1)}, bf16[56,3072]{1,0:T(8,128)(2,1)S(1)}, u32[]{:S(2)}, u32[]{:S(2)}) collective-permute-start(bf16[56,3072]{1,0:T(8,128)(2,1)S(1)} %get-tuple-element.175), channel_id=1, source_target_pairs={{2,4},{4,2},{3,5},{5,3},{10,12},{12,10},{11,13},{13,11},{18,20},{2... | collective-permute-start | bytes 1032200 | tf_op jit(solution)/shard_map/ppermute | solution.py:135
  85.9 13.8 %collective-permute-start.22 = (bf16[56,3072]{1,0:T(8,128)(2,1)S(1)}, bf16[56,3072]{1,0:T(8,128)(2,1)S(1)}, u32[]{:S(2)}, u32[]{:S(2)}) collective-permute-start(bf16[56,3072]{1,0:T(8,128)(2,1)S(1)} %get-tuple-element.174), channel_id=1, source_target_pairs={{0,2},{2,0},{4,6},{6,4},{1,3},{3,1},{5,7},{7,5},{8,10},{10,8},{12,... | collective-permute-start | bytes 1032200 | tf_op jit(solution)/shard_map/ppermute | solution.py:135
  93.2 14.1 %collective-permute-start.20 = (bf16[56,3072]{1,0:T(8,128)(2,1)S(1)}, bf16[56,3072]{1,0:T(8,128)(2,1)S(1)}, u32[]{:S(2)}, u32[]{:S(2)}) collective-permute-start(bf16[56,3072]{1,0:T(8,128)(2,1)S(1)} %get-tuple-element.173), channel_id=1, source_target_pairs={{0,2},{2,0},{4,6},{6,4},{1,3},{3,1},{5,7},{7,5},{8,10},{10,8},{12,... | collective-permute-start | bytes 1032200 | tf_op jit(solution)/shard_map/ppermute | solution.py:135
  99.9 16.7 %collective-permute-start.27 = (bf16[56,3072]{1,0:T(8,128)(2,1)S(1)}, bf16[56,3072]{1,0:T(8,128)(2,1)S(1)}, u32[]{:S(2)}, u32[]{:S(2)}) collective-permute-start(bf16[56,3072]{1,0:T(8,128)(2,1)S(1)} %get-tuple-element.171), channel_id=1, source_target_pairs={{0,2},{2,0},{4,6},{6,4},{1,3},{3,1},{5,7},{7,5},{8,10},{10,8},{12,... | collective-permute-start | bytes 1032200 | tf_op jit(solution)/shard_map/ppermute | solution.py:135
  102.4 14.2 %collective-permute-start.25 = (bf16[56,3072]{1,0:T(8,128)(2,1)S(1)}, bf16[56,3072]{1,0:T(8,128)(2,1)S(1)}, u32[]{:S(2)}, u32[]{:S(2)}) collective-permute-start(bf16[56,3072]{1,0:T(8,128)(2,1)S(1)} %get-tuple-element.170), channel_id=1, source_target_pairs={{2,4},{4,2},{3,5},{5,3},{10,12},{12,10},{11,13},{13,11},{18,20},{2... | collective-permute-start | bytes 1032200 | tf_op jit(solution)/shard_map/ppermute | solution.py:135
  110.8 11.2 %collective-permute-start.23 = (bf16[56,3072]{1,0:T(8,128)(2,1)S(1)}, bf16[56,3072]{1,0:T(8,128)(2,1)S(1)}, u32[]{:S(2)}, u32[]{:S(2)}) collective-permute-start(bf16[56,3072]{1,0:T(8,128)(2,1)S(1)} %get-tuple-element.167), channel_id=1, source_target_pairs={{0,2},{2,0},{4,6},{6,4},{1,3},{3,1},{5,7},{7,5},{8,10},{10,8},{12,... | collective-permute-start | bytes 1032200 | tf_op jit(solution)/shard_map/ppermute | solution.py:135
  116.9 12.3 %collective-permute-start.26 = (bf16[56,3072]{1,0:T(8,128)(2,1)S(1)}, bf16[56,3072]{1,0:T(8,128)(2,1)S(1)}, u32[]{:S(2)}, u32[]{:S(2)}) collective-permute-start(bf16[56,3072]{1,0:T(8,128)(2,1)S(1)} %get-tuple-element.164), channel_id=1, source_target_pairs={{0,2},{2,0},{4,6},{6,4},{1,3},{3,1},{5,7},{7,5},{8,10},{10,8},{12,... | collective-permute-start | bytes 1032200 | tf_op jit(solution)/shard_map/ppermute | solution.py:135
  122.2 14.3 %collective-permute-start.29 = (bf16[56,3072]{1,0:T(8,128)(2,1)S(1)}, bf16[56,3072]{1,0:T(8,128)(2,1)S(1)}, u32[]{:S(2)}, u32[]{:S(2)}) collective-permute-start(bf16[56,3072]{1,0:T(8,128)(2,1)S(1)} %maximum_convert_fusion.1), channel_id=1, source_target_pairs={{0,2},{2,0},{4,6},{6,4},{1,3},{3,1},{5,7},{7,5},{8,10},{10,8},{12,... | collective-permute-start | bytes 1032200 | tf_op jit(solution)/shard_map/ppermute | solution.py:135
  124.5 12.0 %collective-permute-start.32 = (bf16[56,3072]{1,0:T(8,128)(2,1)S(1)}, bf16[56,3072]{1,0:T(8,128)(2,1)S(1)}, u32[]{:S(2)}, u32[]{:S(2)}) collective-permute-start(bf16[56,3072]{1,0:T(8,128)(2,1)S(1)} %maximum_convert_fusion.1), channel_id=1, source_target_pairs={{2,4},{4,2},{3,5},{5,3},{10,12},{12,10},{11,13},{13,11},{18,20},{2... | collective-permute-start | bytes 1032200 | tf_op jit(solution)/shard_map/ppermute | solution.py:135
  129.3 13.6 %collective-permute-start.33 = (bf16[56,3072]{1,0:T(8,128)(2,1)S(1)}, bf16[56,3072]{1,0:T(8,128)(2,1)S(1)}, u32[]{:S(2)}, u32[]{:S(2)}) collective-permute-start(bf16[56,3072]{1,0:T(8,128)(2,1)S(1)} %maximum_convert_fusion), channel_id=1, source_target_pairs={{0,2},{2,0},{4,6},{6,4},{1,3},{3,1},{5,7},{7,5},{8,10},{10,8},{12,... | collective-permute-start | bytes 1032200 | tf_op jit(solution)/shard_map/ppermute | solution.py:135
  134.2 10.9 %collective-permute-start.31 = (bf16[56,3072]{1,0:T(8,128)(2,1)S(1)}, bf16[56,3072]{1,0:T(8,128)(2,1)S(1)}, u32[]{:S(2)}, u32[]{:S(2)}) collective-permute-start(bf16[56,3072]{1,0:T(8,128)(2,1)S(1)} %maximum_convert_fusion), channel_id=1, source_target_pairs={{2,4},{4,2},{3,5},{5,3},{10,12},{12,10},{11,13},{13,11},{18,20},{2... | collective-permute-start | bytes 1032200 | tf_op jit(solution)/shard_map/ppermute | solution.py:135
  146.9 25.0 %collective-permute-start.40 = (bf16[56,3072]{1,0:T(8,128)(2,1)S(1)}, bf16[56,3072]{1,0:T(8,128)(2,1)S(1)}, u32[]{:S(2)}, u32[]{:S(2)}) collective-permute-start(bf16[56,3072]{1,0:T(8,128)(2,1)S(1)} %collective-permute-done.32), channel_id=1, source_target_pairs={{2,0},{4,6},{3,1},{5,7},{10,8},{12,14},{11,9},{13,15},{18,16},{20,... | collective-permute-start | bytes 1032200 | tf_op jit(solution)/shard_map/ppermute | solution.py:135
  148.2 40.2 %collective-permute-start.42 = (bf16[56,3072]{1,0:T(8,128)(2,1)S(1)}, bf16[56,3072]{1,0:T(8,128)(2,1)S(1)}, u32[]{:S(2)}, u32[]{:S(2)}) collective-permute-start(bf16[56,3072]{1,0:T(8,128)(2,1)S(1)} %collective-permute-done.31), channel_id=1, source_target_pairs={{2,0},{4,6},{3,1},{5,7},{10,8},{12,14},{11,9},{13,15},{18,16},{20,... | collective-permute-start | bytes 1032200 | tf_op jit(solution)/shard_map/ppermute | solution.py:135
  149.7 37.0 %collective-permute-start.41 = (bf16[56,3072]{1,0:T(8,128)(2,1)S(1)}, bf16[56,3072]{1,0:T(8,128)(2,1)S(1)}, u32[]{:S(2)}, u32[]{:S(2)}) collective-permute-start(bf16[56,3072]{1,0:T(8,128)(2,1)S(1)} %collective-permute-done.30), channel_id=1, source_target_pairs={{2,0},{4,6},{3,1},{5,7},{10,8},{12,14},{11,9},{13,15},{18,16},{20,... | collective-permute-start | bytes 1032200 | tf_op jit(solution)/shard_map/ppermute | solution.py:135
  151.0 42.8 %collective-permute-start.43 = (bf16[56,3072]{1,0:T(8,128)(2,1)S(1)}, bf16[56,3072]{1,0:T(8,128)(2,1)S(1)}, u32[]{:S(2)}, u32[]{:S(2)}) collective-permute-start(bf16[56,3072]{1,0:T(8,128)(2,1)S(1)} %collective-permute-done.34), channel_id=1, source_target_pairs={{2,0},{4,6},{3,1},{5,7},{10,8},{12,14},{11,9},{13,15},{18,16},{20,... | collective-permute-start | bytes 1032200 | tf_op jit(solution)/shard_map/ppermute | solution.py:135
  201.7 13.6 %collective-permute-start.44 = (bf16[3,2,56,576]{3,2,1,0:T(8,128)(2,1)S(1)}, bf16[3,2,56,576]{3,2,1,0:T(8,128)(2,1)S(1)}, u32[]{:S(2)}, u32[]{:S(2)}) collective-permute-start(bf16[3,2,56,576]{3,2,1,0:T(8,128)(2,1)S(1)} %pad_maximum_fusion.8), channel_id=1, source_target_pairs={{0,1},{1,0},{2,3},{3,2},{4,5},{5,4},{6,7},{7,6},{8,9},{9,8},{10,11... | collective-permute-start | bytes 1161224 | tf_op jit(solution)/shard_map/ppermute | solution.py:200
  215.5 11.8 %collective-permute-start.46 = (bf16[2,56,576]{2,1,0:T(8,128)(2,1)S(1)}, bf16[2,56,576]{2,1,0:T(8,128)(2,1)S(1)}, u32[]{:S(2)}, u32[]{:S(2)}) collective-permute-start(bf16[2,56,576]{2,1,0:T(8,128)(2,1)S(1)} %get-tuple-element.192), channel_id=1, source_target_pairs={{0,8},{16,24},{1,9},{17,25},{2,10},{18,26},{3,11},{19,27},{4,12},{... | collective-permute-start | bytes 387080 | tf_op jit(solution)/shard_map/ppermute | solution.py:213
  (26 other events, 619.8 us)

commit v3 on v2

--- a/solution.py
+++ b/solution.py
@@ -240,11 +240,11 @@
         finish(group)
     for layer in reversed(range(1, layers)):
         for piece in last:
-            sent = piece(layer, every)(sent)
+            sent = piece(layer, every)([sent, residuals.get(GROUPS - 2)] if layer == 1 else sent)
     sent = share_cores(GROUPS - 1, sent)
     sent = share_segments(GROUPS - 1, sent)
     for piece in last:
-        sent = piece(0, every)([sent, residuals.get(GROUPS - 2)])
+        sent = piece(0, every)(sent)
     share_cores(GROUPS - 1, sent, 0)
     finish(GROUPS - 1)
     own = jnp.stack([residuals[group] for group in range(GROUPS)], axis=1)

time: 230 us -> 207 us (0.900)
  waiting for transfers between devices: 96 us -> 73.4 us
    ppermute x36, waiting for transfers between devices: 85.8 us -> 64.2 us  [swap(): return lax.ppermute(value, 'feat', pairs) if pairs else None]
    ppermute x6, waiting for transfers between devices: 4.56 us -> 0.37 us  [share_segments(): lax.ppermute(given[-1], 'segment', [(i, j) for i, j in pairs if i < j < s...]
    ppermute x4, waiting for transfers between devices: 0.15 us -> 3.36 us  [share_cores(): lax.ppermute(given[-1], 'tok', [(i, (i + k) % cores) for i in range(cores)])]
  transfers between devices with their start and end apart: 49 -> 49, of which waited for: 21 -> 22; matrix products, arithmetic and copies ran while one was open for 11% -> 15% of each run, Pallas kernels for 0% -> 0%
where the time goes in v3:
time: 207 us; the launch traced here: 206 us
  starting transfers between devices  86.8 us (42%)
  waiting for transfers between devices  73.4 us (35%)
  matrix products  30.3 us (15%)
  other arithmetic  6.98 us (3%)
  blocking collectives  4.68 us (2%)
    ppermute x36, starting transfers between devices, swap(): return lax.ppermute(value, 'feat', pairs) if pairs else None  64.8 us
    ppermute x36, waiting for transfers between devices, swap(): return lax.ppermute(value, 'feat', pairs) if pairs else None  64.2 us
    dot_general x16, matrix products, run(): lax.dot_general(after(codes[key], sent), decoders[layer, :, chunk * width...  23.2 us
    ppermute x6, starting transfers between devices, share_segments(): lax.ppermute(given[-1], 'segment', [(i, j) for i, j in pairs if i < j < s...  16 us
    dot_general x4, matrix products, partial_sums(): jnp.dot(after(columns[group], sent), weight[:, chunk * width:(chunk + 1)...  7.15 us
    ppermute x3, starting transfers between devices, exchanged(): part = lax.ppermute(part, 'feat', pairs)  5.6 us
    ppermute x3, waiting for transfers between devices, exchanged(): part = lax.ppermute(part, 'feat', pairs)  5.5 us
  transfers between devices with their start and end apart: 49, of which 22 were waited for; matrix products, arithmetic and copies ran while one was open for 15% of the time, Pallas kernels for 0%

profile of v3, /device:TPU:0, one launch (start us, length us, event | category | flops | bytes accessed | tf_op | source)
XLA Modules:
  0.0 205.6 jit_solution(4420711982297102773)
XLA Ops:
  0.7 2.5 %all-gather = bf16[1,112,2304]{2,1,0:T(8,128)(2,1)S(1)} all-gather(bf16[1,112,1152]{2,1,0:T(8,128)(2,1)} %param.5), channel_id=2, replica_groups=mesh['segment'=4,'feat'=4,'tok'=2] {'tok'}, dimensions={2}, use_global_device_ids=true | all-gather | bytes 774144 | tf_op jit(solution)/shard_map/all_gather | solution.py:27
  3.3 3.0 %collective-permute-start = (bf16[56,576]{1,0:T(8,128)(2,1)S(1)}, bf16[56,576]{1,0:T(8,128)(2,1)S(1)}, u32[]{:S(2)}, u32[]{:S(2)}) collective-permute-start(bf16[56,576]{1,0:T(8,128)(2,1)S(1)} %get-tuple-element.214), channel_id=1, source_target_pairs={{0,2},{2,0},{4,6},{6,4},{1,3},{3,1},{5,7},{7,5},{8,10},{10,8},{12,... | collective-permute-start | bytes 193544 | tf_op jit(solution)/shard_map/ppermute | solution.py:40
  6.3 2.6 %collective-permute-start.1 = (bf16[56,576]{1,0:T(8,128)(2,1)S(1)}, bf16[56,576]{1,0:T(8,128)(2,1)S(1)}, u32[]{:S(2)}, u32[]{:S(2)}) collective-permute-start(bf16[56,576]{1,0:T(8,128)(2,1)S(1)} %get-tuple-element.213), channel_id=1, source_target_pairs={{0,4},{2,6},{4,0},{6,2},{1,5},{3,7},{5,1},{7,3},{8,12},{10,14},{12... | collective-permute-start | bytes 193544 | tf_op jit(solution)/shard_map/ppermute | solution.py:40
  9.7 4.6 %collective-permute-done.1 = bf16[56,576]{1,0:T(8,128)(2,1)S(1)} collective-permute-done((bf16[56,576]{1,0:T(8,128)(2,1)S(1)}, bf16[56,576]{1,0:T(8,128)(2,1)S(1)}, u32[]{:S(2)}, u32[]{:S(2)}) %collective-permute-start.1) | collective-permute-done | bytes 64544 | tf_op jit(solution)/shard_map/ppermute | solution.py:40
  17.6 3.4 %convolution_convert_fusion.3 = bf16[224,3072]{1,0:T(8,128)(2,1)S(1)} fusion(bf16[576,6144]{1,0:T(8,128)(2,1)} %bitcast.175, bf16[56,576]{1,0:T(8,128)(2,1)S(1)} %get-tuple-element.205, bf16[56,576]{1,0:T(8,128)(2,1)S(1)} %get-tuple-element.206, bf16[56,576]{1,0:T(8,128)(2,1)S(1)} %get-tuple-element.207, bf16[56,576]{1,0:T(8,128)(2,1)S(1)} %get-tuple-element.208), kind=kOutput, calls=%fused_computation.3 | convolution fusion | flops 794443776 | bytes 5173248 | tf_op jit(solution)/shard_map/dot_general | solution.py:53
  21.1 3.6 %collective-permute-start.3 = (bf16[56,3072]{1,0:T(8,128)(2,1)S(1)}, bf16[56,3072]{1,0:T(8,128)(2,1)S(1)}, u32[]{:S(2)}, u32[]{:S(2)}) collective-permute-start(bf16[56,3072]{1,0:T(8,128)(2,1)S(1)} %get-tuple-element.183), channel_id=1, source_target_pairs={{0,2},{6,4},{1,3},{7,5},{8,10},{14,12},{9,11},{15,13},{16,18},{22,... | collective-permute-start | bytes 1032200 | tf_op jit(solution)/shard_map/ppermute | solution.py:135
  33.9 6.5 %collective-permute-done.5 = bf16[56,3072]{1,0:T(8,128)(2,1)S(1)} collective-permute-done((bf16[56,3072]{1,0:T(8,128)(2,1)S(1)}, bf16[56,3072]{1,0:T(8,128)(2,1)S(1)}, u32[]{:S(2)}, u32[]{:S(2)}) %collective-permute-start.5) | collective-permute-done | bytes 344096 | tf_op jit(solution)/shard_map/ppermute | solution.py:135
  41.3 6.5 %collective-permute-done.7 = bf16[56,3072]{1,0:T(8,128)(2,1)S(1)} collective-permute-done((bf16[56,3072]{1,0:T(8,128)(2,1)S(1)}, bf16[56,3072]{1,0:T(8,128)(2,1)S(1)}, u32[]{:S(2)}, u32[]{:S(2)}) %collective-permute-start.7) | collective-permute-done | bytes 344096 | tf_op jit(solution)/shard_map/ppermute | solution.py:135
  48.1 2.5 %collective-permute-start.6 = (bf16[56,3072]{1,0:T(8,128)(2,1)S(1)}, bf16[56,3072]{1,0:T(8,128)(2,1)S(1)}, u32[]{:S(2)}, u32[]{:S(2)}) collective-permute-start(bf16[56,3072]{1,0:T(8,128)(2,1)S(1)} %get-tuple-element.181), channel_id=1, source_target_pairs={{0,2},{2,0},{4,6},{6,4},{1,3},{3,1},{5,7},{7,5},{8,10},{10,8},{12,... | collective-permute-start | bytes 1032200 | tf_op jit(solution)/shard_map/ppermute | solution.py:135
  51.3 3.9 %collective-permute-done.11 = bf16[56,3072]{1,0:T(8,128)(2,1)S(1)} collective-permute-done((bf16[56,3072]{1,0:T(8,128)(2,1)S(1)}, bf16[56,3072]{1,0:T(8,128)(2,1)S(1)}, u32[]{:S(2)}, u32[]{:S(2)}) %collective-permute-start.11) | collective-permute-done | bytes 344096 | tf_op jit(solution)/shard_map/ppermute | solution.py:135
  55.5 2.5 %collective-permute-start.10 = (bf16[56,3072]{1,0:T(8,128)(2,1)S(1)}, bf16[56,3072]{1,0:T(8,128)(2,1)S(1)}, u32[]{:S(2)}, u32[]{:S(2)}) collective-permute-start(bf16[56,3072]{1,0:T(8,128)(2,1)S(1)} %get-tuple-element.178), channel_id=1, source_target_pairs={{0,2},{2,0},{4,6},{6,4},{1,3},{3,1},{5,7},{7,5},{8,10},{10,8},{12,... | collective-permute-start | bytes 1032200 | tf_op jit(solution)/shard_map/ppermute | solution.py:135
  58.7 3.9 %collective-permute-done.6 = bf16[56,3072]{1,0:T(8,128)(2,1)S(1)} collective-permute-done((bf16[56,3072]{1,0:T(8,128)(2,1)S(1)}, bf16[56,3072]{1,0:T(8,128)(2,1)S(1)}, u32[]{:S(2)}, u32[]{:S(2)}) %collective-permute-start.6) | collective-permute-done | bytes 344096 | tf_op jit(solution)/shard_map/ppermute | solution.py:135
  63.6 5.4 %collective-permute-start.16 = (bf16[56,3072]{1,0:T(8,128)(2,1)S(1)}, bf16[56,3072]{1,0:T(8,128)(2,1)S(1)}, u32[]{:S(2)}, u32[]{:S(2)}) collective-permute-start(bf16[56,3072]{1,0:T(8,128)(2,1)S(1)} %maximum_convert_fusion.3), channel_id=1, source_target_pairs={{0,2},{2,0},{4,6},{6,4},{1,3},{3,1},{5,7},{7,5},{8,10},{10,8},{12,... | collective-permute-start | bytes 1032200 | tf_op jit(solution)/shard_map/ppermute | solution.py:135
  70.2 2.5 %collective-permute-start.17 = (bf16[56,3072]{1,0:T(8,128)(2,1)S(1)}, bf16[56,3072]{1,0:T(8,128)(2,1)S(1)}, u32[]{:S(2)}, u32[]{:S(2)}) collective-permute-start(bf16[56,3072]{1,0:T(8,128)(2,1)S(1)} %maximum_convert_fusion.2), channel_id=1, source_target_pairs={{0,2},{2,0},{4,6},{6,4},{1,3},{3,1},{5,7},{7,5},{8,10},{10,8},{12,... | collective-permute-start | bytes 1032200 | tf_op jit(solution)/shard_map/ppermute | solution.py:135
  73.4 4.6 %collective-permute-done.16 = bf16[56,3072]{1,0:T(8,128)(2,1)S(1)} collective-permute-done((bf16[56,3072]{1,0:T(8,128)(2,1)S(1)}, bf16[56,3072]{1,0:T(8,128)(2,1)S(1)}, u32[]{:S(2)}, u32[]{:S(2)}) %collective-permute-start.16) | collective-permute-done | bytes 344096 | tf_op jit(solution)/shard_map/ppermute | solution.py:135
  78.9 4.6 %collective-permute-start.14 = (bf16[56,3072]{1,0:T(8,128)(2,1)S(1)}, bf16[56,3072]{1,0:T(8,128)(2,1)S(1)}, u32[]{:S(2)}, u32[]{:S(2)}) collective-permute-start(bf16[56,3072]{1,0:T(8,128)(2,1)S(1)} %get-tuple-element.177), channel_id=1, source_target_pairs={{0,2},{2,0},{4,6},{6,4},{1,3},{3,1},{5,7},{7,5},{8,10},{10,8},{12,... | collective-permute-start | bytes 1032200 | tf_op jit(solution)/shard_map/ppermute | solution.py:135
  85.9 5.1 %collective-permute-start.22 = (bf16[56,3072]{1,0:T(8,128)(2,1)S(1)}, bf16[56,3072]{1,0:T(8,128)(2,1)S(1)}, u32[]{:S(2)}, u32[]{:S(2)}) collective-permute-start(bf16[56,3072]{1,0:T(8,128)(2,1)S(1)} %get-tuple-element.174), channel_id=1, source_target_pairs={{0,2},{2,0},{4,6},{6,4},{1,3},{3,1},{5,7},{7,5},{8,10},{10,8},{12,... | collective-permute-start | bytes 1032200 | tf_op jit(solution)/shard_map/ppermute | solution.py:135
  93.2 5.1 %collective-permute-start.20 = (bf16[56,3072]{1,0:T(8,128)(2,1)S(1)}, bf16[56,3072]{1,0:T(8,128)(2,1)S(1)}, u32[]{:S(2)}, u32[]{:S(2)}) collective-permute-start(bf16[56,3072]{1,0:T(8,128)(2,1)S(1)} %get-tuple-element.173), channel_id=1, source_target_pairs={{0,2},{2,0},{4,6},{6,4},{1,3},{3,1},{5,7},{7,5},{8,10},{10,8},{12,... | collective-permute-start | bytes 1032200 | tf_op jit(solution)/shard_map/ppermute | solution.py:135
  99.9 2.5 %collective-permute-start.27 = (bf16[56,3072]{1,0:T(8,128)(2,1)S(1)}, bf16[56,3072]{1,0:T(8,128)(2,1)S(1)}, u32[]{:S(2)}, u32[]{:S(2)}) collective-permute-start(bf16[56,3072]{1,0:T(8,128)(2,1)S(1)} %get-tuple-element.171), channel_id=1, source_target_pairs={{0,2},{2,0},{4,6},{6,4},{1,3},{3,1},{5,7},{7,5},{8,10},{10,8},{12,... | collective-permute-start | bytes 1032200 | tf_op jit(solution)/shard_map/ppermute | solution.py:135
  103.3 4.0 %collective-permute-done.20 = bf16[56,3072]{1,0:T(8,128)(2,1)S(1)} collective-permute-done((bf16[56,3072]{1,0:T(8,128)(2,1)S(1)}, bf16[56,3072]{1,0:T(8,128)(2,1)S(1)}, u32[]{:S(2)}, u32[]{:S(2)}) %collective-permute-start.20) | collective-permute-done | bytes 344096 | tf_op jit(solution)/shard_map/ppermute | solution.py:135
  110.7 2.3 %collective-permute-start.23 = (bf16[56,3072]{1,0:T(8,128)(2,1)S(1)}, bf16[56,3072]{1,0:T(8,128)(2,1)S(1)}, u32[]{:S(2)}, u32[]{:S(2)}) collective-permute-start(bf16[56,3072]{1,0:T(8,128)(2,1)S(1)} %get-tuple-element.167), channel_id=1, source_target_pairs={{0,2},{2,0},{4,6},{6,4},{1,3},{3,1},{5,7},{7,5},{8,10},{10,8},{12,... | collective-permute-start | bytes 1032200 | tf_op jit(solution)/shard_map/ppermute | solution.py:135
  116.9 2.6 %collective-permute-start.26 = (bf16[56,3072]{1,0:T(8,128)(2,1)S(1)}, bf16[56,3072]{1,0:T(8,128)(2,1)S(1)}, u32[]{:S(2)}, u32[]{:S(2)}) collective-permute-start(bf16[56,3072]{1,0:T(8,128)(2,1)S(1)} %get-tuple-element.164), channel_id=1, source_target_pairs={{0,2},{2,0},{4,6},{6,4},{1,3},{3,1},{5,7},{7,5},{8,10},{10,8},{12,... | collective-permute-start | bytes 1032200 | tf_op jit(solution)/shard_map/ppermute | solution.py:135
  126.3 2.9 %collective-permute-done.26 = bf16[56,3072]{1,0:T(8,128)(2,1)S(1)} collective-permute-done((bf16[56,3072]{1,0:T(8,128)(2,1)S(1)}, bf16[56,3072]{1,0:T(8,128)(2,1)S(1)}, u32[]{:S(2)}, u32[]{:S(2)}) %collective-permute-start.26) | collective-permute-done | bytes 344096 | tf_op jit(solution)/shard_map/ppermute | solution.py:135
  129.3 3.3 %collective-permute-start.33 = (bf16[56,3072]{1,0:T(8,128)(2,1)S(1)}, bf16[56,3072]{1,0:T(8,128)(2,1)S(1)}, u32[]{:S(2)}, u32[]{:S(2)}) collective-permute-start(bf16[56,3072]{1,0:T(8,128)(2,1)S(1)} %maximum_convert_fusion), channel_id=1, source_target_pairs={{0,2},{2,0},{4,6},{6,4},{1,3},{3,1},{5,7},{7,5},{8,10},{10,8},{12,... | collective-permute-start | bytes 1032200 | tf_op jit(solution)/shard_map/ppermute | solution.py:135
  137.2 5.7 %collective-permute-done.33 = bf16[56,3072]{1,0:T(8,128)(2,1)S(1)} collective-permute-done((bf16[56,3072]{1,0:T(8,128)(2,1)S(1)}, bf16[56,3072]{1,0:T(8,128)(2,1)S(1)}, u32[]{:S(2)}, u32[]{:S(2)}) %collective-permute-start.33) | collective-permute-done | bytes 344096 | tf_op jit(solution)/shard_map/ppermute | solution.py:135
  152.9 7.6 %collective-permute-done.40 = bf16[56,3072]{1,0:T(8,128)(2,1)S(1)} collective-permute-done((bf16[56,3072]{1,0:T(8,128)(2,1)S(1)}, bf16[56,3072]{1,0:T(8,128)(2,1)S(1)}, u32[]{:S(2)}, u32[]{:S(2)}) %collective-permute-start.40) | collective-permute-done | bytes 344096 | tf_op jit(solution)/shard_map/ppermute | solution.py:135
  160.5 3.4 %collective-permute-start.37 = (bf16[2,56,576]{2,1,0:T(8,128)(2,1)S(1)}, bf16[2,56,576]{2,1,0:T(8,128)(2,1)S(1)}, u32[]{:S(2)}, u32[]{:S(2)}) collective-permute-start(bf16[2,56,576]{2,1,0:T(8,128)(2,1)S(1)} %get-tuple-element.195), channel_id=1, source_target_pairs={{0,8},{16,24},{1,9},{17,25},{2,10},{18,26},{3,11},{19,27},{4,12},{... | collective-permute-start | bytes 387080 | tf_op jit(solution)/shard_map/ppermute | solution.py:213
  163.9 11.3 %collective-permute-done.41 = bf16[56,3072]{1,0:T(8,128)(2,1)S(1)} collective-permute-done((bf16[56,3072]{1,0:T(8,128)(2,1)S(1)}, bf16[56,3072]{1,0:T(8,128)(2,1)S(1)}, u32[]{:S(2)}, u32[]{:S(2)}) %collective-permute-start.41) | collective-permute-done | bytes 344096 | tf_op jit(solution)/shard_map/ppermute | solution.py:135
  175.3 3.4 %collective-permute-start.38 = (bf16[2,56,576]{2,1,0:T(8,128)(2,1)S(1)}, bf16[2,56,576]{2,1,0:T(8,128)(2,1)S(1)}, u32[]{:S(2)}, u32[]{:S(2)}) collective-permute-start(bf16[2,56,576]{2,1,0:T(8,128)(2,1)S(1)} %get-tuple-element.194), channel_id=1, source_target_pairs={{0,16},{8,24},{1,17},{9,25},{2,18},{10,26},{3,19},{11,27},{4,20},{... | collective-permute-start | bytes 387080 | tf_op jit(solution)/shard_map/ppermute | solution.py:213
  180.4 2.2 %collective-permute-start.39 = (bf16[2,56,576]{2,1,0:T(8,128)(2,1)S(1)}, bf16[2,56,576]{2,1,0:T(8,128)(2,1)S(1)}, u32[]{:S(2)}, u32[]{:S(2)}) collective-permute-start(bf16[2,56,576]{2,1,0:T(8,128)(2,1)S(1)} %get-tuple-element.193), channel_id=1, source_target_pairs={{0,24},{8,16},{1,25},{9,17},{2,26},{10,18},{3,27},{11,19},{4,28},{... | collective-permute-start | bytes 387080 | tf_op jit(solution)/shard_map/ppermute | solution.py:213
  192.6 2.5 %collective-permute-start.46 = (bf16[2,56,576]{2,1,0:T(8,128)(2,1)S(1)}, bf16[2,56,576]{2,1,0:T(8,128)(2,1)S(1)}, u32[]{:S(2)}, u32[]{:S(2)}) collective-permute-start(bf16[2,56,576]{2,1,0:T(8,128)(2,1)S(1)} %get-tuple-element.192), channel_id=1, source_target_pairs={{0,8},{16,24},{1,9},{17,25},{2,10},{18,26},{3,11},{19,27},{4,12},{... | collective-permute-start | bytes 387080 | tf_op jit(solution)/shard_map/ppermute | solution.py:213
  195.1 3.2 %collective-permute-start.47 = (bf16[2,56,576]{2,1,0:T(8,128)(2,1)S(1)}, bf16[2,56,576]{2,1,0:T(8,128)(2,1)S(1)}, u32[]{:S(2)}, u32[]{:S(2)}) collective-permute-start(bf16[2,56,576]{2,1,0:T(8,128)(2,1)S(1)} %get-tuple-element.191), channel_id=1, source_target_pairs={{0,16},{8,24},{1,17},{9,25},{2,18},{10,26},{3,19},{11,27},{4,20},{... | collective-permute-start | bytes 387080 | tf_op jit(solution)/shard_map/ppermute | solution.py:213
  (163 shorter events, 74.0 us)
Async XLA Ops:
  21.1 12.0 %collective-permute-start.3 = (bf16[56,3072]{1,0:T(8,128)(2,1)S(1)}, bf16[56,3072]{1,0:T(8,128)(2,1)S(1)}, u32[]{:S(2)}, u32[]{:S(2)}) collective-permute-start(bf16[56,3072]{1,0:T(8,128)(2,1)S(1)} %get-tuple-element.183), channel_id=1, source_target_pairs={{0,2},{6,4},{1,3},{7,5},{8,10},{14,12},{9,11},{15,13},{16,18},{22,... | collective-permute-start | bytes 1032200 | tf_op jit(solution)/shard_map/ppermute | solution.py:135
  26.1 14.4 %collective-permute-start.5 = (bf16[56,3072]{1,0:T(8,128)(2,1)S(1)}, bf16[56,3072]{1,0:T(8,128)(2,1)S(1)}, u32[]{:S(2)}, u32[]{:S(2)}) collective-permute-start(bf16[56,3072]{1,0:T(8,128)(2,1)S(1)} %get-tuple-element.184), channel_id=1, source_target_pairs={{0,2},{6,4},{1,3},{7,5},{8,10},{14,12},{9,11},{15,13},{16,18},{22,... | collective-permute-start | bytes 1032200 | tf_op jit(solution)/shard_map/ppermute | solution.py:135
  27.4 20.5 %collective-permute-start.7 = (bf16[56,3072]{1,0:T(8,128)(2,1)S(1)}, bf16[56,3072]{1,0:T(8,128)(2,1)S(1)}, u32[]{:S(2)}, u32[]{:S(2)}) collective-permute-start(bf16[56,3072]{1,0:T(8,128)(2,1)S(1)} %get-tuple-element.182), channel_id=1, source_target_pairs={{0,2},{6,4},{1,3},{7,5},{8,10},{14,12},{9,11},{15,13},{16,18},{22,... | collective-permute-start | bytes 1032200 | tf_op jit(solution)/shard_map/ppermute | solution.py:135
  28.7 26.5 %collective-permute-start.11 = (bf16[56,3072]{1,0:T(8,128)(2,1)S(1)}, bf16[56,3072]{1,0:T(8,128)(2,1)S(1)}, u32[]{:S(2)}, u32[]{:S(2)}) collective-permute-start(bf16[56,3072]{1,0:T(8,128)(2,1)S(1)} %get-tuple-element.185), channel_id=1, source_target_pairs={{0,2},{6,4},{1,3},{7,5},{8,10},{14,12},{9,11},{15,13},{16,18},{22,... | collective-permute-start | bytes 1032200 | tf_op jit(solution)/shard_map/ppermute | solution.py:135
  33.3 14.6 %collective-permute-start.4 = (bf16[56,3072]{1,0:T(8,128)(2,1)S(1)}, bf16[56,3072]{1,0:T(8,128)(2,1)S(1)}, u32[]{:S(2)}, u32[]{:S(2)}) collective-permute-start(bf16[56,3072]{1,0:T(8,128)(2,1)S(1)} %add_convert_fusion.17), channel_id=1, source_target_pairs={{2,4},{4,2},{3,5},{5,3},{10,12},{12,10},{11,13},{13,11},{18,20},{2... | collective-permute-start | bytes 1032200 | tf_op jit(solution)/shard_map/ppermute | solution.py:135
  40.6 14.6 %collective-permute-start.9 = (bf16[56,3072]{1,0:T(8,128)(2,1)S(1)}, bf16[56,3072]{1,0:T(8,128)(2,1)S(1)}, u32[]{:S(2)}, u32[]{:S(2)}) collective-permute-start(bf16[56,3072]{1,0:T(8,128)(2,1)S(1)} %add_convert_fusion.16), channel_id=1, source_target_pairs={{2,4},{4,2},{3,5},{5,3},{10,12},{12,10},{11,13},{13,11},{18,20},{2... | collective-permute-start | bytes 1032200 | tf_op jit(solution)/shard_map/ppermute | solution.py:135
  48.1 14.5 %collective-permute-start.6 = (bf16[56,3072]{1,0:T(8,128)(2,1)S(1)}, bf16[56,3072]{1,0:T(8,128)(2,1)S(1)}, u32[]{:S(2)}, u32[]{:S(2)}) collective-permute-start(bf16[56,3072]{1,0:T(8,128)(2,1)S(1)} %get-tuple-element.181), channel_id=1, source_target_pairs={{0,2},{2,0},{4,6},{6,4},{1,3},{3,1},{5,7},{7,5},{8,10},{10,8},{12,... | collective-permute-start | bytes 1032200 | tf_op jit(solution)/shard_map/ppermute | solution.py:135
  50.7 11.9 %collective-permute-start.8 = (bf16[56,3072]{1,0:T(8,128)(2,1)S(1)}, bf16[56,3072]{1,0:T(8,128)(2,1)S(1)}, u32[]{:S(2)}, u32[]{:S(2)}) collective-permute-start(bf16[56,3072]{1,0:T(8,128)(2,1)S(1)} %get-tuple-element.180), channel_id=1, source_target_pairs={{2,4},{4,2},{3,5},{5,3},{10,12},{12,10},{11,13},{13,11},{18,20},{2... | collective-permute-start | bytes 1032200 | tf_op jit(solution)/shard_map/ppermute | solution.py:135
  55.5 14.5 %collective-permute-start.10 = (bf16[56,3072]{1,0:T(8,128)(2,1)S(1)}, bf16[56,3072]{1,0:T(8,128)(2,1)S(1)}, u32[]{:S(2)}, u32[]{:S(2)}) collective-permute-start(bf16[56,3072]{1,0:T(8,128)(2,1)S(1)} %get-tuple-element.178), channel_id=1, source_target_pairs={{0,2},{2,0},{4,6},{6,4},{1,3},{3,1},{5,7},{7,5},{8,10},{10,8},{12,... | collective-permute-start | bytes 1032200 | tf_op jit(solution)/shard_map/ppermute | solution.py:135
  58.0 11.9 %collective-permute-start.12 = (bf16[56,3072]{1,0:T(8,128)(2,1)S(1)}, bf16[56,3072]{1,0:T(8,128)(2,1)S(1)}, u32[]{:S(2)}, u32[]{:S(2)}) collective-permute-start(bf16[56,3072]{1,0:T(8,128)(2,1)S(1)} %get-tuple-element.179), channel_id=1, source_target_pairs={{2,4},{4,2},{3,5},{5,3},{10,12},{12,10},{11,13},{13,11},{18,20},{2... | collective-permute-start | bytes 1032200 | tf_op jit(solution)/shard_map/ppermute | solution.py:135
  63.6 14.4 %collective-permute-start.16 = (bf16[56,3072]{1,0:T(8,128)(2,1)S(1)}, bf16[56,3072]{1,0:T(8,128)(2,1)S(1)}, u32[]{:S(2)}, u32[]{:S(2)}) collective-permute-start(bf16[56,3072]{1,0:T(8,128)(2,1)S(1)} %maximum_convert_fusion.3), channel_id=1, source_target_pairs={{0,2},{2,0},{4,6},{6,4},{1,3},{3,1},{5,7},{7,5},{8,10},{10,8},{12,... | collective-permute-start | bytes 1032200 | tf_op jit(solution)/shard_map/ppermute | solution.py:135
  70.2 14.8 %collective-permute-start.17 = (bf16[56,3072]{1,0:T(8,128)(2,1)S(1)}, bf16[56,3072]{1,0:T(8,128)(2,1)S(1)}, u32[]{:S(2)}, u32[]{:S(2)}) collective-permute-start(bf16[56,3072]{1,0:T(8,128)(2,1)S(1)} %maximum_convert_fusion.2), channel_id=1, source_target_pairs={{0,2},{2,0},{4,6},{6,4},{1,3},{3,1},{5,7},{7,5},{8,10},{10,8},{12,... | collective-permute-start | bytes 1032200 | tf_op jit(solution)/shard_map/ppermute | solution.py:135
  72.7 12.2 %collective-permute-start.15 = (bf16[56,3072]{1,0:T(8,128)(2,1)S(1)}, bf16[56,3072]{1,0:T(8,128)(2,1)S(1)}, u32[]{:S(2)}, u32[]{:S(2)}) collective-permute-start(bf16[56,3072]{1,0:T(8,128)(2,1)S(1)} %maximum_convert_fusion.2), channel_id=1, source_target_pairs={{2,4},{4,2},{3,5},{5,3},{10,12},{12,10},{11,13},{13,11},{18,20},{2... | collective-permute-start | bytes 1032200 | tf_op jit(solution)/shard_map/ppermute | solution.py:135
  78.3 12.7 %collective-permute-start.19 = (bf16[56,3072]{1,0:T(8,128)(2,1)S(1)}, bf16[56,3072]{1,0:T(8,128)(2,1)S(1)}, u32[]{:S(2)}, u32[]{:S(2)}) collective-permute-start(bf16[56,3072]{1,0:T(8,128)(2,1)S(1)} %get-tuple-element.176), channel_id=1, source_target_pairs={{2,4},{4,2},{3,5},{5,3},{10,12},{12,10},{11,13},{13,11},{18,20},{2... | collective-permute-start | bytes 1032200 | tf_op jit(solution)/shard_map/ppermute | solution.py:135
  78.9 13.3 %collective-permute-start.14 = (bf16[56,3072]{1,0:T(8,128)(2,1)S(1)}, bf16[56,3072]{1,0:T(8,128)(2,1)S(1)}, u32[]{:S(2)}, u32[]{:S(2)}) collective-permute-start(bf16[56,3072]{1,0:T(8,128)(2,1)S(1)} %get-tuple-element.177), channel_id=1, source_target_pairs={{0,2},{2,0},{4,6},{6,4},{1,3},{3,1},{5,7},{7,5},{8,10},{10,8},{12,... | collective-permute-start | bytes 1032200 | tf_op jit(solution)/shard_map/ppermute | solution.py:135
  85.2 13.1 %collective-permute-start.21 = (bf16[56,3072]{1,0:T(8,128)(2,1)S(1)}, bf16[56,3072]{1,0:T(8,128)(2,1)S(1)}, u32[]{:S(2)}, u32[]{:S(2)}) collective-permute-start(bf16[56,3072]{1,0:T(8,128)(2,1)S(1)} %get-tuple-element.175), channel_id=1, source_target_pairs={{2,4},{4,2},{3,5},{5,3},{10,12},{12,10},{11,13},{13,11},{18,20},{2... | collective-permute-start | bytes 1032200 | tf_op jit(solution)/shard_map/ppermute | solution.py:135
  85.9 13.8 %collective-permute-start.22 = (bf16[56,3072]{1,0:T(8,128)(2,1)S(1)}, bf16[56,3072]{1,0:T(8,128)(2,1)S(1)}, u32[]{:S(2)}, u32[]{:S(2)}) collective-permute-start(bf16[56,3072]{1,0:T(8,128)(2,1)S(1)} %get-tuple-element.174), channel_id=1, source_target_pairs={{0,2},{2,0},{4,6},{6,4},{1,3},{3,1},{5,7},{7,5},{8,10},{10,8},{12,... | collective-permute-start | bytes 1032200 | tf_op jit(solution)/shard_map/ppermute | solution.py:135
  93.2 14.1 %collective-permute-start.20 = (bf16[56,3072]{1,0:T(8,128)(2,1)S(1)}, bf16[56,3072]{1,0:T(8,128)(2,1)S(1)}, u32[]{:S(2)}, u32[]{:S(2)}) collective-permute-start(bf16[56,3072]{1,0:T(8,128)(2,1)S(1)} %get-tuple-element.173), channel_id=1, source_target_pairs={{0,2},{2,0},{4,6},{6,4},{1,3},{3,1},{5,7},{7,5},{8,10},{10,8},{12,... | collective-permute-start | bytes 1032200 | tf_op jit(solution)/shard_map/ppermute | solution.py:135
  99.9 16.7 %collective-permute-start.27 = (bf16[56,3072]{1,0:T(8,128)(2,1)S(1)}, bf16[56,3072]{1,0:T(8,128)(2,1)S(1)}, u32[]{:S(2)}, u32[]{:S(2)}) collective-permute-start(bf16[56,3072]{1,0:T(8,128)(2,1)S(1)} %get-tuple-element.171), channel_id=1, source_target_pairs={{0,2},{2,0},{4,6},{6,4},{1,3},{3,1},{5,7},{7,5},{8,10},{10,8},{12,... | collective-permute-start | bytes 1032200 | tf_op jit(solution)/shard_map/ppermute | solution.py:135
  102.4 14.2 %collective-permute-start.25 = (bf16[56,3072]{1,0:T(8,128)(2,1)S(1)}, bf16[56,3072]{1,0:T(8,128)(2,1)S(1)}, u32[]{:S(2)}, u32[]{:S(2)}) collective-permute-start(bf16[56,3072]{1,0:T(8,128)(2,1)S(1)} %get-tuple-element.170), channel_id=1, source_target_pairs={{2,4},{4,2},{3,5},{5,3},{10,12},{12,10},{11,13},{13,11},{18,20},{2... | collective-permute-start | bytes 1032200 | tf_op jit(solution)/shard_map/ppermute | solution.py:135
  110.7 12.6 %collective-permute-start.23 = (bf16[56,3072]{1,0:T(8,128)(2,1)S(1)}, bf16[56,3072]{1,0:T(8,128)(2,1)S(1)}, u32[]{:S(2)}, u32[]{:S(2)}) collective-permute-start(bf16[56,3072]{1,0:T(8,128)(2,1)S(1)} %get-tuple-element.167), channel_id=1, source_target_pairs={{0,2},{2,0},{4,6},{6,4},{1,3},{3,1},{5,7},{7,5},{8,10},{10,8},{12,... | collective-permute-start | bytes 1032200 | tf_op jit(solution)/shard_map/ppermute | solution.py:135
  116.9 12.3 %collective-permute-start.26 = (bf16[56,3072]{1,0:T(8,128)(2,1)S(1)}, bf16[56,3072]{1,0:T(8,128)(2,1)S(1)}, u32[]{:S(2)}, u32[]{:S(2)}) collective-permute-start(bf16[56,3072]{1,0:T(8,128)(2,1)S(1)} %get-tuple-element.164), channel_id=1, source_target_pairs={{0,2},{2,0},{4,6},{6,4},{1,3},{3,1},{5,7},{7,5},{8,10},{10,8},{12,... | collective-permute-start | bytes 1032200 | tf_op jit(solution)/shard_map/ppermute | solution.py:135
  123.6 13.0 %collective-permute-start.29 = (bf16[56,3072]{1,0:T(8,128)(2,1)S(1)}, bf16[56,3072]{1,0:T(8,128)(2,1)S(1)}, u32[]{:S(2)}, u32[]{:S(2)}) collective-permute-start(bf16[56,3072]{1,0:T(8,128)(2,1)S(1)} %maximum_convert_fusion.1), channel_id=1, source_target_pairs={{0,2},{2,0},{4,6},{6,4},{1,3},{3,1},{5,7},{7,5},{8,10},{10,8},{12,... | collective-permute-start | bytes 1032200 | tf_op jit(solution)/shard_map/ppermute | solution.py:135
  129.3 13.6 %collective-permute-start.33 = (bf16[56,3072]{1,0:T(8,128)(2,1)S(1)}, bf16[56,3072]{1,0:T(8,128)(2,1)S(1)}, u32[]{:S(2)}, u32[]{:S(2)}) collective-permute-start(bf16[56,3072]{1,0:T(8,128)(2,1)S(1)} %maximum_convert_fusion), channel_id=1, source_target_pairs={{0,2},{2,0},{4,6},{6,4},{1,3},{3,1},{5,7},{7,5},{8,10},{10,8},{12,... | collective-permute-start | bytes 1032200 | tf_op jit(solution)/shard_map/ppermute | solution.py:135
  132.7 13.7 %collective-permute-start.31 = (bf16[56,3072]{1,0:T(8,128)(2,1)S(1)}, bf16[56,3072]{1,0:T(8,128)(2,1)S(1)}, u32[]{:S(2)}, u32[]{:S(2)}) collective-permute-start(bf16[56,3072]{1,0:T(8,128)(2,1)S(1)} %maximum_convert_fusion), channel_id=1, source_target_pairs={{2,4},{4,2},{3,5},{5,3},{10,12},{12,10},{11,13},{13,11},{18,20},{2... | collective-permute-start | bytes 1032200 | tf_op jit(solution)/shard_map/ppermute | solution.py:135
  145.0 15.5 %collective-permute-start.40 = (bf16[56,3072]{1,0:T(8,128)(2,1)S(1)}, bf16[56,3072]{1,0:T(8,128)(2,1)S(1)}, u32[]{:S(2)}, u32[]{:S(2)}) collective-permute-start(bf16[56,3072]{1,0:T(8,128)(2,1)S(1)} %collective-permute-done.32), channel_id=1, source_target_pairs={{2,0},{4,6},{3,1},{5,7},{10,8},{12,14},{11,9},{13,15},{18,16},{20,... | collective-permute-start | bytes 1032200 | tf_op jit(solution)/shard_map/ppermute | solution.py:135
  146.3 34.0 %collective-permute-start.42 = (bf16[56,3072]{1,0:T(8,128)(2,1)S(1)}, bf16[56,3072]{1,0:T(8,128)(2,1)S(1)}, u32[]{:S(2)}, u32[]{:S(2)}) collective-permute-start(bf16[56,3072]{1,0:T(8,128)(2,1)S(1)} %collective-permute-done.31), channel_id=1, source_target_pairs={{2,0},{4,6},{3,1},{5,7},{10,8},{12,14},{11,9},{13,15},{18,16},{20,... | collective-permute-start | bytes 1032200 | tf_op jit(solution)/shard_map/ppermute | solution.py:135
  147.7 27.6 %collective-permute-start.41 = (bf16[56,3072]{1,0:T(8,128)(2,1)S(1)}, bf16[56,3072]{1,0:T(8,128)(2,1)S(1)}, u32[]{:S(2)}, u32[]{:S(2)}) collective-permute-start(bf16[56,3072]{1,0:T(8,128)(2,1)S(1)} %collective-permute-done.30), channel_id=1, source_target_pairs={{2,0},{4,6},{3,1},{5,7},{10,8},{12,14},{11,9},{13,15},{18,16},{20,... | collective-permute-start | bytes 1032200 | tf_op jit(solution)/shard_map/ppermute | solution.py:135
  149.0 33.6 %collective-permute-start.43 = (bf16[56,3072]{1,0:T(8,128)(2,1)S(1)}, bf16[56,3072]{1,0:T(8,128)(2,1)S(1)}, u32[]{:S(2)}, u32[]{:S(2)}) collective-permute-start(bf16[56,3072]{1,0:T(8,128)(2,1)S(1)} %collective-permute-done.34), channel_id=1, source_target_pairs={{2,0},{4,6},{3,1},{5,7},{10,8},{12,14},{11,9},{13,15},{18,16},{20,... | collective-permute-start | bytes 1032200 | tf_op jit(solution)/shard_map/ppermute | solution.py:135
  152.6 34.6 %collective-permute-start.35 = (bf16[1,2,56,576]{3,2,1,0:T(8,128)(2,1)S(1)}, bf16[1,2,56,576]{3,2,1,0:T(8,128)(2,1)S(1)}, u32[]{:S(2)}, u32[]{:S(2)}) collective-permute-start(bf16[1,2,56,576]{3,2,1,0:T(8,128)(2,1)S(1)} %pad_maximum_fusion.12), channel_id=1, source_target_pairs={{0,1},{1,0},{2,3},{3,2},{4,5},{5,4},{6,7},{7,6},{8,9},{9,8},{10,11... | collective-permute-start | bytes 387080 | tf_op jit(solution)/shard_map/ppermute | solution.py:200
  160.5 26.7 %collective-permute-start.37 = (bf16[2,56,576]{2,1,0:T(8,128)(2,1)S(1)}, bf16[2,56,576]{2,1,0:T(8,128)(2,1)S(1)}, u32[]{:S(2)}, u32[]{:S(2)}) collective-permute-start(bf16[2,56,576]{2,1,0:T(8,128)(2,1)S(1)} %get-tuple-element.195), channel_id=1, source_target_pairs={{0,8},{16,24},{1,9},{17,25},{2,10},{18,26},{3,11},{19,27},{4,12},{... | collective-permute-start | bytes 387080 | tf_op jit(solution)/shard_map/ppermute | solution.py:213
  175.3 12.0 %collective-permute-start.38 = (bf16[2,56,576]{2,1,0:T(8,128)(2,1)S(1)}, bf16[2,56,576]{2,1,0:T(8,128)(2,1)S(1)}, u32[]{:S(2)}, u32[]{:S(2)}) collective-permute-start(bf16[2,56,576]{2,1,0:T(8,128)(2,1)S(1)} %get-tuple-element.194), channel_id=1, source_target_pairs={{0,16},{8,24},{1,17},{9,25},{2,18},{10,26},{3,19},{11,27},{4,20},{... | collective-permute-start | bytes 387080 | tf_op jit(solution)/shard_map/ppermute | solution.py:213
  (26 other events, 619.1 us)

commit v4 on v3

--- a/solution.py
+++ b/solution.py
@@ -240,7 +240,7 @@
         finish(group)
     for layer in reversed(range(1, layers)):
         for piece in last:
-            sent = piece(layer, every)([sent, residuals.get(GROUPS - 2)] if layer == 1 else sent)
+            sent = piece(layer, every)([sent, residuals.get(GROUPS - 2)] if layer == 1 and piece is last[-1] else sent)
     sent = share_cores(GROUPS - 1, sent)
     sent = share_segments(GROUPS - 1, sent)
     for piece in last:

time: 207 us -> 206 us (level)
  transfers between devices with their start and end apart: 49 -> 49, of which waited for: 22 -> 22; matrix products, arithmetic and copies ran while one was open for 15% -> 16% of each run, Pallas kernels for 0% -> 0%
where the time goes in v4:
time: 206 us; the launch traced here: 205 us
  starting transfers between devices  86.2 us (42%)
  waiting for transfers between devices  73.2 us (36%)
  matrix products  30.5 us (15%)
  other arithmetic  6.97 us (3%)
  blocking collectives  4.68 us (2%)
    ppermute x36, starting transfers between devices, swap(): return lax.ppermute(value, 'feat', pairs) if pairs else None  64.8 us
    ppermute x36, waiting for transfers between devices, swap(): return lax.ppermute(value, 'feat', pairs) if pairs else None  64 us
    dot_general x16, matrix products, run(): lax.dot_general(after(codes[key], sent), decoders[layer, :, chunk * width...  23.3 us
    ppermute x6, starting transfers between devices, share_segments(): lax.ppermute(given[-1], 'segment', [(i, j) for i, j in pairs if i < j < s...  15.5 us
    dot_general x4, matrix products, partial_sums(): jnp.dot(after(columns[group], sent), weight[:, chunk * width:(chunk + 1)...  7.21 us
    ppermute x3, starting transfers between devices, exchanged(): part = lax.ppermute(part, 'feat', pairs)  5.6 us
    ppermute x3, waiting for transfers between devices, exchanged(): part = lax.ppermute(part, 'feat', pairs)  5.5 us
  transfers between devices with their start and end apart: 49, of which 22 were waited for; matrix products, arithmetic and copies ran while one was open for 16% of the time, Pallas kernels for 0%

profile of v4, /device:TPU:0, one launch (start us, length us, event | category | flops | bytes accessed | tf_op | source)
XLA Modules:
  0.0 205.1 jit_solution(4413764954350561824)
XLA Ops:
  0.7 2.5 %all-gather = bf16[1,112,2304]{2,1,0:T(8,128)(2,1)S(1)} all-gather(bf16[1,112,1152]{2,1,0:T(8,128)(2,1)} %param.5), channel_id=2, replica_groups=mesh['segment'=4,'feat'=4,'tok'=2] {'tok'}, dimensions={2}, use_global_device_ids=true | all-gather | bytes 774144 | tf_op jit(solution)/shard_map/all_gather | solution.py:27
  3.3 3.0 %collective-permute-start = (bf16[56,576]{1,0:T(8,128)(2,1)S(1)}, bf16[56,576]{1,0:T(8,128)(2,1)S(1)}, u32[]{:S(2)}, u32[]{:S(2)}) collective-permute-start(bf16[56,576]{1,0:T(8,128)(2,1)S(1)} %get-tuple-element.214), channel_id=1, source_target_pairs={{0,2},{2,0},{4,6},{6,4},{1,3},{3,1},{5,7},{7,5},{8,10},{10,8},{12,... | collective-permute-start | bytes 193544 | tf_op jit(solution)/shard_map/ppermute | solution.py:40
  6.3 2.6 %collective-permute-start.1 = (bf16[56,576]{1,0:T(8,128)(2,1)S(1)}, bf16[56,576]{1,0:T(8,128)(2,1)S(1)}, u32[]{:S(2)}, u32[]{:S(2)}) collective-permute-start(bf16[56,576]{1,0:T(8,128)(2,1)S(1)} %get-tuple-element.213), channel_id=1, source_target_pairs={{0,4},{2,6},{4,0},{6,2},{1,5},{3,7},{5,1},{7,3},{8,12},{10,14},{12... | collective-permute-start | bytes 193544 | tf_op jit(solution)/shard_map/ppermute | solution.py:40
  9.7 4.6 %collective-permute-done.1 = bf16[56,576]{1,0:T(8,128)(2,1)S(1)} collective-permute-done((bf16[56,576]{1,0:T(8,128)(2,1)S(1)}, bf16[56,576]{1,0:T(8,128)(2,1)S(1)}, u32[]{:S(2)}, u32[]{:S(2)}) %collective-permute-start.1) | collective-permute-done | bytes 64544 | tf_op jit(solution)/shard_map/ppermute | solution.py:40
  17.6 3.4 %convolution_convert_fusion.3 = bf16[224,3072]{1,0:T(8,128)(2,1)S(1)} fusion(bf16[576,6144]{1,0:T(8,128)(2,1)} %bitcast.175, bf16[56,576]{1,0:T(8,128)(2,1)S(1)} %get-tuple-element.205, bf16[56,576]{1,0:T(8,128)(2,1)S(1)} %get-tuple-element.206, bf16[56,576]{1,0:T(8,128)(2,1)S(1)} %get-tuple-element.207, bf16[56,576]{1,0:T(8,128)(2,1)S(1)} %get-tuple-element.208), kind=kOutput, calls=%fused_computation.3 | convolution fusion | flops 794443776 | bytes 5173248 | tf_op jit(solution)/shard_map/dot_general | solution.py:53
  21.1 3.6 %collective-permute-start.3 = (bf16[56,3072]{1,0:T(8,128)(2,1)S(1)}, bf16[56,3072]{1,0:T(8,128)(2,1)S(1)}, u32[]{:S(2)}, u32[]{:S(2)}) collective-permute-start(bf16[56,3072]{1,0:T(8,128)(2,1)S(1)} %get-tuple-element.183), channel_id=1, source_target_pairs={{0,2},{6,4},{1,3},{7,5},{8,10},{14,12},{9,11},{15,13},{16,18},{22,... | collective-permute-start | bytes 1032200 | tf_op jit(solution)/shard_map/ppermute | solution.py:135
  33.9 6.5 %collective-permute-done.5 = bf16[56,3072]{1,0:T(8,128)(2,1)S(1)} collective-permute-done((bf16[56,3072]{1,0:T(8,128)(2,1)S(1)}, bf16[56,3072]{1,0:T(8,128)(2,1)S(1)}, u32[]{:S(2)}, u32[]{:S(2)}) %collective-permute-start.5) | collective-permute-done | bytes 344096 | tf_op jit(solution)/shard_map/ppermute | solution.py:135
  41.3 6.5 %collective-permute-done.7 = bf16[56,3072]{1,0:T(8,128)(2,1)S(1)} collective-permute-done((bf16[56,3072]{1,0:T(8,128)(2,1)S(1)}, bf16[56,3072]{1,0:T(8,128)(2,1)S(1)}, u32[]{:S(2)}, u32[]{:S(2)}) %collective-permute-start.7) | collective-permute-done | bytes 344096 | tf_op jit(solution)/shard_map/ppermute | solution.py:135
  48.1 2.5 %collective-permute-start.6 = (bf16[56,3072]{1,0:T(8,128)(2,1)S(1)}, bf16[56,3072]{1,0:T(8,128)(2,1)S(1)}, u32[]{:S(2)}, u32[]{:S(2)}) collective-permute-start(bf16[56,3072]{1,0:T(8,128)(2,1)S(1)} %get-tuple-element.181), channel_id=1, source_target_pairs={{0,2},{2,0},{4,6},{6,4},{1,3},{3,1},{5,7},{7,5},{8,10},{10,8},{12,... | collective-permute-start | bytes 1032200 | tf_op jit(solution)/shard_map/ppermute | solution.py:135
  51.3 3.9 %collective-permute-done.11 = bf16[56,3072]{1,0:T(8,128)(2,1)S(1)} collective-permute-done((bf16[56,3072]{1,0:T(8,128)(2,1)S(1)}, bf16[56,3072]{1,0:T(8,128)(2,1)S(1)}, u32[]{:S(2)}, u32[]{:S(2)}) %collective-permute-start.11) | collective-permute-done | bytes 344096 | tf_op jit(solution)/shard_map/ppermute | solution.py:135
  55.5 2.5 %collective-permute-start.10 = (bf16[56,3072]{1,0:T(8,128)(2,1)S(1)}, bf16[56,3072]{1,0:T(8,128)(2,1)S(1)}, u32[]{:S(2)}, u32[]{:S(2)}) collective-permute-start(bf16[56,3072]{1,0:T(8,128)(2,1)S(1)} %get-tuple-element.178), channel_id=1, source_target_pairs={{0,2},{2,0},{4,6},{6,4},{1,3},{3,1},{5,7},{7,5},{8,10},{10,8},{12,... | collective-permute-start | bytes 1032200 | tf_op jit(solution)/shard_map/ppermute | solution.py:135
  58.7 3.9 %collective-permute-done.6 = bf16[56,3072]{1,0:T(8,128)(2,1)S(1)} collective-permute-done((bf16[56,3072]{1,0:T(8,128)(2,1)S(1)}, bf16[56,3072]{1,0:T(8,128)(2,1)S(1)}, u32[]{:S(2)}, u32[]{:S(2)}) %collective-permute-start.6) | collective-permute-done | bytes 344096 | tf_op jit(solution)/shard_map/ppermute | solution.py:135
  63.6 5.4 %collective-permute-start.16 = (bf16[56,3072]{1,0:T(8,128)(2,1)S(1)}, bf16[56,3072]{1,0:T(8,128)(2,1)S(1)}, u32[]{:S(2)}, u32[]{:S(2)}) collective-permute-start(bf16[56,3072]{1,0:T(8,128)(2,1)S(1)} %maximum_convert_fusion.3), channel_id=1, source_target_pairs={{0,2},{2,0},{4,6},{6,4},{1,3},{3,1},{5,7},{7,5},{8,10},{10,8},{12,... | collective-permute-start | bytes 1032200 | tf_op jit(solution)/shard_map/ppermute | solution.py:135
  70.2 2.5 %collective-permute-start.17 = (bf16[56,3072]{1,0:T(8,128)(2,1)S(1)}, bf16[56,3072]{1,0:T(8,128)(2,1)S(1)}, u32[]{:S(2)}, u32[]{:S(2)}) collective-permute-start(bf16[56,3072]{1,0:T(8,128)(2,1)S(1)} %maximum_convert_fusion.2), channel_id=1, source_target_pairs={{0,2},{2,0},{4,6},{6,4},{1,3},{3,1},{5,7},{7,5},{8,10},{10,8},{12,... | collective-permute-start | bytes 1032200 | tf_op jit(solution)/shard_map/ppermute | solution.py:135
  73.4 4.6 %collective-permute-done.16 = bf16[56,3072]{1,0:T(8,128)(2,1)S(1)} collective-permute-done((bf16[56,3072]{1,0:T(8,128)(2,1)S(1)}, bf16[56,3072]{1,0:T(8,128)(2,1)S(1)}, u32[]{:S(2)}, u32[]{:S(2)}) %collective-permute-start.16) | collective-permute-done | bytes 344096 | tf_op jit(solution)/shard_map/ppermute | solution.py:135
  78.9 4.6 %collective-permute-start.14 = (bf16[56,3072]{1,0:T(8,128)(2,1)S(1)}, bf16[56,3072]{1,0:T(8,128)(2,1)S(1)}, u32[]{:S(2)}, u32[]{:S(2)}) collective-permute-start(bf16[56,3072]{1,0:T(8,128)(2,1)S(1)} %get-tuple-element.177), channel_id=1, source_target_pairs={{0,2},{2,0},{4,6},{6,4},{1,3},{3,1},{5,7},{7,5},{8,10},{10,8},{12,... | collective-permute-start | bytes 1032200 | tf_op jit(solution)/shard_map/ppermute | solution.py:135
  85.9 5.1 %collective-permute-start.22 = (bf16[56,3072]{1,0:T(8,128)(2,1)S(1)}, bf16[56,3072]{1,0:T(8,128)(2,1)S(1)}, u32[]{:S(2)}, u32[]{:S(2)}) collective-permute-start(bf16[56,3072]{1,0:T(8,128)(2,1)S(1)} %get-tuple-element.174), channel_id=1, source_target_pairs={{0,2},{2,0},{4,6},{6,4},{1,3},{3,1},{5,7},{7,5},{8,10},{10,8},{12,... | collective-permute-start | bytes 1032200 | tf_op jit(solution)/shard_map/ppermute | solution.py:135
  93.2 5.1 %collective-permute-start.20 = (bf16[56,3072]{1,0:T(8,128)(2,1)S(1)}, bf16[56,3072]{1,0:T(8,128)(2,1)S(1)}, u32[]{:S(2)}, u32[]{:S(2)}) collective-permute-start(bf16[56,3072]{1,0:T(8,128)(2,1)S(1)} %get-tuple-element.173), channel_id=1, source_target_pairs={{0,2},{2,0},{4,6},{6,4},{1,3},{3,1},{5,7},{7,5},{8,10},{10,8},{12,... | collective-permute-start | bytes 1032200 | tf_op jit(solution)/shard_map/ppermute | solution.py:135
  99.9 2.5 %collective-permute-start.27 = (bf16[56,3072]{1,0:T(8,128)(2,1)S(1)}, bf16[56,3072]{1,0:T(8,128)(2,1)S(1)}, u32[]{:S(2)}, u32[]{:S(2)}) collective-permute-start(bf16[56,3072]{1,0:T(8,128)(2,1)S(1)} %get-tuple-element.171), channel_id=1, source_target_pairs={{0,2},{2,0},{4,6},{6,4},{1,3},{3,1},{5,7},{7,5},{8,10},{10,8},{12,... | collective-permute-start | bytes 1032200 | tf_op jit(solution)/shard_map/ppermute | solution.py:135
  103.3 4.0 %collective-permute-done.20 = bf16[56,3072]{1,0:T(8,128)(2,1)S(1)} collective-permute-done((bf16[56,3072]{1,0:T(8,128)(2,1)S(1)}, bf16[56,3072]{1,0:T(8,128)(2,1)S(1)}, u32[]{:S(2)}, u32[]{:S(2)}) %collective-permute-start.20) | collective-permute-done | bytes 344096 | tf_op jit(solution)/shard_map/ppermute | solution.py:135
  110.8 2.3 %collective-permute-start.23 = (bf16[56,3072]{1,0:T(8,128)(2,1)S(1)}, bf16[56,3072]{1,0:T(8,128)(2,1)S(1)}, u32[]{:S(2)}, u32[]{:S(2)}) collective-permute-start(bf16[56,3072]{1,0:T(8,128)(2,1)S(1)} %get-tuple-element.167), channel_id=1, source_target_pairs={{0,2},{2,0},{4,6},{6,4},{1,3},{3,1},{5,7},{7,5},{8,10},{10,8},{12,... | collective-permute-start | bytes 1032200 | tf_op jit(solution)/shard_map/ppermute | solution.py:135
  116.9 2.6 %collective-permute-start.26 = (bf16[56,3072]{1,0:T(8,128)(2,1)S(1)}, bf16[56,3072]{1,0:T(8,128)(2,1)S(1)}, u32[]{:S(2)}, u32[]{:S(2)}) collective-permute-start(bf16[56,3072]{1,0:T(8,128)(2,1)S(1)} %get-tuple-element.164), channel_id=1, source_target_pairs={{0,2},{2,0},{4,6},{6,4},{1,3},{3,1},{5,7},{7,5},{8,10},{10,8},{12,... | collective-permute-start | bytes 1032200 | tf_op jit(solution)/shard_map/ppermute | solution.py:135
  126.4 2.8 %collective-permute-done.26 = bf16[56,3072]{1,0:T(8,128)(2,1)S(1)} collective-permute-done((bf16[56,3072]{1,0:T(8,128)(2,1)S(1)}, bf16[56,3072]{1,0:T(8,128)(2,1)S(1)}, u32[]{:S(2)}, u32[]{:S(2)}) %collective-permute-start.26) | collective-permute-done | bytes 344096 | tf_op jit(solution)/shard_map/ppermute | solution.py:135
  129.3 3.4 %collective-permute-start.33 = (bf16[56,3072]{1,0:T(8,128)(2,1)S(1)}, bf16[56,3072]{1,0:T(8,128)(2,1)S(1)}, u32[]{:S(2)}, u32[]{:S(2)}) collective-permute-start(bf16[56,3072]{1,0:T(8,128)(2,1)S(1)} %maximum_convert_fusion), channel_id=1, source_target_pairs={{0,2},{2,0},{4,6},{6,4},{1,3},{3,1},{5,7},{7,5},{8,10},{10,8},{12,... | collective-permute-start | bytes 1032200 | tf_op jit(solution)/shard_map/ppermute | solution.py:135
  137.2 5.7 %collective-permute-done.33 = bf16[56,3072]{1,0:T(8,128)(2,1)S(1)} collective-permute-done((bf16[56,3072]{1,0:T(8,128)(2,1)S(1)}, bf16[56,3072]{1,0:T(8,128)(2,1)S(1)}, u32[]{:S(2)}, u32[]{:S(2)}) %collective-permute-start.33) | collective-permute-done | bytes 344096 | tf_op jit(solution)/shard_map/ppermute | solution.py:135
  152.9 7.6 %collective-permute-done.40 = bf16[56,3072]{1,0:T(8,128)(2,1)S(1)} collective-permute-done((bf16[56,3072]{1,0:T(8,128)(2,1)S(1)}, bf16[56,3072]{1,0:T(8,128)(2,1)S(1)}, u32[]{:S(2)}, u32[]{:S(2)}) %collective-permute-start.40) | collective-permute-done | bytes 344096 | tf_op jit(solution)/shard_map/ppermute | solution.py:135
  160.5 3.4 %collective-permute-start.37 = (bf16[2,56,576]{2,1,0:T(8,128)(2,1)S(1)}, bf16[2,56,576]{2,1,0:T(8,128)(2,1)S(1)}, u32[]{:S(2)}, u32[]{:S(2)}) collective-permute-start(bf16[2,56,576]{2,1,0:T(8,128)(2,1)S(1)} %get-tuple-element.195), channel_id=1, source_target_pairs={{0,8},{16,24},{1,9},{17,25},{2,10},{18,26},{3,11},{19,27},{4,12},{... | collective-permute-start | bytes 387080 | tf_op jit(solution)/shard_map/ppermute | solution.py:213
  163.9 11.3 %collective-permute-done.41 = bf16[56,3072]{1,0:T(8,128)(2,1)S(1)} collective-permute-done((bf16[56,3072]{1,0:T(8,128)(2,1)S(1)}, bf16[56,3072]{1,0:T(8,128)(2,1)S(1)}, u32[]{:S(2)}, u32[]{:S(2)}) %collective-permute-start.41) | collective-permute-done | bytes 344096 | tf_op jit(solution)/shard_map/ppermute | solution.py:135
  175.3 3.4 %collective-permute-start.38 = (bf16[2,56,576]{2,1,0:T(8,128)(2,1)S(1)}, bf16[2,56,576]{2,1,0:T(8,128)(2,1)S(1)}, u32[]{:S(2)}, u32[]{:S(2)}) collective-permute-start(bf16[2,56,576]{2,1,0:T(8,128)(2,1)S(1)} %get-tuple-element.194), channel_id=1, source_target_pairs={{0,16},{8,24},{1,17},{9,25},{2,18},{10,26},{3,19},{11,27},{4,20},{... | collective-permute-start | bytes 387080 | tf_op jit(solution)/shard_map/ppermute | solution.py:213
  180.4 2.2 %collective-permute-start.39 = (bf16[2,56,576]{2,1,0:T(8,128)(2,1)S(1)}, bf16[2,56,576]{2,1,0:T(8,128)(2,1)S(1)}, u32[]{:S(2)}, u32[]{:S(2)}) collective-permute-start(bf16[2,56,576]{2,1,0:T(8,128)(2,1)S(1)} %get-tuple-element.193), channel_id=1, source_target_pairs={{0,24},{8,16},{1,25},{9,17},{2,26},{10,18},{3,27},{11,19},{4,28},{... | collective-permute-start | bytes 387080 | tf_op jit(solution)/shard_map/ppermute | solution.py:213
  192.6 2.5 %collective-permute-start.46 = (bf16[2,56,576]{2,1,0:T(8,128)(2,1)S(1)}, bf16[2,56,576]{2,1,0:T(8,128)(2,1)S(1)}, u32[]{:S(2)}, u32[]{:S(2)}) collective-permute-start(bf16[2,56,576]{2,1,0:T(8,128)(2,1)S(1)} %get-tuple-element.192), channel_id=1, source_target_pairs={{0,8},{16,24},{1,9},{17,25},{2,10},{18,26},{3,11},{19,27},{4,12},{... | collective-permute-start | bytes 387080 | tf_op jit(solution)/shard_map/ppermute | solution.py:213
  195.1 2.6 %collective-permute-start.47 = (bf16[2,56,576]{2,1,0:T(8,128)(2,1)S(1)}, bf16[2,56,576]{2,1,0:T(8,128)(2,1)S(1)}, u32[]{:S(2)}, u32[]{:S(2)}) collective-permute-start(bf16[2,56,576]{2,1,0:T(8,128)(2,1)S(1)} %get-tuple-element.191), channel_id=1, source_target_pairs={{0,16},{8,24},{1,17},{9,25},{2,18},{10,26},{3,19},{11,27},{4,20},{... | collective-permute-start | bytes 387080 | tf_op jit(solution)/shard_map/ppermute | solution.py:213
  (163 shorter events, 74.1 us)
Async XLA Ops:
  21.1 12.0 %collective-permute-start.3 = (bf16[56,3072]{1,0:T(8,128)(2,1)S(1)}, bf16[56,3072]{1,0:T(8,128)(2,1)S(1)}, u32[]{:S(2)}, u32[]{:S(2)}) collective-permute-start(bf16[56,3072]{1,0:T(8,128)(2,1)S(1)} %get-tuple-element.183), channel_id=1, source_target_pairs={{0,2},{6,4},{1,3},{7,5},{8,10},{14,12},{9,11},{15,13},{16,18},{22,... | collective-permute-start | bytes 1032200 | tf_op jit(solution)/shard_map/ppermute | solution.py:135
  26.1 14.4 %collective-permute-start.5 = (bf16[56,3072]{1,0:T(8,128)(2,1)S(1)}, bf16[56,3072]{1,0:T(8,128)(2,1)S(1)}, u32[]{:S(2)}, u32[]{:S(2)}) collective-permute-start(bf16[56,3072]{1,0:T(8,128)(2,1)S(1)} %get-tuple-element.184), channel_id=1, source_target_pairs={{0,2},{6,4},{1,3},{7,5},{8,10},{14,12},{9,11},{15,13},{16,18},{22,... | collective-permute-start | bytes 1032200 | tf_op jit(solution)/shard_map/ppermute | solution.py:135
  27.4 20.4 %collective-permute-start.7 = (bf16[56,3072]{1,0:T(8,128)(2,1)S(1)}, bf16[56,3072]{1,0:T(8,128)(2,1)S(1)}, u32[]{:S(2)}, u32[]{:S(2)}) collective-permute-start(bf16[56,3072]{1,0:T(8,128)(2,1)S(1)} %get-tuple-element.182), channel_id=1, source_target_pairs={{0,2},{6,4},{1,3},{7,5},{8,10},{14,12},{9,11},{15,13},{16,18},{22,... | collective-permute-start | bytes 1032200 | tf_op jit(solution)/shard_map/ppermute | solution.py:135
  28.7 26.5 %collective-permute-start.11 = (bf16[56,3072]{1,0:T(8,128)(2,1)S(1)}, bf16[56,3072]{1,0:T(8,128)(2,1)S(1)}, u32[]{:S(2)}, u32[]{:S(2)}) collective-permute-start(bf16[56,3072]{1,0:T(8,128)(2,1)S(1)} %get-tuple-element.185), channel_id=1, source_target_pairs={{0,2},{6,4},{1,3},{7,5},{8,10},{14,12},{9,11},{15,13},{16,18},{22,... | collective-permute-start | bytes 1032200 | tf_op jit(solution)/shard_map/ppermute | solution.py:135
  33.3 14.6 %collective-permute-start.4 = (bf16[56,3072]{1,0:T(8,128)(2,1)S(1)}, bf16[56,3072]{1,0:T(8,128)(2,1)S(1)}, u32[]{:S(2)}, u32[]{:S(2)}) collective-permute-start(bf16[56,3072]{1,0:T(8,128)(2,1)S(1)} %add_convert_fusion.17), channel_id=1, source_target_pairs={{2,4},{4,2},{3,5},{5,3},{10,12},{12,10},{11,13},{13,11},{18,20},{2... | collective-permute-start | bytes 1032200 | tf_op jit(solution)/shard_map/ppermute | solution.py:135
  40.6 14.6 %collective-permute-start.9 = (bf16[56,3072]{1,0:T(8,128)(2,1)S(1)}, bf16[56,3072]{1,0:T(8,128)(2,1)S(1)}, u32[]{:S(2)}, u32[]{:S(2)}) collective-permute-start(bf16[56,3072]{1,0:T(8,128)(2,1)S(1)} %add_convert_fusion.16), channel_id=1, source_target_pairs={{2,4},{4,2},{3,5},{5,3},{10,12},{12,10},{11,13},{13,11},{18,20},{2... | collective-permute-start | bytes 1032200 | tf_op jit(solution)/shard_map/ppermute | solution.py:135
  48.1 14.5 %collective-permute-start.6 = (bf16[56,3072]{1,0:T(8,128)(2,1)S(1)}, bf16[56,3072]{1,0:T(8,128)(2,1)S(1)}, u32[]{:S(2)}, u32[]{:S(2)}) collective-permute-start(bf16[56,3072]{1,0:T(8,128)(2,1)S(1)} %get-tuple-element.181), channel_id=1, source_target_pairs={{0,2},{2,0},{4,6},{6,4},{1,3},{3,1},{5,7},{7,5},{8,10},{10,8},{12,... | collective-permute-start | bytes 1032200 | tf_op jit(solution)/shard_map/ppermute | solution.py:135
  50.7 11.9 %collective-permute-start.8 = (bf16[56,3072]{1,0:T(8,128)(2,1)S(1)}, bf16[56,3072]{1,0:T(8,128)(2,1)S(1)}, u32[]{:S(2)}, u32[]{:S(2)}) collective-permute-start(bf16[56,3072]{1,0:T(8,128)(2,1)S(1)} %get-tuple-element.180), channel_id=1, source_target_pairs={{2,4},{4,2},{3,5},{5,3},{10,12},{12,10},{11,13},{13,11},{18,20},{2... | collective-permute-start | bytes 1032200 | tf_op jit(solution)/shard_map/ppermute | solution.py:135
  55.5 14.5 %collective-permute-start.10 = (bf16[56,3072]{1,0:T(8,128)(2,1)S(1)}, bf16[56,3072]{1,0:T(8,128)(2,1)S(1)}, u32[]{:S(2)}, u32[]{:S(2)}) collective-permute-start(bf16[56,3072]{1,0:T(8,128)(2,1)S(1)} %get-tuple-element.178), channel_id=1, source_target_pairs={{0,2},{2,0},{4,6},{6,4},{1,3},{3,1},{5,7},{7,5},{8,10},{10,8},{12,... | collective-permute-start | bytes 1032200 | tf_op jit(solution)/shard_map/ppermute | solution.py:135
  58.0 11.9 %collective-permute-start.12 = (bf16[56,3072]{1,0:T(8,128)(2,1)S(1)}, bf16[56,3072]{1,0:T(8,128)(2,1)S(1)}, u32[]{:S(2)}, u32[]{:S(2)}) collective-permute-start(bf16[56,3072]{1,0:T(8,128)(2,1)S(1)} %get-tuple-element.179), channel_id=1, source_target_pairs={{2,4},{4,2},{3,5},{5,3},{10,12},{12,10},{11,13},{13,11},{18,20},{2... | collective-permute-start | bytes 1032200 | tf_op jit(solution)/shard_map/ppermute | solution.py:135
  63.6 14.4 %collective-permute-start.16 = (bf16[56,3072]{1,0:T(8,128)(2,1)S(1)}, bf16[56,3072]{1,0:T(8,128)(2,1)S(1)}, u32[]{:S(2)}, u32[]{:S(2)}) collective-permute-start(bf16[56,3072]{1,0:T(8,128)(2,1)S(1)} %maximum_convert_fusion.3), channel_id=1, source_target_pairs={{0,2},{2,0},{4,6},{6,4},{1,3},{3,1},{5,7},{7,5},{8,10},{10,8},{12,... | collective-permute-start | bytes 1032200 | tf_op jit(solution)/shard_map/ppermute | solution.py:135
  70.2 14.8 %collective-permute-start.17 = (bf16[56,3072]{1,0:T(8,128)(2,1)S(1)}, bf16[56,3072]{1,0:T(8,128)(2,1)S(1)}, u32[]{:S(2)}, u32[]{:S(2)}) collective-permute-start(bf16[56,3072]{1,0:T(8,128)(2,1)S(1)} %maximum_convert_fusion.2), channel_id=1, source_target_pairs={{0,2},{2,0},{4,6},{6,4},{1,3},{3,1},{5,7},{7,5},{8,10},{10,8},{12,... | collective-permute-start | bytes 1032200 | tf_op jit(solution)/shard_map/ppermute | solution.py:135
  72.7 12.2 %collective-permute-start.15 = (bf16[56,3072]{1,0:T(8,128)(2,1)S(1)}, bf16[56,3072]{1,0:T(8,128)(2,1)S(1)}, u32[]{:S(2)}, u32[]{:S(2)}) collective-permute-start(bf16[56,3072]{1,0:T(8,128)(2,1)S(1)} %maximum_convert_fusion.2), channel_id=1, source_target_pairs={{2,4},{4,2},{3,5},{5,3},{10,12},{12,10},{11,13},{13,11},{18,20},{2... | collective-permute-start | bytes 1032200 | tf_op jit(solution)/shard_map/ppermute | solution.py:135
  78.3 12.7 %collective-permute-start.19 = (bf16[56,3072]{1,0:T(8,128)(2,1)S(1)}, bf16[56,3072]{1,0:T(8,128)(2,1)S(1)}, u32[]{:S(2)}, u32[]{:S(2)}) collective-permute-start(bf16[56,3072]{1,0:T(8,128)(2,1)S(1)} %get-tuple-element.176), channel_id=1, source_target_pairs={{2,4},{4,2},{3,5},{5,3},{10,12},{12,10},{11,13},{13,11},{18,20},{2... | collective-permute-start | bytes 1032200 | tf_op jit(solution)/shard_map/ppermute | solution.py:135
  78.9 13.3 %collective-permute-start.14 = (bf16[56,3072]{1,0:T(8,128)(2,1)S(1)}, bf16[56,3072]{1,0:T(8,128)(2,1)S(1)}, u32[]{:S(2)}, u32[]{:S(2)}) collective-permute-start(bf16[56,3072]{1,0:T(8,128)(2,1)S(1)} %get-tuple-element.177), channel_id=1, source_target_pairs={{0,2},{2,0},{4,6},{6,4},{1,3},{3,1},{5,7},{7,5},{8,10},{10,8},{12,... | collective-permute-start | bytes 1032200 | tf_op jit(solution)/shard_map/ppermute | solution.py:135
  85.2 13.1 %collective-permute-start.21 = (bf16[56,3072]{1,0:T(8,128)(2,1)S(1)}, bf16[56,3072]{1,0:T(8,128)(2,1)S(1)}, u32[]{:S(2)}, u32[]{:S(2)}) collective-permute-start(bf16[56,3072]{1,0:T(8,128)(2,1)S(1)} %get-tuple-element.175), channel_id=1, source_target_pairs={{2,4},{4,2},{3,5},{5,3},{10,12},{12,10},{11,13},{13,11},{18,20},{2... | collective-permute-start | bytes 1032200 | tf_op jit(solution)/shard_map/ppermute | solution.py:135
  85.9 13.8 %collective-permute-start.22 = (bf16[56,3072]{1,0:T(8,128)(2,1)S(1)}, bf16[56,3072]{1,0:T(8,128)(2,1)S(1)}, u32[]{:S(2)}, u32[]{:S(2)}) collective-permute-start(bf16[56,3072]{1,0:T(8,128)(2,1)S(1)} %get-tuple-element.174), channel_id=1, source_target_pairs={{0,2},{2,0},{4,6},{6,4},{1,3},{3,1},{5,7},{7,5},{8,10},{10,8},{12,... | collective-permute-start | bytes 1032200 | tf_op jit(solution)/shard_map/ppermute | solution.py:135
  93.2 14.1 %collective-permute-start.20 = (bf16[56,3072]{1,0:T(8,128)(2,1)S(1)}, bf16[56,3072]{1,0:T(8,128)(2,1)S(1)}, u32[]{:S(2)}, u32[]{:S(2)}) collective-permute-start(bf16[56,3072]{1,0:T(8,128)(2,1)S(1)} %get-tuple-element.173), channel_id=1, source_target_pairs={{0,2},{2,0},{4,6},{6,4},{1,3},{3,1},{5,7},{7,5},{8,10},{10,8},{12,... | collective-permute-start | bytes 1032200 | tf_op jit(solution)/shard_map/ppermute | solution.py:135
  99.9 16.8 %collective-permute-start.27 = (bf16[56,3072]{1,0:T(8,128)(2,1)S(1)}, bf16[56,3072]{1,0:T(8,128)(2,1)S(1)}, u32[]{:S(2)}, u32[]{:S(2)}) collective-permute-start(bf16[56,3072]{1,0:T(8,128)(2,1)S(1)} %get-tuple-element.171), channel_id=1, source_target_pairs={{0,2},{2,0},{4,6},{6,4},{1,3},{3,1},{5,7},{7,5},{8,10},{10,8},{12,... | collective-permute-start | bytes 1032200 | tf_op jit(solution)/shard_map/ppermute | solution.py:135
  102.4 14.2 %collective-permute-start.25 = (bf16[56,3072]{1,0:T(8,128)(2,1)S(1)}, bf16[56,3072]{1,0:T(8,128)(2,1)S(1)}, u32[]{:S(2)}, u32[]{:S(2)}) collective-permute-start(bf16[56,3072]{1,0:T(8,128)(2,1)S(1)} %get-tuple-element.170), channel_id=1, source_target_pairs={{2,4},{4,2},{3,5},{5,3},{10,12},{12,10},{11,13},{13,11},{18,20},{2... | collective-permute-start | bytes 1032200 | tf_op jit(solution)/shard_map/ppermute | solution.py:135
  110.8 12.7 %collective-permute-start.23 = (bf16[56,3072]{1,0:T(8,128)(2,1)S(1)}, bf16[56,3072]{1,0:T(8,128)(2,1)S(1)}, u32[]{:S(2)}, u32[]{:S(2)}) collective-permute-start(bf16[56,3072]{1,0:T(8,128)(2,1)S(1)} %get-tuple-element.167), channel_id=1, source_target_pairs={{0,2},{2,0},{4,6},{6,4},{1,3},{3,1},{5,7},{7,5},{8,10},{10,8},{12,... | collective-permute-start | bytes 1032200 | tf_op jit(solution)/shard_map/ppermute | solution.py:135
  116.9 12.2 %collective-permute-start.26 = (bf16[56,3072]{1,0:T(8,128)(2,1)S(1)}, bf16[56,3072]{1,0:T(8,128)(2,1)S(1)}, u32[]{:S(2)}, u32[]{:S(2)}) collective-permute-start(bf16[56,3072]{1,0:T(8,128)(2,1)S(1)} %get-tuple-element.164), channel_id=1, source_target_pairs={{0,2},{2,0},{4,6},{6,4},{1,3},{3,1},{5,7},{7,5},{8,10},{10,8},{12,... | collective-permute-start | bytes 1032200 | tf_op jit(solution)/shard_map/ppermute | solution.py:135
  123.6 12.9 %collective-permute-start.29 = (bf16[56,3072]{1,0:T(8,128)(2,1)S(1)}, bf16[56,3072]{1,0:T(8,128)(2,1)S(1)}, u32[]{:S(2)}, u32[]{:S(2)}) collective-permute-start(bf16[56,3072]{1,0:T(8,128)(2,1)S(1)} %maximum_convert_fusion.1), channel_id=1, source_target_pairs={{0,2},{2,0},{4,6},{6,4},{1,3},{3,1},{5,7},{7,5},{8,10},{10,8},{12,... | collective-permute-start | bytes 1032200 | tf_op jit(solution)/shard_map/ppermute | solution.py:135
  129.3 13.6 %collective-permute-start.33 = (bf16[56,3072]{1,0:T(8,128)(2,1)S(1)}, bf16[56,3072]{1,0:T(8,128)(2,1)S(1)}, u32[]{:S(2)}, u32[]{:S(2)}) collective-permute-start(bf16[56,3072]{1,0:T(8,128)(2,1)S(1)} %maximum_convert_fusion), channel_id=1, source_target_pairs={{0,2},{2,0},{4,6},{6,4},{1,3},{3,1},{5,7},{7,5},{8,10},{10,8},{12,... | collective-permute-start | bytes 1032200 | tf_op jit(solution)/shard_map/ppermute | solution.py:135
  132.7 13.6 %collective-permute-start.31 = (bf16[56,3072]{1,0:T(8,128)(2,1)S(1)}, bf16[56,3072]{1,0:T(8,128)(2,1)S(1)}, u32[]{:S(2)}, u32[]{:S(2)}) collective-permute-start(bf16[56,3072]{1,0:T(8,128)(2,1)S(1)} %maximum_convert_fusion), channel_id=1, source_target_pairs={{2,4},{4,2},{3,5},{5,3},{10,12},{12,10},{11,13},{13,11},{18,20},{2... | collective-permute-start | bytes 1032200 | tf_op jit(solution)/shard_map/ppermute | solution.py:135
  145.0 15.5 %collective-permute-start.40 = (bf16[56,3072]{1,0:T(8,128)(2,1)S(1)}, bf16[56,3072]{1,0:T(8,128)(2,1)S(1)}, u32[]{:S(2)}, u32[]{:S(2)}) collective-permute-start(bf16[56,3072]{1,0:T(8,128)(2,1)S(1)} %collective-permute-done.32), channel_id=1, source_target_pairs={{2,0},{4,6},{3,1},{5,7},{10,8},{12,14},{11,9},{13,15},{18,16},{20,... | collective-permute-start | bytes 1032200 | tf_op jit(solution)/shard_map/ppermute | solution.py:135
  146.3 34.0 %collective-permute-start.42 = (bf16[56,3072]{1,0:T(8,128)(2,1)S(1)}, bf16[56,3072]{1,0:T(8,128)(2,1)S(1)}, u32[]{:S(2)}, u32[]{:S(2)}) collective-permute-start(bf16[56,3072]{1,0:T(8,128)(2,1)S(1)} %collective-permute-done.31), channel_id=1, source_target_pairs={{2,0},{4,6},{3,1},{5,7},{10,8},{12,14},{11,9},{13,15},{18,16},{20,... | collective-permute-start | bytes 1032200 | tf_op jit(solution)/shard_map/ppermute | solution.py:135
  147.7 27.6 %collective-permute-start.41 = (bf16[56,3072]{1,0:T(8,128)(2,1)S(1)}, bf16[56,3072]{1,0:T(8,128)(2,1)S(1)}, u32[]{:S(2)}, u32[]{:S(2)}) collective-permute-start(bf16[56,3072]{1,0:T(8,128)(2,1)S(1)} %collective-permute-done.30), channel_id=1, source_target_pairs={{2,0},{4,6},{3,1},{5,7},{10,8},{12,14},{11,9},{13,15},{18,16},{20,... | collective-permute-start | bytes 1032200 | tf_op jit(solution)/shard_map/ppermute | solution.py:135
  149.0 33.6 %collective-permute-start.43 = (bf16[56,3072]{1,0:T(8,128)(2,1)S(1)}, bf16[56,3072]{1,0:T(8,128)(2,1)S(1)}, u32[]{:S(2)}, u32[]{:S(2)}) collective-permute-start(bf16[56,3072]{1,0:T(8,128)(2,1)S(1)} %collective-permute-done.34), channel_id=1, source_target_pairs={{2,0},{4,6},{3,1},{5,7},{10,8},{12,14},{11,9},{13,15},{18,16},{20,... | collective-permute-start | bytes 1032200 | tf_op jit(solution)/shard_map/ppermute | solution.py:135
  152.6 36.1 %collective-permute-start.35 = (bf16[1,2,56,576]{3,2,1,0:T(8,128)(2,1)S(1)}, bf16[1,2,56,576]{3,2,1,0:T(8,128)(2,1)S(1)}, u32[]{:S(2)}, u32[]{:S(2)}) collective-permute-start(bf16[1,2,56,576]{3,2,1,0:T(8,128)(2,1)S(1)} %pad_maximum_fusion.12), channel_id=1, source_target_pairs={{0,1},{1,0},{2,3},{3,2},{4,5},{5,4},{6,7},{7,6},{8,9},{9,8},{10,11... | collective-permute-start | bytes 387080 | tf_op jit(solution)/shard_map/ppermute | solution.py:200
  160.5 28.2 %collective-permute-start.37 = (bf16[2,56,576]{2,1,0:T(8,128)(2,1)S(1)}, bf16[2,56,576]{2,1,0:T(8,128)(2,1)S(1)}, u32[]{:S(2)}, u32[]{:S(2)}) collective-permute-start(bf16[2,56,576]{2,1,0:T(8,128)(2,1)S(1)} %get-tuple-element.195), channel_id=1, source_target_pairs={{0,8},{16,24},{1,9},{17,25},{2,10},{18,26},{3,11},{19,27},{4,12},{... | collective-permute-start | bytes 387080 | tf_op jit(solution)/shard_map/ppermute | solution.py:213
  175.3 13.4 %collective-permute-start.38 = (bf16[2,56,576]{2,1,0:T(8,128)(2,1)S(1)}, bf16[2,56,576]{2,1,0:T(8,128)(2,1)S(1)}, u32[]{:S(2)}, u32[]{:S(2)}) collective-permute-start(bf16[2,56,576]{2,1,0:T(8,128)(2,1)S(1)} %get-tuple-element.194), channel_id=1, source_target_pairs={{0,16},{8,24},{1,17},{9,25},{2,18},{10,26},{3,19},{11,27},{4,20},{... | collective-permute-start | bytes 387080 | tf_op jit(solution)/shard_map/ppermute | solution.py:213
  (26 other events, 619.3 us)

commit v5 on v4

--- a/solution.py
+++ b/solution.py
@@ -24,13 +24,22 @@
     layers = decoders.shape[0]
     per_core = ring // cores
 
-    own_rows = lax.all_gather(layer_inputs[0], "tok", axis=1, tiled=True)
 
     swaps = ring & (ring - 1) == 0
 
     def exchanged():
-        share = own_rows.shape[0] // cores
-        block = lax.dynamic_slice_in_dim(own_rows, core * share, share, axis=0)
+        share = layer_inputs.shape[1] // cores
+        halves = []
+        for k in range(cores):
+            half = lax.dynamic_slice_in_dim(layer_inputs[0], (core + k) % cores * share, share, axis=0)
+            if k:
+                half = lax.ppermute(half, "tok", [(i, (i + k) % cores) for i in range(cores)])
+            halves.append(half)
+        halves = jnp.stack(halves)
+        block = jnp.concatenate(
+            [lax.dynamic_index_in_dim(halves, (core - c) % cores, axis=0, keepdims=False) for c in range(cores)],
+            axis=1,
+        )
         parts = []
         for k in range(ring):
             to = z ^ k if swaps else (z + k) % ring

time: 206 us -> 206 us (level)
  blocking collectives: 4.68 us -> 2.22 us
    all_gather x1 -> x0, blocking collectives: 2.47 us -> none  [local(): own_rows = lax.all_gather(layer_inputs[0], 'tok', axis=1, tiled=True)]
  transfers between devices with their start and end apart: 49 -> 50, of which waited for: 22 -> 23; matrix products, arithmetic and copies ran while one was open for 16% -> 16% of each run, Pallas kernels for 0% -> 0%
where the time goes in v5:
time: 206 us; the launch traced here: 205 us
  starting transfers between devices  86.8 us (42%)
  waiting for transfers between devices  74.2 us (36%)
  matrix products  30.5 us (15%)
  other arithmetic  7.4 us (4%)
  local copies, waits for them, and re-layouts  2.69 us (1%)
  blocking collectives  2.22 us (1%)
    ppermute x36, starting transfers between devices, swap(): return lax.ppermute(value, 'feat', pairs) if pairs else None  64.9 us
    ppermute x36, waiting for transfers between devices, swap(): return lax.ppermute(value, 'feat', pairs) if pairs else None  64 us
    dot_general x16, matrix products, run(): lax.dot_general(after(codes[key], sent), decoders[layer, :, chunk * width...  23.2 us
    ppermute x6, starting transfers between devices, share_segments(): lax.ppermute(given[-1], 'segment', [(i, j) for i, j in pairs if i < j < s...  15.4 us
    dot_general x4, matrix products, partial_sums(): jnp.dot(after(columns[group], sent), weight[:, chunk * width:(chunk + 1)...  7.21 us
    ppermute x3, starting transfers between devices, exchanged(): part = lax.ppermute(part, 'feat', pairs)  5.59 us
    ppermute x3, waiting for transfers between devices, exchanged(): part = lax.ppermute(part, 'feat', pairs)  5.51 us
  transfers between devices with their start and end apart: 50, of which 23 were waited for; matrix products, arithmetic and copies ran while one was open for 16% of the time, Pallas kernels for 0%

profile of v5, /device:TPU:0, one launch (start us, length us, event | category | flops | bytes accessed | tf_op | source)
XLA Modules:
  0.0 205.4 jit_solution(7161747206911039946)
XLA Ops:
  3.6 3.0 %collective-permute-start.1 = (bf16[56,576]{1,0:T(8,128)(2,1)S(1)}, bf16[56,576]{1,0:T(8,128)(2,1)S(1)}, u32[]{:S(2)}, u32[]{:S(2)}) collective-permute-start(bf16[56,576]{1,0:T(8,128)(2,1)S(1)} %get-tuple-element.213), channel_id=1, source_target_pairs={{0,2},{2,0},{4,6},{6,4},{1,3},{3,1},{5,7},{7,5},{8,10},{10,8},{12,... | collective-permute-start | bytes 193544 | tf_op jit(solution)/shard_map/ppermute | solution.py:49
  6.6 2.6 %collective-permute-start.2 = (bf16[56,576]{1,0:T(8,128)(2,1)S(1)}, bf16[56,576]{1,0:T(8,128)(2,1)S(1)}, u32[]{:S(2)}, u32[]{:S(2)}) collective-permute-start(bf16[56,576]{1,0:T(8,128)(2,1)S(1)} %get-tuple-element.214), channel_id=1, source_target_pairs={{0,4},{2,6},{4,0},{6,2},{1,5},{3,7},{5,1},{7,3},{8,12},{10,14},{12... | collective-permute-start | bytes 193544 | tf_op jit(solution)/shard_map/ppermute | solution.py:49
  9.9 4.6 %collective-permute-done.2 = bf16[56,576]{1,0:T(8,128)(2,1)S(1)} collective-permute-done((bf16[56,576]{1,0:T(8,128)(2,1)S(1)}, bf16[56,576]{1,0:T(8,128)(2,1)S(1)}, u32[]{:S(2)}, u32[]{:S(2)}) %collective-permute-start.2) | collective-permute-done | bytes 64544 | tf_op jit(solution)/shard_map/ppermute | solution.py:49
  15.5 2.2 %all_gather.3 = bf16[4,112,576]{2,1,0:T(8,128)(2,1)S(1)} all-gather(bf16[4,56,576]{2,1,0:T(8,128)(2,1)S(1)} %pad_maximum_fusion.9), channel_id=1, replica_groups=mesh['segment'=4,'feat'=4,'tok'=2] {'tok'}, dimensions={1}, use_global_device_ids=true | all-gather | bytes 774144 | tf_op jit(solution)/shard_map/all_gather | solution.py:51
  17.8 3.4 %convolution_convert_fusion.3 = bf16[224,3072]{1,0:T(8,128)(2,1)S(1)} fusion(bf16[576,6144]{1,0:T(8,128)(2,1)} %bitcast.179, bf16[56,576]{1,0:T(8,128)(2,1)S(1)} %get-tuple-element.205, bf16[56,576]{1,0:T(8,128)(2,1)S(1)} %get-tuple-element.206, bf16[56,576]{1,0:T(8,128)(2,1)S(1)} %get-tuple-element.207, bf16[56,576]{1,0:T(8,128)(2,1)S(1)} %get-tuple-element.208), kind=kOutput, calls=%fused_computation.3 | convolution fusion | flops 794443776 | bytes 5173248 | tf_op jit(solution)/shard_map/dot_general | solution.py:62
  21.4 3.6 %collective-permute-start.4 = (bf16[56,3072]{1,0:T(8,128)(2,1)S(1)}, bf16[56,3072]{1,0:T(8,128)(2,1)S(1)}, u32[]{:S(2)}, u32[]{:S(2)}) collective-permute-start(bf16[56,3072]{1,0:T(8,128)(2,1)S(1)} %get-tuple-element.183), channel_id=1, source_target_pairs={{0,2},{6,4},{1,3},{7,5},{8,10},{14,12},{9,11},{15,13},{16,18},{22,... | collective-permute-start | bytes 1032200 | tf_op jit(solution)/shard_map/ppermute | solution.py:144
  34.2 6.5 %collective-permute-done.6 = bf16[56,3072]{1,0:T(8,128)(2,1)S(1)} collective-permute-done((bf16[56,3072]{1,0:T(8,128)(2,1)S(1)}, bf16[56,3072]{1,0:T(8,128)(2,1)S(1)}, u32[]{:S(2)}, u32[]{:S(2)}) %collective-permute-start.6) | collective-permute-done | bytes 344096 | tf_op jit(solution)/shard_map/ppermute | solution.py:144
  41.6 6.5 %collective-permute-done.8 = bf16[56,3072]{1,0:T(8,128)(2,1)S(1)} collective-permute-done((bf16[56,3072]{1,0:T(8,128)(2,1)S(1)}, bf16[56,3072]{1,0:T(8,128)(2,1)S(1)}, u32[]{:S(2)}, u32[]{:S(2)}) %collective-permute-start.8) | collective-permute-done | bytes 344096 | tf_op jit(solution)/shard_map/ppermute | solution.py:144
  48.4 2.5 %collective-permute-start.7 = (bf16[56,3072]{1,0:T(8,128)(2,1)S(1)}, bf16[56,3072]{1,0:T(8,128)(2,1)S(1)}, u32[]{:S(2)}, u32[]{:S(2)}) collective-permute-start(bf16[56,3072]{1,0:T(8,128)(2,1)S(1)} %get-tuple-element.181), channel_id=1, source_target_pairs={{0,2},{2,0},{4,6},{6,4},{1,3},{3,1},{5,7},{7,5},{8,10},{10,8},{12,... | collective-permute-start | bytes 1032200 | tf_op jit(solution)/shard_map/ppermute | solution.py:144
  51.6 3.9 %collective-permute-done.12 = bf16[56,3072]{1,0:T(8,128)(2,1)S(1)} collective-permute-done((bf16[56,3072]{1,0:T(8,128)(2,1)S(1)}, bf16[56,3072]{1,0:T(8,128)(2,1)S(1)}, u32[]{:S(2)}, u32[]{:S(2)}) %collective-permute-start.12) | collective-permute-done | bytes 344096 | tf_op jit(solution)/shard_map/ppermute | solution.py:144
  55.8 2.5 %collective-permute-start.11 = (bf16[56,3072]{1,0:T(8,128)(2,1)S(1)}, bf16[56,3072]{1,0:T(8,128)(2,1)S(1)}, u32[]{:S(2)}, u32[]{:S(2)}) collective-permute-start(bf16[56,3072]{1,0:T(8,128)(2,1)S(1)} %get-tuple-element.178), channel_id=1, source_target_pairs={{0,2},{2,0},{4,6},{6,4},{1,3},{3,1},{5,7},{7,5},{8,10},{10,8},{12,... | collective-permute-start | bytes 1032200 | tf_op jit(solution)/shard_map/ppermute | solution.py:144
  59.0 3.9 %collective-permute-done.7 = bf16[56,3072]{1,0:T(8,128)(2,1)S(1)} collective-permute-done((bf16[56,3072]{1,0:T(8,128)(2,1)S(1)}, bf16[56,3072]{1,0:T(8,128)(2,1)S(1)}, u32[]{:S(2)}, u32[]{:S(2)}) %collective-permute-start.7) | collective-permute-done | bytes 344096 | tf_op jit(solution)/shard_map/ppermute | solution.py:144
  63.9 5.4 %collective-permute-start.17 = (bf16[56,3072]{1,0:T(8,128)(2,1)S(1)}, bf16[56,3072]{1,0:T(8,128)(2,1)S(1)}, u32[]{:S(2)}, u32[]{:S(2)}) collective-permute-start(bf16[56,3072]{1,0:T(8,128)(2,1)S(1)} %maximum_convert_fusion.3), channel_id=1, source_target_pairs={{0,2},{2,0},{4,6},{6,4},{1,3},{3,1},{5,7},{7,5},{8,10},{10,8},{12,... | collective-permute-start | bytes 1032200 | tf_op jit(solution)/shard_map/ppermute | solution.py:144
  70.4 2.5 %collective-permute-start.18 = (bf16[56,3072]{1,0:T(8,128)(2,1)S(1)}, bf16[56,3072]{1,0:T(8,128)(2,1)S(1)}, u32[]{:S(2)}, u32[]{:S(2)}) collective-permute-start(bf16[56,3072]{1,0:T(8,128)(2,1)S(1)} %maximum_convert_fusion.2), channel_id=1, source_target_pairs={{0,2},{2,0},{4,6},{6,4},{1,3},{3,1},{5,7},{7,5},{8,10},{10,8},{12,... | collective-permute-start | bytes 1032200 | tf_op jit(solution)/shard_map/ppermute | solution.py:144
  73.7 4.6 %collective-permute-done.17 = bf16[56,3072]{1,0:T(8,128)(2,1)S(1)} collective-permute-done((bf16[56,3072]{1,0:T(8,128)(2,1)S(1)}, bf16[56,3072]{1,0:T(8,128)(2,1)S(1)}, u32[]{:S(2)}, u32[]{:S(2)}) %collective-permute-start.17) | collective-permute-done | bytes 344096 | tf_op jit(solution)/shard_map/ppermute | solution.py:144
  79.2 4.6 %collective-permute-start.15 = (bf16[56,3072]{1,0:T(8,128)(2,1)S(1)}, bf16[56,3072]{1,0:T(8,128)(2,1)S(1)}, u32[]{:S(2)}, u32[]{:S(2)}) collective-permute-start(bf16[56,3072]{1,0:T(8,128)(2,1)S(1)} %get-tuple-element.177), channel_id=1, source_target_pairs={{0,2},{2,0},{4,6},{6,4},{1,3},{3,1},{5,7},{7,5},{8,10},{10,8},{12,... | collective-permute-start | bytes 1032200 | tf_op jit(solution)/shard_map/ppermute | solution.py:144
  86.1 5.1 %collective-permute-start.23 = (bf16[56,3072]{1,0:T(8,128)(2,1)S(1)}, bf16[56,3072]{1,0:T(8,128)(2,1)S(1)}, u32[]{:S(2)}, u32[]{:S(2)}) collective-permute-start(bf16[56,3072]{1,0:T(8,128)(2,1)S(1)} %get-tuple-element.174), channel_id=1, source_target_pairs={{0,2},{2,0},{4,6},{6,4},{1,3},{3,1},{5,7},{7,5},{8,10},{10,8},{12,... | collective-permute-start | bytes 1032200 | tf_op jit(solution)/shard_map/ppermute | solution.py:144
  93.5 5.1 %collective-permute-start.21 = (bf16[56,3072]{1,0:T(8,128)(2,1)S(1)}, bf16[56,3072]{1,0:T(8,128)(2,1)S(1)}, u32[]{:S(2)}, u32[]{:S(2)}) collective-permute-start(bf16[56,3072]{1,0:T(8,128)(2,1)S(1)} %get-tuple-element.173), channel_id=1, source_target_pairs={{0,2},{2,0},{4,6},{6,4},{1,3},{3,1},{5,7},{7,5},{8,10},{10,8},{12,... | collective-permute-start | bytes 1032200 | tf_op jit(solution)/shard_map/ppermute | solution.py:144
  100.2 2.5 %collective-permute-start.28 = (bf16[56,3072]{1,0:T(8,128)(2,1)S(1)}, bf16[56,3072]{1,0:T(8,128)(2,1)S(1)}, u32[]{:S(2)}, u32[]{:S(2)}) collective-permute-start(bf16[56,3072]{1,0:T(8,128)(2,1)S(1)} %get-tuple-element.171), channel_id=1, source_target_pairs={{0,2},{2,0},{4,6},{6,4},{1,3},{3,1},{5,7},{7,5},{8,10},{10,8},{12,... | collective-permute-start | bytes 1032200 | tf_op jit(solution)/shard_map/ppermute | solution.py:144
  103.6 4.0 %collective-permute-done.21 = bf16[56,3072]{1,0:T(8,128)(2,1)S(1)} collective-permute-done((bf16[56,3072]{1,0:T(8,128)(2,1)S(1)}, bf16[56,3072]{1,0:T(8,128)(2,1)S(1)}, u32[]{:S(2)}, u32[]{:S(2)}) %collective-permute-start.21) | collective-permute-done | bytes 344096 | tf_op jit(solution)/shard_map/ppermute | solution.py:144
  111.0 2.3 %collective-permute-start.24 = (bf16[56,3072]{1,0:T(8,128)(2,1)S(1)}, bf16[56,3072]{1,0:T(8,128)(2,1)S(1)}, u32[]{:S(2)}, u32[]{:S(2)}) collective-permute-start(bf16[56,3072]{1,0:T(8,128)(2,1)S(1)} %get-tuple-element.167), channel_id=1, source_target_pairs={{0,2},{2,0},{4,6},{6,4},{1,3},{3,1},{5,7},{7,5},{8,10},{10,8},{12,... | collective-permute-start | bytes 1032200 | tf_op jit(solution)/shard_map/ppermute | solution.py:144
  117.2 2.6 %collective-permute-start.27 = (bf16[56,3072]{1,0:T(8,128)(2,1)S(1)}, bf16[56,3072]{1,0:T(8,128)(2,1)S(1)}, u32[]{:S(2)}, u32[]{:S(2)}) collective-permute-start(bf16[56,3072]{1,0:T(8,128)(2,1)S(1)} %get-tuple-element.164), channel_id=1, source_target_pairs={{0,2},{2,0},{4,6},{6,4},{1,3},{3,1},{5,7},{7,5},{8,10},{10,8},{12,... | collective-permute-start | bytes 1032200 | tf_op jit(solution)/shard_map/ppermute | solution.py:144
  126.7 2.8 %collective-permute-done.27 = bf16[56,3072]{1,0:T(8,128)(2,1)S(1)} collective-permute-done((bf16[56,3072]{1,0:T(8,128)(2,1)S(1)}, bf16[56,3072]{1,0:T(8,128)(2,1)S(1)}, u32[]{:S(2)}, u32[]{:S(2)}) %collective-permute-start.27) | collective-permute-done | bytes 344096 | tf_op jit(solution)/shard_map/ppermute | solution.py:144
  129.6 3.4 %collective-permute-start.34 = (bf16[56,3072]{1,0:T(8,128)(2,1)S(1)}, bf16[56,3072]{1,0:T(8,128)(2,1)S(1)}, u32[]{:S(2)}, u32[]{:S(2)}) collective-permute-start(bf16[56,3072]{1,0:T(8,128)(2,1)S(1)} %maximum_convert_fusion), channel_id=1, source_target_pairs={{0,2},{2,0},{4,6},{6,4},{1,3},{3,1},{5,7},{7,5},{8,10},{10,8},{12,... | collective-permute-start | bytes 1032200 | tf_op jit(solution)/shard_map/ppermute | solution.py:144
  137.5 5.7 %collective-permute-done.34 = bf16[56,3072]{1,0:T(8,128)(2,1)S(1)} collective-permute-done((bf16[56,3072]{1,0:T(8,128)(2,1)S(1)}, bf16[56,3072]{1,0:T(8,128)(2,1)S(1)}, u32[]{:S(2)}, u32[]{:S(2)}) %collective-permute-start.34) | collective-permute-done | bytes 344096 | tf_op jit(solution)/shard_map/ppermute | solution.py:144
  153.2 7.6 %collective-permute-done.41 = bf16[56,3072]{1,0:T(8,128)(2,1)S(1)} collective-permute-done((bf16[56,3072]{1,0:T(8,128)(2,1)S(1)}, bf16[56,3072]{1,0:T(8,128)(2,1)S(1)}, u32[]{:S(2)}, u32[]{:S(2)}) %collective-permute-start.41) | collective-permute-done | bytes 344096 | tf_op jit(solution)/shard_map/ppermute | solution.py:144
  160.8 3.4 %collective-permute-start.38 = (bf16[2,56,576]{2,1,0:T(8,128)(2,1)S(1)}, bf16[2,56,576]{2,1,0:T(8,128)(2,1)S(1)}, u32[]{:S(2)}, u32[]{:S(2)}) collective-permute-start(bf16[2,56,576]{2,1,0:T(8,128)(2,1)S(1)} %get-tuple-element.195), channel_id=1, source_target_pairs={{0,8},{16,24},{1,9},{17,25},{2,10},{18,26},{3,11},{19,27},{4,12},{... | collective-permute-start | bytes 387080 | tf_op jit(solution)/shard_map/ppermute | solution.py:222
  164.2 11.3 %collective-permute-done.42 = bf16[56,3072]{1,0:T(8,128)(2,1)S(1)} collective-permute-done((bf16[56,3072]{1,0:T(8,128)(2,1)S(1)}, bf16[56,3072]{1,0:T(8,128)(2,1)S(1)}, u32[]{:S(2)}, u32[]{:S(2)}) %collective-permute-start.42) | collective-permute-done | bytes 344096 | tf_op jit(solution)/shard_map/ppermute | solution.py:144
  175.5 3.4 %collective-permute-start.39 = (bf16[2,56,576]{2,1,0:T(8,128)(2,1)S(1)}, bf16[2,56,576]{2,1,0:T(8,128)(2,1)S(1)}, u32[]{:S(2)}, u32[]{:S(2)}) collective-permute-start(bf16[2,56,576]{2,1,0:T(8,128)(2,1)S(1)} %get-tuple-element.194), channel_id=1, source_target_pairs={{0,16},{8,24},{1,17},{9,25},{2,18},{10,26},{3,19},{11,27},{4,20},{... | collective-permute-start | bytes 387080 | tf_op jit(solution)/shard_map/ppermute | solution.py:222
  180.6 2.2 %collective-permute-start.40 = (bf16[2,56,576]{2,1,0:T(8,128)(2,1)S(1)}, bf16[2,56,576]{2,1,0:T(8,128)(2,1)S(1)}, u32[]{:S(2)}, u32[]{:S(2)}) collective-permute-start(bf16[2,56,576]{2,1,0:T(8,128)(2,1)S(1)} %get-tuple-element.193), channel_id=1, source_target_pairs={{0,24},{8,16},{1,25},{9,17},{2,26},{10,18},{3,27},{11,19},{4,28},{... | collective-permute-start | bytes 387080 | tf_op jit(solution)/shard_map/ppermute | solution.py:222
  192.8 2.5 %collective-permute-start.47 = (bf16[2,56,576]{2,1,0:T(8,128)(2,1)S(1)}, bf16[2,56,576]{2,1,0:T(8,128)(2,1)S(1)}, u32[]{:S(2)}, u32[]{:S(2)}) collective-permute-start(bf16[2,56,576]{2,1,0:T(8,128)(2,1)S(1)} %get-tuple-element.192), channel_id=1, source_target_pairs={{0,8},{16,24},{1,9},{17,25},{2,10},{18,26},{3,11},{19,27},{4,12},{... | collective-permute-start | bytes 387080 | tf_op jit(solution)/shard_map/ppermute | solution.py:222
  195.3 2.6 %collective-permute-start.48 = (bf16[2,56,576]{2,1,0:T(8,128)(2,1)S(1)}, bf16[2,56,576]{2,1,0:T(8,128)(2,1)S(1)}, u32[]{:S(2)}, u32[]{:S(2)}) collective-permute-start(bf16[2,56,576]{2,1,0:T(8,128)(2,1)S(1)} %get-tuple-element.191), channel_id=1, source_target_pairs={{0,16},{8,24},{1,17},{9,25},{2,18},{10,26},{3,19},{11,27},{4,20},{... | collective-permute-start | bytes 387080 | tf_op jit(solution)/shard_map/ppermute | solution.py:222
  (166 shorter events, 74.6 us)
Async XLA Ops:
  21.4 12.0 %collective-permute-start.4 = (bf16[56,3072]{1,0:T(8,128)(2,1)S(1)}, bf16[56,3072]{1,0:T(8,128)(2,1)S(1)}, u32[]{:S(2)}, u32[]{:S(2)}) collective-permute-start(bf16[56,3072]{1,0:T(8,128)(2,1)S(1)} %get-tuple-element.183), channel_id=1, source_target_pairs={{0,2},{6,4},{1,3},{7,5},{8,10},{14,12},{9,11},{15,13},{16,18},{22,... | collective-permute-start | bytes 1032200 | tf_op jit(solution)/shard_map/ppermute | solution.py:144
  26.4 14.4 %collective-permute-start.6 = (bf16[56,3072]{1,0:T(8,128)(2,1)S(1)}, bf16[56,3072]{1,0:T(8,128)(2,1)S(1)}, u32[]{:S(2)}, u32[]{:S(2)}) collective-permute-start(bf16[56,3072]{1,0:T(8,128)(2,1)S(1)} %get-tuple-element.184), channel_id=1, source_target_pairs={{0,2},{6,4},{1,3},{7,5},{8,10},{14,12},{9,11},{15,13},{16,18},{22,... | collective-permute-start | bytes 1032200 | tf_op jit(solution)/shard_map/ppermute | solution.py:144
  27.7 20.4 %collective-permute-start.8 = (bf16[56,3072]{1,0:T(8,128)(2,1)S(1)}, bf16[56,3072]{1,0:T(8,128)(2,1)S(1)}, u32[]{:S(2)}, u32[]{:S(2)}) collective-permute-start(bf16[56,3072]{1,0:T(8,128)(2,1)S(1)} %get-tuple-element.182), channel_id=1, source_target_pairs={{0,2},{6,4},{1,3},{7,5},{8,10},{14,12},{9,11},{15,13},{16,18},{22,... | collective-permute-start | bytes 1032200 | tf_op jit(solution)/shard_map/ppermute | solution.py:144
  29.0 26.5 %collective-permute-start.12 = (bf16[56,3072]{1,0:T(8,128)(2,1)S(1)}, bf16[56,3072]{1,0:T(8,128)(2,1)S(1)}, u32[]{:S(2)}, u32[]{:S(2)}) collective-permute-start(bf16[56,3072]{1,0:T(8,128)(2,1)S(1)} %get-tuple-element.185), channel_id=1, source_target_pairs={{0,2},{6,4},{1,3},{7,5},{8,10},{14,12},{9,11},{15,13},{16,18},{22,... | collective-permute-start | bytes 1032200 | tf_op jit(solution)/shard_map/ppermute | solution.py:144
  33.5 14.6 %collective-permute-start.5 = (bf16[56,3072]{1,0:T(8,128)(2,1)S(1)}, bf16[56,3072]{1,0:T(8,128)(2,1)S(1)}, u32[]{:S(2)}, u32[]{:S(2)}) collective-permute-start(bf16[56,3072]{1,0:T(8,128)(2,1)S(1)} %add_convert_fusion.17), channel_id=1, source_target_pairs={{2,4},{4,2},{3,5},{5,3},{10,12},{12,10},{11,13},{13,11},{18,20},{2... | collective-permute-start | bytes 1032200 | tf_op jit(solution)/shard_map/ppermute | solution.py:144
  40.9 14.6 %collective-permute-start.10 = (bf16[56,3072]{1,0:T(8,128)(2,1)S(1)}, bf16[56,3072]{1,0:T(8,128)(2,1)S(1)}, u32[]{:S(2)}, u32[]{:S(2)}) collective-permute-start(bf16[56,3072]{1,0:T(8,128)(2,1)S(1)} %add_convert_fusion.16), channel_id=1, source_target_pairs={{2,4},{4,2},{3,5},{5,3},{10,12},{12,10},{11,13},{13,11},{18,20},{2... | collective-permute-start | bytes 1032200 | tf_op jit(solution)/shard_map/ppermute | solution.py:144
  48.4 14.5 %collective-permute-start.7 = (bf16[56,3072]{1,0:T(8,128)(2,1)S(1)}, bf16[56,3072]{1,0:T(8,128)(2,1)S(1)}, u32[]{:S(2)}, u32[]{:S(2)}) collective-permute-start(bf16[56,3072]{1,0:T(8,128)(2,1)S(1)} %get-tuple-element.181), channel_id=1, source_target_pairs={{0,2},{2,0},{4,6},{6,4},{1,3},{3,1},{5,7},{7,5},{8,10},{10,8},{12,... | collective-permute-start | bytes 1032200 | tf_op jit(solution)/shard_map/ppermute | solution.py:144
  50.9 11.9 %collective-permute-start.9 = (bf16[56,3072]{1,0:T(8,128)(2,1)S(1)}, bf16[56,3072]{1,0:T(8,128)(2,1)S(1)}, u32[]{:S(2)}, u32[]{:S(2)}) collective-permute-start(bf16[56,3072]{1,0:T(8,128)(2,1)S(1)} %get-tuple-element.180), channel_id=1, source_target_pairs={{2,4},{4,2},{3,5},{5,3},{10,12},{12,10},{11,13},{13,11},{18,20},{2... | collective-permute-start | bytes 1032200 | tf_op jit(solution)/shard_map/ppermute | solution.py:144
  55.8 14.5 %collective-permute-start.11 = (bf16[56,3072]{1,0:T(8,128)(2,1)S(1)}, bf16[56,3072]{1,0:T(8,128)(2,1)S(1)}, u32[]{:S(2)}, u32[]{:S(2)}) collective-permute-start(bf16[56,3072]{1,0:T(8,128)(2,1)S(1)} %get-tuple-element.178), channel_id=1, source_target_pairs={{0,2},{2,0},{4,6},{6,4},{1,3},{3,1},{5,7},{7,5},{8,10},{10,8},{12,... | collective-permute-start | bytes 1032200 | tf_op jit(solution)/shard_map/ppermute | solution.py:144
  58.3 11.9 %collective-permute-start.13 = (bf16[56,3072]{1,0:T(8,128)(2,1)S(1)}, bf16[56,3072]{1,0:T(8,128)(2,1)S(1)}, u32[]{:S(2)}, u32[]{:S(2)}) collective-permute-start(bf16[56,3072]{1,0:T(8,128)(2,1)S(1)} %get-tuple-element.179), channel_id=1, source_target_pairs={{2,4},{4,2},{3,5},{5,3},{10,12},{12,10},{11,13},{13,11},{18,20},{2... | collective-permute-start | bytes 1032200 | tf_op jit(solution)/shard_map/ppermute | solution.py:144
  63.9 14.4 %collective-permute-start.17 = (bf16[56,3072]{1,0:T(8,128)(2,1)S(1)}, bf16[56,3072]{1,0:T(8,128)(2,1)S(1)}, u32[]{:S(2)}, u32[]{:S(2)}) collective-permute-start(bf16[56,3072]{1,0:T(8,128)(2,1)S(1)} %maximum_convert_fusion.3), channel_id=1, source_target_pairs={{0,2},{2,0},{4,6},{6,4},{1,3},{3,1},{5,7},{7,5},{8,10},{10,8},{12,... | collective-permute-start | bytes 1032200 | tf_op jit(solution)/shard_map/ppermute | solution.py:144
  70.4 14.8 %collective-permute-start.18 = (bf16[56,3072]{1,0:T(8,128)(2,1)S(1)}, bf16[56,3072]{1,0:T(8,128)(2,1)S(1)}, u32[]{:S(2)}, u32[]{:S(2)}) collective-permute-start(bf16[56,3072]{1,0:T(8,128)(2,1)S(1)} %maximum_convert_fusion.2), channel_id=1, source_target_pairs={{0,2},{2,0},{4,6},{6,4},{1,3},{3,1},{5,7},{7,5},{8,10},{10,8},{12,... | collective-permute-start | bytes 1032200 | tf_op jit(solution)/shard_map/ppermute | solution.py:144
  73.0 12.2 %collective-permute-start.16 = (bf16[56,3072]{1,0:T(8,128)(2,1)S(1)}, bf16[56,3072]{1,0:T(8,128)(2,1)S(1)}, u32[]{:S(2)}, u32[]{:S(2)}) collective-permute-start(bf16[56,3072]{1,0:T(8,128)(2,1)S(1)} %maximum_convert_fusion.2), channel_id=1, source_target_pairs={{2,4},{4,2},{3,5},{5,3},{10,12},{12,10},{11,13},{13,11},{18,20},{2... | collective-permute-start | bytes 1032200 | tf_op jit(solution)/shard_map/ppermute | solution.py:144
  78.5 12.7 %collective-permute-start.20 = (bf16[56,3072]{1,0:T(8,128)(2,1)S(1)}, bf16[56,3072]{1,0:T(8,128)(2,1)S(1)}, u32[]{:S(2)}, u32[]{:S(2)}) collective-permute-start(bf16[56,3072]{1,0:T(8,128)(2,1)S(1)} %get-tuple-element.176), channel_id=1, source_target_pairs={{2,4},{4,2},{3,5},{5,3},{10,12},{12,10},{11,13},{13,11},{18,20},{2... | collective-permute-start | bytes 1032200 | tf_op jit(solution)/shard_map/ppermute | solution.py:144
  79.2 13.3 %collective-permute-start.15 = (bf16[56,3072]{1,0:T(8,128)(2,1)S(1)}, bf16[56,3072]{1,0:T(8,128)(2,1)S(1)}, u32[]{:S(2)}, u32[]{:S(2)}) collective-permute-start(bf16[56,3072]{1,0:T(8,128)(2,1)S(1)} %get-tuple-element.177), channel_id=1, source_target_pairs={{0,2},{2,0},{4,6},{6,4},{1,3},{3,1},{5,7},{7,5},{8,10},{10,8},{12,... | collective-permute-start | bytes 1032200 | tf_op jit(solution)/shard_map/ppermute | solution.py:144
  85.4 13.1 %collective-permute-start.22 = (bf16[56,3072]{1,0:T(8,128)(2,1)S(1)}, bf16[56,3072]{1,0:T(8,128)(2,1)S(1)}, u32[]{:S(2)}, u32[]{:S(2)}) collective-permute-start(bf16[56,3072]{1,0:T(8,128)(2,1)S(1)} %get-tuple-element.175), channel_id=1, source_target_pairs={{2,4},{4,2},{3,5},{5,3},{10,12},{12,10},{11,13},{13,11},{18,20},{2... | collective-permute-start | bytes 1032200 | tf_op jit(solution)/shard_map/ppermute | solution.py:144
  86.1 13.8 %collective-permute-start.23 = (bf16[56,3072]{1,0:T(8,128)(2,1)S(1)}, bf16[56,3072]{1,0:T(8,128)(2,1)S(1)}, u32[]{:S(2)}, u32[]{:S(2)}) collective-permute-start(bf16[56,3072]{1,0:T(8,128)(2,1)S(1)} %get-tuple-element.174), channel_id=1, source_target_pairs={{0,2},{2,0},{4,6},{6,4},{1,3},{3,1},{5,7},{7,5},{8,10},{10,8},{12,... | collective-permute-start | bytes 1032200 | tf_op jit(solution)/shard_map/ppermute | solution.py:144
  93.5 14.1 %collective-permute-start.21 = (bf16[56,3072]{1,0:T(8,128)(2,1)S(1)}, bf16[56,3072]{1,0:T(8,128)(2,1)S(1)}, u32[]{:S(2)}, u32[]{:S(2)}) collective-permute-start(bf16[56,3072]{1,0:T(8,128)(2,1)S(1)} %get-tuple-element.173), channel_id=1, source_target_pairs={{0,2},{2,0},{4,6},{6,4},{1,3},{3,1},{5,7},{7,5},{8,10},{10,8},{12,... | collective-permute-start | bytes 1032200 | tf_op jit(solution)/shard_map/ppermute | solution.py:144
  100.2 16.8 %collective-permute-start.28 = (bf16[56,3072]{1,0:T(8,128)(2,1)S(1)}, bf16[56,3072]{1,0:T(8,128)(2,1)S(1)}, u32[]{:S(2)}, u32[]{:S(2)}) collective-permute-start(bf16[56,3072]{1,0:T(8,128)(2,1)S(1)} %get-tuple-element.171), channel_id=1, source_target_pairs={{0,2},{2,0},{4,6},{6,4},{1,3},{3,1},{5,7},{7,5},{8,10},{10,8},{12,... | collective-permute-start | bytes 1032200 | tf_op jit(solution)/shard_map/ppermute | solution.py:144
  102.7 14.2 %collective-permute-start.26 = (bf16[56,3072]{1,0:T(8,128)(2,1)S(1)}, bf16[56,3072]{1,0:T(8,128)(2,1)S(1)}, u32[]{:S(2)}, u32[]{:S(2)}) collective-permute-start(bf16[56,3072]{1,0:T(8,128)(2,1)S(1)} %get-tuple-element.170), channel_id=1, source_target_pairs={{2,4},{4,2},{3,5},{5,3},{10,12},{12,10},{11,13},{13,11},{18,20},{2... | collective-permute-start | bytes 1032200 | tf_op jit(solution)/shard_map/ppermute | solution.py:144
  111.0 12.7 %collective-permute-start.24 = (bf16[56,3072]{1,0:T(8,128)(2,1)S(1)}, bf16[56,3072]{1,0:T(8,128)(2,1)S(1)}, u32[]{:S(2)}, u32[]{:S(2)}) collective-permute-start(bf16[56,3072]{1,0:T(8,128)(2,1)S(1)} %get-tuple-element.167), channel_id=1, source_target_pairs={{0,2},{2,0},{4,6},{6,4},{1,3},{3,1},{5,7},{7,5},{8,10},{10,8},{12,... | collective-permute-start | bytes 1032200 | tf_op jit(solution)/shard_map/ppermute | solution.py:144
  117.2 12.2 %collective-permute-start.27 = (bf16[56,3072]{1,0:T(8,128)(2,1)S(1)}, bf16[56,3072]{1,0:T(8,128)(2,1)S(1)}, u32[]{:S(2)}, u32[]{:S(2)}) collective-permute-start(bf16[56,3072]{1,0:T(8,128)(2,1)S(1)} %get-tuple-element.164), channel_id=1, source_target_pairs={{0,2},{2,0},{4,6},{6,4},{1,3},{3,1},{5,7},{7,5},{8,10},{10,8},{12,... | collective-permute-start | bytes 1032200 | tf_op jit(solution)/shard_map/ppermute | solution.py:144
  123.9 12.9 %collective-permute-start.30 = (bf16[56,3072]{1,0:T(8,128)(2,1)S(1)}, bf16[56,3072]{1,0:T(8,128)(2,1)S(1)}, u32[]{:S(2)}, u32[]{:S(2)}) collective-permute-start(bf16[56,3072]{1,0:T(8,128)(2,1)S(1)} %maximum_convert_fusion.1), channel_id=1, source_target_pairs={{0,2},{2,0},{4,6},{6,4},{1,3},{3,1},{5,7},{7,5},{8,10},{10,8},{12,... | collective-permute-start | bytes 1032200 | tf_op jit(solution)/shard_map/ppermute | solution.py:144
  129.6 13.6 %collective-permute-start.34 = (bf16[56,3072]{1,0:T(8,128)(2,1)S(1)}, bf16[56,3072]{1,0:T(8,128)(2,1)S(1)}, u32[]{:S(2)}, u32[]{:S(2)}) collective-permute-start(bf16[56,3072]{1,0:T(8,128)(2,1)S(1)} %maximum_convert_fusion), channel_id=1, source_target_pairs={{0,2},{2,0},{4,6},{6,4},{1,3},{3,1},{5,7},{7,5},{8,10},{10,8},{12,... | collective-permute-start | bytes 1032200 | tf_op jit(solution)/shard_map/ppermute | solution.py:144
  133.0 13.6 %collective-permute-start.32 = (bf16[56,3072]{1,0:T(8,128)(2,1)S(1)}, bf16[56,3072]{1,0:T(8,128)(2,1)S(1)}, u32[]{:S(2)}, u32[]{:S(2)}) collective-permute-start(bf16[56,3072]{1,0:T(8,128)(2,1)S(1)} %maximum_convert_fusion), channel_id=1, source_target_pairs={{2,4},{4,2},{3,5},{5,3},{10,12},{12,10},{11,13},{13,11},{18,20},{2... | collective-permute-start | bytes 1032200 | tf_op jit(solution)/shard_map/ppermute | solution.py:144
  145.3 15.5 %collective-permute-start.41 = (bf16[56,3072]{1,0:T(8,128)(2,1)S(1)}, bf16[56,3072]{1,0:T(8,128)(2,1)S(1)}, u32[]{:S(2)}, u32[]{:S(2)}) collective-permute-start(bf16[56,3072]{1,0:T(8,128)(2,1)S(1)} %collective-permute-done.33), channel_id=1, source_target_pairs={{2,0},{4,6},{3,1},{5,7},{10,8},{12,14},{11,9},{13,15},{18,16},{20,... | collective-permute-start | bytes 1032200 | tf_op jit(solution)/shard_map/ppermute | solution.py:144
  146.6 34.0 %collective-permute-start.43 = (bf16[56,3072]{1,0:T(8,128)(2,1)S(1)}, bf16[56,3072]{1,0:T(8,128)(2,1)S(1)}, u32[]{:S(2)}, u32[]{:S(2)}) collective-permute-start(bf16[56,3072]{1,0:T(8,128)(2,1)S(1)} %collective-permute-done.32), channel_id=1, source_target_pairs={{2,0},{4,6},{3,1},{5,7},{10,8},{12,14},{11,9},{13,15},{18,16},{20,... | collective-permute-start | bytes 1032200 | tf_op jit(solution)/shard_map/ppermute | solution.py:144
  148.0 27.6 %collective-permute-start.42 = (bf16[56,3072]{1,0:T(8,128)(2,1)S(1)}, bf16[56,3072]{1,0:T(8,128)(2,1)S(1)}, u32[]{:S(2)}, u32[]{:S(2)}) collective-permute-start(bf16[56,3072]{1,0:T(8,128)(2,1)S(1)} %collective-permute-done.31), channel_id=1, source_target_pairs={{2,0},{4,6},{3,1},{5,7},{10,8},{12,14},{11,9},{13,15},{18,16},{20,... | collective-permute-start | bytes 1032200 | tf_op jit(solution)/shard_map/ppermute | solution.py:144
  149.3 33.6 %collective-permute-start.44 = (bf16[56,3072]{1,0:T(8,128)(2,1)S(1)}, bf16[56,3072]{1,0:T(8,128)(2,1)S(1)}, u32[]{:S(2)}, u32[]{:S(2)}) collective-permute-start(bf16[56,3072]{1,0:T(8,128)(2,1)S(1)} %collective-permute-done.35), channel_id=1, source_target_pairs={{2,0},{4,6},{3,1},{5,7},{10,8},{12,14},{11,9},{13,15},{18,16},{20,... | collective-permute-start | bytes 1032200 | tf_op jit(solution)/shard_map/ppermute | solution.py:144
  152.9 36.1 %collective-permute-start.36 = (bf16[1,2,56,576]{3,2,1,0:T(8,128)(2,1)S(1)}, bf16[1,2,56,576]{3,2,1,0:T(8,128)(2,1)S(1)}, u32[]{:S(2)}, u32[]{:S(2)}) collective-permute-start(bf16[1,2,56,576]{3,2,1,0:T(8,128)(2,1)S(1)} %pad_maximum_fusion.12), channel_id=1, source_target_pairs={{0,1},{1,0},{2,3},{3,2},{4,5},{5,4},{6,7},{7,6},{8,9},{9,8},{10,11... | collective-permute-start | bytes 387080 | tf_op jit(solution)/shard_map/ppermute | solution.py:209
  160.8 28.2 %collective-permute-start.38 = (bf16[2,56,576]{2,1,0:T(8,128)(2,1)S(1)}, bf16[2,56,576]{2,1,0:T(8,128)(2,1)S(1)}, u32[]{:S(2)}, u32[]{:S(2)}) collective-permute-start(bf16[2,56,576]{2,1,0:T(8,128)(2,1)S(1)} %get-tuple-element.195), channel_id=1, source_target_pairs={{0,8},{16,24},{1,9},{17,25},{2,10},{18,26},{3,11},{19,27},{4,12},{... | collective-permute-start | bytes 387080 | tf_op jit(solution)/shard_map/ppermute | solution.py:222
  175.5 13.4 %collective-permute-start.39 = (bf16[2,56,576]{2,1,0:T(8,128)(2,1)S(1)}, bf16[2,56,576]{2,1,0:T(8,128)(2,1)S(1)}, u32[]{:S(2)}, u32[]{:S(2)}) collective-permute-start(bf16[2,56,576]{2,1,0:T(8,128)(2,1)S(1)} %get-tuple-element.194), channel_id=1, source_target_pairs={{0,16},{8,24},{1,17},{9,25},{2,18},{10,26},{3,19},{11,27},{4,20},{... | collective-permute-start | bytes 387080 | tf_op jit(solution)/shard_map/ppermute | solution.py:222
  (27 other events, 620.7 us)
